TPU v7x, 32 devices: a whole 2x2x4 slice. The times are simulated.
32 devices in a mesh: pairs: 8 (over z, x), seq: 4 (over y, core).
Axes of the slice: x: 2, y: 2, z: 4, core: 2. Of those that a mesh axis runs over, the one named last changes fastest.
Arguments:
- enc_input: bfloat16 [32, 512, 768], P('pairs', 'seq'), may hold values from -6 to 6
- dec_input: bfloat16 [32, 768], P(('pairs', 'seq')), may hold values from -6 to 6
- lengths: int32 [32], P('pairs'), may hold values from 129 to 512, as said below
- attend_gain: float32 [768], replicated, may hold values from 0.5 to 1.5
- query_weight: bfloat16 [768, 768], replicated, may hold values from -0.0390625 to 0.0390625
- key_weight: bfloat16 [768, 768], replicated, may hold values from -0.21875 to 0.21875
- value_weight: bfloat16 [768, 768], replicated, may hold values from -0.21875 to 0.21875
- output_weight: bfloat16 [768, 768], replicated, may hold values from -1.25 to 1.25
- bias_table: float32 [32, 12], replicated, may hold values from -4 to 4
- expand_gain: float32 [768], replicated, may hold values from 0.5 to 1.5
- expand_weight: bfloat16 [768, 3072], replicated, may hold values from -0.21875 to 0.21875
- reduce_weight: bfloat16 [3072, 768], replicated, may hold values from -0.109375 to 0.109375
- final_gain: float32 [768], replicated, may hold values from 0.5 to 1.5
- self_gain: float32 [768], replicated, may hold values from 0.5 to 1.5
- self_value: bfloat16 [768, 768], replicated, may hold values from -0.21875 to 0.21875
- self_output: bfloat16 [768, 768], replicated, may hold values from -0.21875 to 0.21875
- cross_gain: float32 [768], replicated, may hold values from 0.5 to 1.5
- cross_query: bfloat16 [768, 768], replicated, may hold values from -0.0390625 to 0.0390625
- cross_key: bfloat16 [768, 768], replicated, may hold values from -0.21875 to 0.21875
- cross_value: bfloat16 [768, 768], replicated, may hold values from -0.21875 to 0.21875
- cross_output: bfloat16 [768, 768], replicated, may hold values from -1.25 to 1.25
- feed_gain: float32 [768], replicated, may hold values from 0.5 to 1.5
- feed_expand: bfloat16 [768, 3072], replicated, may hold values from -0.21875 to 0.21875
- feed_reduce: bfloat16 [3072, 768], replicated, may hold values from -0.109375 to 0.109375
- enc_cotangent: bfloat16 [32, 512, 768], P('pairs', 'seq'), may hold values from -6 to 6
- dec_cotangent: bfloat16 [32, 768], P(('pairs', 'seq')), may hold values from -6 to 6
Outputs:
- encoded: bfloat16 [32, 512, 768], P('pairs', 'seq')
- decoded: bfloat16 [32, 768], P(('pairs', 'seq'))
- enc_input_grad: bfloat16 [32, 512, 768], P('pairs', 'seq')
- dec_input_grad: bfloat16 [32, 768], P(('pairs', 'seq'))
- attend_gain_grad: float32 [768], replicated
- query_weight_grad: float32 [768, 768], P('pairs', 'seq')
- key_weight_grad: float32 [768, 768], P('pairs', 'seq')
- value_weight_grad: float32 [768, 768], P('pairs', 'seq')
- output_weight_grad: float32 [768, 768], P('pairs', 'seq')
- bias_table_grad: float32 [32, 12], replicated
- expand_gain_grad: float32 [768], replicated
- expand_weight_grad: float32 [768, 3072], P('pairs', 'seq')
- reduce_weight_grad: float32 [3072, 768], P('pairs', 'seq')
- final_gain_grad: float32 [768], replicated
- self_gain_grad: float32 [768], replicated
- self_value_grad: float32 [768, 768], P('pairs', 'seq')
- self_output_grad: float32 [768, 768], P('pairs', 'seq')
- cross_gain_grad: float32 [768], replicated
- cross_query_grad: float32 [768, 768], P('pairs', 'seq')
- cross_key_grad: float32 [768, 768], P('pairs', 'seq')
- cross_value_grad: float32 [768, 768], P('pairs', 'seq')
- cross_output_grad: float32 [768, 768], P('pairs', 'seq')
- feed_gain_grad: float32 [768], replicated
- feed_expand_grad: float32 [768, 3072], P('pairs', 'seq')
- feed_reduce_grad: float32 [3072, 768], P('pairs', 'seq')
Inputs may be any that keep to these rules, and one draw needn't show every extreme that they name: A pair whose length exceeds 512 // 2 has bucket 512, else bucket 512 // 2 and lengths over 128. In each aligned block of 4 pairs one pair has length 512.
All inputs are finite; a program needn't handle non-finite values.
Results may differ from a plain program's by a relative error of at most 0.023.
Values may be sent and summed in bfloat16 or wider, within the bound.
A program may use at most 256 MiB of HBM per device.

v0:
```python
import jax
import jax.numpy as jnp
from jax import lax
from jax.sharding import PartitionSpec as P

EPSILON = 1e-06
EDGES = (12, 16, 23, 32, 46, 64, 91)
HIGHEST = lax.Precision.HIGHEST


def rel_bucket(query_pos, key_pos):
    offset = key_pos[None, :] - query_pos[:, None]
    distance = jnp.abs(offset)
    far_bucket = jnp.full_like(distance, 8)
    for threshold in EDGES:
        far_bucket = far_bucket + (distance >= threshold).astype(jnp.int32)
    bucket_id = jnp.where(distance < 8, distance, far_bucket)
    return bucket_id + 16 * (offset > 0).astype(jnp.int32)


def rms_norm(values, gains):
    return values * lax.rsqrt(jnp.mean(values * values, axis=-1, keepdims=True) + EPSILON) * gains


def smooth(values):
    return (
        0.5
        * values
        * (1.0 + jnp.tanh(0.7978845608 * (values + 0.044715 * values * values * values)))
    )


def matmul_acc(inputs, matrix):
    return jnp.dot(inputs, matrix, preferred_element_type=jnp.float32)


def weight_grad(inputs, upstream):
    flat_in = inputs.reshape(-1, inputs.shape[-1])
    flat_up = upstream.reshape(-1, upstream.shape[-1])
    return lax.dot_general(
        flat_in, flat_up, (((0,), (0,)), ((), ())), preferred_element_type=jnp.float32
    )


def back_matmul(upstream, matrix):
    return lax.dot_general(
        upstream,
        matrix,
        (((upstream.ndim - 1,), (1,)), ((), ())),
        preferred_element_type=jnp.float32,
    )


def norm_back(values, gains, upstream):
    pullback = jax.vjp(rms_norm, values, gains)[1]
    return pullback(upstream)


def smooth_back(values, upstream):
    return jax.vjp(smooth, values)[1](upstream)[0]


def softmax_rows(scores, visible):
    masked = jnp.where(visible, scores, -1e30)
    row_max = jnp.max(masked, axis=-1, keepdims=True)
    raised = jnp.exp(masked - row_max)
    row_total = jnp.sum(raised, axis=-1, keepdims=True)
    return (raised / row_total, row_max + jnp.log(row_total))


def untouched(key, value):
    return (key, value)


def per_device(
    enc_input,
    dec_input,
    lengths,
    attend_gain,
    query_weight,
    key_weight,
    value_weight,
    output_weight,
    bias_table,
    expand_gain,
    expand_weight,
    reduce_weight,
    final_gain,
    self_gain,
    self_value,
    self_output,
    cross_gain,
    cross_query,
    cross_key,
    cross_value,
    cross_output,
    feed_gain,
    feed_expand,
    feed_reduce,
    enc_cotangent,
    dec_cotangent,
):
    pairs_here, local_rows, model_width = enc_input.shape
    head_count = bias_table.shape[1]
    head_size = model_width // head_count
    seq_parts = lax.axis_size("seq")
    seq_place = lax.axis_index("seq")
    seq_len = local_rows * seq_parts
    own_rows = dec_input.shape[0]
    key_pos = jnp.arange(seq_len, dtype=jnp.int32)
    dec_lengths = lax.dynamic_slice_in_dim(lengths, seq_place * own_rows, own_rows)
    enc_work, cot_work = (
        lax.all_to_all(enc_input, "seq", split_axis=0, concat_axis=1, tiled=True),
        lax.all_to_all(enc_cotangent, "seq", split_axis=0, concat_axis=1, tiled=True),
    )
    work_pairs, work_rows = (enc_work.shape[0], enc_work.shape[1])
    visible = (key_pos[None, :] < dec_lengths[:, None])[:, None, None, :]
    row_live = (key_pos[None, :] < dec_lengths[:, None]).astype(jnp.float32)[:, :, None]
    onehot = (
        rel_bucket(key_pos, key_pos)[:, :, None]
        == jnp.arange(bias_table.shape[0], dtype=jnp.int32)[None, None, :]
    ).astype(jnp.float32)
    position_bias = jnp.einsum("tub,bh->htu", onehot, bias_table, precision=HIGHEST)
    enc_value = enc_work.astype(jnp.float32)

    def heads_of(array, length):
        return array.reshape(work_pairs, length, head_count, head_size)

    def encode(fetch):
        normed = rms_norm(enc_value, attend_gain).astype(jnp.bfloat16)
        query = matmul_acc(normed, query_weight).astype(jnp.bfloat16)
        key = matmul_acc(normed, key_weight).astype(jnp.bfloat16)
        value = matmul_acc(normed, value_weight).astype(jnp.bfloat16)
        key_all, value_all = fetch(key, value)
        scores = (
            jnp.einsum(
                "pthd,puhd->phtu",
                heads_of(query, work_rows),
                heads_of(key_all, seq_len),
                preferred_element_type=jnp.float32,
            )
            + position_bias[None]
        )
        probs, log_total = softmax_rows(scores, visible)
        context = (
            jnp.einsum(
                "phtu,puhd->pthd",
                probs.astype(jnp.bfloat16),
                heads_of(value_all, seq_len),
                preferred_element_type=jnp.float32,
            )
            .astype(jnp.bfloat16)
            .reshape(work_pairs, work_rows, model_width)
        )
        hidden = enc_value + matmul_acc(context, output_weight)
        mixed = rms_norm(hidden, expand_gain).astype(jnp.bfloat16)
        upper = matmul_acc(mixed, expand_weight)
        active = smooth(upper).astype(jnp.bfloat16)
        enc_block = row_live * (hidden + matmul_acc(active, reduce_weight))
        return (
            normed,
            query,
            key_all,
            value_all,
            log_total,
            context,
            hidden,
            mixed,
            upper,
            active,
            enc_block,
        )

    first_state = encode(untouched)
    enc_normed = rms_norm(first_state[10], final_gain).astype(jnp.bfloat16)
    dec_visible = (key_pos[None, :] < dec_lengths[:, None])[:, None, :]
    dec_value = dec_input.astype(jnp.float32)
    self_normed = rms_norm(dec_value, self_gain).astype(jnp.bfloat16)
    self_values = matmul_acc(self_normed, self_value).astype(jnp.bfloat16)
    after = dec_value + matmul_acc(self_values, self_output)
    cross_normed = rms_norm(after, cross_gain).astype(jnp.bfloat16)
    cross_q = (
        matmul_acc(cross_normed, cross_query)
        .astype(jnp.bfloat16)
        .reshape(own_rows, head_count, head_size)
    )
    cross_k = (
        matmul_acc(enc_normed, cross_key)
        .astype(jnp.bfloat16)
        .reshape(own_rows, seq_len, head_count, head_size)
    )
    cross_v = (
        matmul_acc(enc_normed, cross_value)
        .astype(jnp.bfloat16)
        .reshape(own_rows, seq_len, head_count, head_size)
    )
    cross_scores = jnp.einsum("rhd,ruhd->rhu", cross_q, cross_k, preferred_element_type=jnp.float32)
    cross_probs, cross_log = softmax_rows(cross_scores, dec_visible)
    cross_low = cross_probs.astype(jnp.bfloat16)
    cross_context = (
        jnp.einsum("rhu,ruhd->rhd", cross_low, cross_v, preferred_element_type=jnp.float32)
        .astype(jnp.bfloat16)
        .reshape(own_rows, model_width)
    )
    middle = after + matmul_acc(cross_context, cross_output)
    feed_normed = rms_norm(middle, feed_gain).astype(jnp.bfloat16)
    dec_upper = matmul_acc(feed_normed, feed_expand)
    dec_active = smooth(dec_upper).astype(jnp.bfloat16)
    dec_block = middle + matmul_acc(dec_active, feed_reduce)
    dec_grad_out = dec_cotangent.astype(jnp.float32)
    dec_branch = dec_grad_out.astype(jnp.bfloat16)
    grad_feed_reduce = weight_grad(dec_active, dec_branch)
    dec_upper_grad = smooth_back(dec_upper, back_matmul(dec_branch, feed_reduce)).astype(
        jnp.bfloat16
    )
    grad_feed_expand = weight_grad(feed_normed, dec_upper_grad)
    middle_norm, grad_feed_gain = norm_back(
        middle, feed_gain, back_matmul(dec_upper_grad, feed_expand)
    )
    middle_grad = dec_grad_out + middle_norm
    cross_branch = middle_grad.astype(jnp.bfloat16)
    grad_cross_output = weight_grad(cross_context, cross_branch)
    context_grad = (
        back_matmul(cross_branch, cross_output)
        .astype(jnp.bfloat16)
        .reshape(own_rows, head_count, head_size)
    )
    cross_prob_grad = jnp.einsum(
        "rhd,ruhd->rhu", context_grad, cross_v, preferred_element_type=jnp.float32
    )
    cross_v_grad = (
        jnp.einsum("rhu,rhd->ruhd", cross_low, context_grad, preferred_element_type=jnp.float32)
        .astype(jnp.bfloat16)
        .reshape(own_rows, seq_len, model_width)
    )
    cross_score_grad = (
        cross_probs
        * (cross_prob_grad - jnp.sum(cross_probs * cross_prob_grad, axis=-1, keepdims=True))
    ).astype(jnp.bfloat16)
    cross_q_grad = (
        jnp.einsum("rhu,ruhd->rhd", cross_score_grad, cross_k, preferred_element_type=jnp.float32)
        .astype(jnp.bfloat16)
        .reshape(own_rows, model_width)
    )
    cross_k_grad = (
        jnp.einsum("rhu,rhd->ruhd", cross_score_grad, cross_q, preferred_element_type=jnp.float32)
        .astype(jnp.bfloat16)
        .reshape(own_rows, seq_len, model_width)
    )
    grad_cross_query = weight_grad(cross_normed, cross_q_grad)
    grad_cross_key = weight_grad(enc_normed, cross_k_grad)
    grad_cross_value = weight_grad(enc_normed, cross_v_grad)
    rows_grad = (
        back_matmul(cross_k_grad, cross_key) + back_matmul(cross_v_grad, cross_value)
    ).astype(jnp.bfloat16)
    after_norm, grad_cross_gain = norm_back(
        after, cross_gain, back_matmul(cross_q_grad, cross_query)
    )
    after_grad = middle_grad + after_norm
    self_branch = after_grad.astype(jnp.bfloat16)
    grad_self_output = weight_grad(self_values, self_branch)
    self_values_grad = back_matmul(self_branch, self_output).astype(jnp.bfloat16)
    grad_self_value = weight_grad(self_normed, self_values_grad)
    dec_norm, grad_self_gain = norm_back(
        dec_value, self_gain, back_matmul(self_values_grad, self_value)
    )
    dec_input_grad = (after_grad + dec_norm).astype(jnp.bfloat16)
    state = encode(untouched)
    (
        normed,
        query,
        key_all,
        value_all,
        log_total,
        context,
        hidden,
        mixed,
        upper,
        active,
        enc_block,
    ) = state
    block_norm, grad_final_gain = norm_back(enc_block, final_gain, rows_grad.astype(jnp.float32))
    block_grad = row_live * (cot_work.astype(jnp.float32) + block_norm)
    reduce_branch = block_grad.astype(jnp.bfloat16)
    grad_reduce = weight_grad(active, reduce_branch)
    upper_grad = smooth_back(upper, back_matmul(reduce_branch, reduce_weight)).astype(jnp.bfloat16)
    grad_expand = weight_grad(mixed, upper_grad)
    hidden_norm, grad_expand_gain = norm_back(
        hidden, expand_gain, back_matmul(upper_grad, expand_weight)
    )
    hidden_grad = block_grad + hidden_norm
    attend_branch = hidden_grad.astype(jnp.bfloat16)
    grad_output = weight_grad(context, attend_branch)
    context_back = (
        back_matmul(attend_branch, output_weight)
        .astype(jnp.bfloat16)
        .reshape(work_pairs, work_rows, head_count, head_size)
    )
    query_heads = heads_of(query, work_rows)
    key_heads = heads_of(key_all, seq_len)
    value_heads = heads_of(value_all, seq_len)
    scores = (
        jnp.einsum("pthd,puhd->phtu", query_heads, key_heads, preferred_element_type=jnp.float32)
        + position_bias[None]
    )
    probs = jnp.exp(jnp.where(visible, scores, -1e30) - log_total)
    prob_grad = jnp.einsum(
        "pthd,puhd->phtu", context_back, value_heads, preferred_element_type=jnp.float32
    )
    value_all_grad = jnp.einsum(
        "phtu,pthd->puhd",
        probs.astype(jnp.bfloat16),
        context_back,
        preferred_element_type=jnp.float32,
    ).reshape(work_pairs, seq_len, model_width)
    score_grad = (probs * (prob_grad - jnp.sum(probs * prob_grad, axis=-1, keepdims=True))).astype(
        jnp.bfloat16
    )
    grad_bias = jnp.einsum(
        "htu,tub->bh", jnp.sum(score_grad, axis=0, dtype=jnp.float32), onehot, precision=HIGHEST
    )
    query_grad = (
        jnp.einsum("phtu,puhd->pthd", score_grad, key_heads, preferred_element_type=jnp.float32)
        .astype(jnp.bfloat16)
        .reshape(work_pairs, work_rows, model_width)
    )
    key_all_grad = jnp.einsum(
        "phtu,pthd->puhd", score_grad, query_heads, preferred_element_type=jnp.float32
    ).reshape(work_pairs, seq_len, model_width)
    key_sum, value_sum = (key_all_grad, value_all_grad)
    key_grad = key_sum.astype(jnp.bfloat16)
    value_grad = value_sum.astype(jnp.bfloat16)
    grad_query = weight_grad(normed, query_grad)
    grad_key = weight_grad(normed, key_grad)
    grad_value = weight_grad(normed, value_grad)
    normed_grad = (
        back_matmul(query_grad, query_weight)
        + back_matmul(key_grad, key_weight)
        + back_matmul(value_grad, value_weight)
    )
    input_norm, grad_attend_gain = norm_back(enc_value, attend_gain, normed_grad)
    input_grad_low = (hidden_grad + input_norm).astype(jnp.bfloat16)
    block_low = enc_block.astype(jnp.bfloat16)
    encoded, enc_input_grad = (
        lax.all_to_all(block_low, "seq", split_axis=1, concat_axis=0, tiled=True),
        lax.all_to_all(input_grad_low, "seq", split_axis=1, concat_axis=0, tiled=True),
    )
    small_sums = lax.psum(
        (
            grad_bias,
            grad_attend_gain,
            grad_expand_gain,
            grad_final_gain,
            grad_self_gain,
            grad_cross_gain,
            grad_feed_gain,
        ),
        ("pairs", "seq"),
    )
    all_columns = (
        lax.psum_scatter(
            grad_self_value.astype(jnp.bfloat16), "seq", scatter_dimension=1, tiled=True
        ).astype(jnp.float32),
        lax.psum_scatter(
            grad_self_output.astype(jnp.bfloat16), "seq", scatter_dimension=1, tiled=True
        ).astype(jnp.float32),
        lax.psum_scatter(
            grad_cross_query.astype(jnp.bfloat16), "seq", scatter_dimension=1, tiled=True
        ).astype(jnp.float32),
        lax.psum_scatter(
            grad_cross_key.astype(jnp.bfloat16), "seq", scatter_dimension=1, tiled=True
        ).astype(jnp.float32),
        lax.psum_scatter(
            grad_cross_value.astype(jnp.bfloat16), "seq", scatter_dimension=1, tiled=True
        ).astype(jnp.float32),
        lax.psum_scatter(
            grad_cross_output.astype(jnp.bfloat16), "seq", scatter_dimension=1, tiled=True
        ).astype(jnp.float32),
        lax.psum_scatter(
            grad_feed_expand.astype(jnp.bfloat16), "seq", scatter_dimension=1, tiled=True
        ).astype(jnp.float32),
        lax.psum_scatter(
            grad_feed_reduce.astype(jnp.bfloat16), "seq", scatter_dimension=1, tiled=True
        ).astype(jnp.float32),
        lax.psum_scatter(
            grad_query.astype(jnp.bfloat16), "seq", scatter_dimension=1, tiled=True
        ).astype(jnp.float32),
        lax.psum_scatter(
            grad_key.astype(jnp.bfloat16), "seq", scatter_dimension=1, tiled=True
        ).astype(jnp.float32),
        lax.psum_scatter(
            grad_value.astype(jnp.bfloat16), "seq", scatter_dimension=1, tiled=True
        ).astype(jnp.float32),
        lax.psum_scatter(
            grad_output.astype(jnp.bfloat16), "seq", scatter_dimension=1, tiled=True
        ).astype(jnp.float32),
        lax.psum_scatter(
            grad_expand.astype(jnp.bfloat16), "seq", scatter_dimension=1, tiled=True
        ).astype(jnp.float32),
        lax.psum_scatter(
            grad_reduce.astype(jnp.bfloat16), "seq", scatter_dimension=1, tiled=True
        ).astype(jnp.float32),
    )
    all_summed = (
        lax.psum_scatter(all_columns[0], "pairs", scatter_dimension=0, tiled=True),
        lax.psum_scatter(all_columns[1], "pairs", scatter_dimension=0, tiled=True),
        lax.psum_scatter(all_columns[2], "pairs", scatter_dimension=0, tiled=True),
        lax.psum_scatter(all_columns[3], "pairs", scatter_dimension=0, tiled=True),
        lax.psum_scatter(all_columns[4], "pairs", scatter_dimension=0, tiled=True),
        lax.psum_scatter(all_columns[5], "pairs", scatter_dimension=0, tiled=True),
        lax.psum_scatter(all_columns[6], "pairs", scatter_dimension=0, tiled=True),
        lax.psum_scatter(all_columns[7], "pairs", scatter_dimension=0, tiled=True),
        lax.psum_scatter(all_columns[8], "pairs", scatter_dimension=0, tiled=True),
        lax.psum_scatter(all_columns[9], "pairs", scatter_dimension=0, tiled=True),
        lax.psum_scatter(all_columns[10], "pairs", scatter_dimension=0, tiled=True),
        lax.psum_scatter(all_columns[11], "pairs", scatter_dimension=0, tiled=True),
        lax.psum_scatter(all_columns[12], "pairs", scatter_dimension=0, tiled=True),
        lax.psum_scatter(all_columns[13], "pairs", scatter_dimension=0, tiled=True),
    )
    dec_summed = all_summed[:8]
    enc_summed = all_summed[8:]
    return (
        encoded,
        dec_block.astype(jnp.bfloat16),
        enc_input_grad,
        dec_input_grad,
        small_sums[1],
        enc_summed[0],
        enc_summed[1],
        enc_summed[2],
        enc_summed[3],
        small_sums[0],
        small_sums[2],
        enc_summed[4],
        enc_summed[5],
        small_sums[3],
        small_sums[4],
        dec_summed[0],
        dec_summed[1],
        small_sums[5],
        dec_summed[2],
        dec_summed[3],
        dec_summed[4],
        dec_summed[5],
        small_sums[6],
        dec_summed[6],
        dec_summed[7],
    )


def solution(mesh):
    placed = (
        P("pairs", "seq", None),
        P(("pairs", "seq"), None),
        P("pairs"),
        P(),
        P(),
        P(),
        P(),
        P(),
        P(),
        P(),
        P(),
        P(),
        P(),
        P(),
        P(),
        P(),
        P(),
        P(),
        P(),
        P(),
        P(),
        P(),
        P(),
        P(),
        P("pairs", "seq", None),
        P(("pairs", "seq"), None),
    )
    return jax.shard_map(
        per_device,
        mesh=mesh,
        in_specs=placed,
        out_specs=(
            P("pairs", "seq", None),
            P(("pairs", "seq"), None),
            P("pairs", "seq", None),
            P(("pairs", "seq"), None),
            P(),
            P("pairs", "seq"),
            P("pairs", "seq"),
            P("pairs", "seq"),
            P("pairs", "seq"),
            P(),
            P(),
            P("pairs", "seq"),
            P("pairs", "seq"),
            P(),
            P(),
            P("pairs", "seq"),
            P("pairs", "seq"),
            P(),
            P("pairs", "seq"),
            P("pairs", "seq"),
            P("pairs", "seq"),
            P("pairs", "seq"),
            P(),
            P("pairs", "seq"),
            P("pairs", "seq"),
        ),
        check_vma=False,
    )
```

profile of v0, /device:TPU:0, one launch (start us, length us, event | category | flops | bytes accessed | tf_op | source)
XLA Modules:
  0.0 1590.8 jit_solution(6603658603111546248)
XLA Ops:
  7.2 4.4 all-to-all-start
  18.0 13.7 fusion.1
  32.8 17.8 %copy.132 = f32[512,512,12]{0,1,2:T(8,128)} copy(f32[512,512,12]{1,2,0:T(8,128)} %fusion.1) | data formatting | bytes 25165824 | tf_op jit(solution)/shard_map/tub,bh->htu/dot_general | solution.py:123
  54.1 4.3 fusion.81
  58.4 4.3 all-to-all-start.2
  72.2 3.5 convolution_convert_fusion.13
  78.0 6.2 fusion.105
  93.0 5.3 fusion.97
  98.4 3.9 multiply_reduce_fusion.3
  125.6 3.8 fusion.106
  164.0 10.6 fusion.10
  202.1 11.2 multiply_reduce_fusion
  215.3 7.0 multiply_convert_fusion
  227.7 4.0 convolution_convert_fusion.15
  234.5 6.8 fusion.34
  244.1 7.3 convolution_convert_fusion.1
  251.6 8.3 convolution_convert_fusion
  276.6 19.7 %reduce-scatter.71.cloned.1.call-done = bf16[768,192]{0,1:T(8,128)(2,1)} async-done(((bf16[768,768]{0,1:T(8,128)(2,1)}), bf16[768,192]{0,1:T(8,128)(2,1)}) %reduce-scatter.71.cloned.1.call-update) | async-done | bytes 294928 | tf_op jit(solution)/shard_map/reduce_scatter | solution.py:370
  298.4 26.2 %reduce-scatter.93.cloned.1.call-done = bf16[192,768]{1,0:T(8,128)(2,1)} async-done(((bf16[768,768]{1,0:T(8,128)(2,1)}), bf16[192,768]{1,0:T(8,128)(2,1)}) %reduce-scatter.93.cloned.1.call-update) | async-done | bytes 294928
  326.7 26.2 %reduce-scatter.95.cloned.1.call-done = bf16[192,768]{1,0:T(8,128)(2,1)} async-done(((bf16[768,768]{1,0:T(8,128)(2,1)}), bf16[192,768]{1,0:T(8,128)(2,1)}) %reduce-scatter.95.cloned.1.call-update) | async-done | bytes 294928
  355.0 26.3 %reduce-scatter.51.cloned.1.call-done = bf16[768,192]{0,1:T(8,128)(2,1)} async-done(((bf16[768,768]{0,1:T(8,128)(2,1)}), bf16[768,192]{0,1:T(8,128)(2,1)}) %reduce-scatter.51.cloned.1.call-update) | async-done | bytes 294928 | tf_op jit(solution)/shard_map/reduce_scatter | solution.py:388
  383.5 26.2 %reduce-scatter.49.cloned.1.call-done = bf16[768,192]{0,1:T(8,128)(2,1)} async-done(((bf16[768,768]{0,1:T(8,128)(2,1)}), bf16[768,192]{0,1:T(8,128)(2,1)}) %reduce-scatter.49.cloned.1.call-update) | async-done | bytes 294928 | tf_op jit(solution)/shard_map/reduce_scatter | solution.py:385
  411.7 26.2 %reduce-scatter.53.cloned.1.call-done = bf16[768,192]{0,1:T(8,128)(2,1)} async-done(((bf16[768,768]{0,1:T(8,128)(2,1)}), bf16[768,192]{0,1:T(8,128)(2,1)}) %reduce-scatter.53.cloned.1.call-update) | async-done | bytes 294928 | tf_op jit(solution)/shard_map/reduce_scatter | solution.py:391
  440.0 48.3 %reduce-scatter.57.cloned.1.call-done = bf16[768,768]{1,0:T(8,128)(2,1)} async-done(((bf16[768,3072]{1,0:T(8,128)(2,1)}), bf16[768,768]{1,0:T(8,128)(2,1)}) %reduce-scatter.57.cloned.1.call-update) | async-done | bytes 1179664 | tf_op jit(solution)/shard_map/reduce_scatter | solution.py:397
  491.3 47.5 %reduce-scatter.61.cloned.1.call-done = bf16[3072,192]{0,1:T(8,128)(2,1)} async-done(((bf16[3072,768]{0,1:T(8,128)(2,1)}), bf16[3072,192]{0,1:T(8,128)(2,1)}) %reduce-scatter.61.cloned.1.call-update) | async-done | bytes 1179664 | tf_op jit(solution)/shard_map/reduce_scatter | solution.py:400
  541.8 47.4 %reduce-scatter.77.cloned.1.call-done = bf16[768,768]{1,0:T(8,128)(2,1)} async-done(((bf16[768,3072]{1,0:T(8,128)(2,1)}), bf16[768,768]{1,0:T(8,128)(2,1)}) %reduce-scatter.77.cloned.1.call-update) | async-done | bytes 1179664 | tf_op jit(solution)/shard_map/reduce_scatter | solution.py:379
  592.4 47.3 %reduce-scatter.81.cloned.1.call-done = bf16[3072,192]{0,1:T(8,128)(2,1)} async-done(((bf16[3072,768]{0,1:T(8,128)(2,1)}), bf16[3072,192]{0,1:T(8,128)(2,1)}) %reduce-scatter.81.cloned.1.call-update) | async-done | bytes 1179664 | tf_op jit(solution)/shard_map/reduce_scatter | solution.py:382
  643.3 14.5 copy.142
  665.1 5.4 reduce.71
  671.6 4.5 all-to-all-start.3
  677.3 5.4 reduce.70
  685.5 7.3 fusion.38
  692.9 3.6 all-to-all-start.1
  697.8 45.7 %all-reduce = (f32[768]{0:T(1024)}, f32[32,12]{0,1:T(8,128)}, f32[768]{0:T(1024)}, f32[768]{0:T(1024)}, f32[768]{0:T(1024)}, /*index=5*/f32[768]{0:T(1024)}, f32[768]{0:T(1024)}) all-reduce(f32[768]{0:T(1024)S(1)} %get-tuple-element.154, f32[32,12]{0,1:T(8,128)S(1)} %fusion.38, ...), channel_id=1, replica_groups=mesh['pairs'=8,'seq'=4] {'pairs','seq'}, use_global_device_ids=true, to_apply=%region_19.20 | all-reduce | flops 4992 | bytes 39936 | tf_op jit(solution)/shard_map/psum | solution.py:348
  744.2 3.7 fusion.39
  753.0 18.4 %reduce-scatter.91.cloned.1.call-done = f32[96,192]{1,0:T(8,128)} async-done(((f32[768,192]{1,0:T(8,128)}), f32[96,192]{1,0:T(8,128)}) %reduce-scatter.91.cloned.1.call-update) | async-done | bytes 73744
  771.4 65.2 %reduce-scatter.75.cloned.1.call-done = f32[96,192]{1,0:T(8,128)} async-done(((f32[768,192]{1,0:T(8,128)}), f32[96,192]{1,0:T(8,128)}) %reduce-scatter.75.cloned.1.call-update) | async-done | bytes 73744 | tf_op jit(solution)/shard_map/reduce_scatter | solution.py:410
  836.6 65.6 %reduce-scatter.101.cloned.1.call-done = f32[96,192]{1,0:T(8,128)} async-done(((f32[768,192]{1,0:T(8,128)}), f32[96,192]{1,0:T(8,128)}) %reduce-scatter.101.cloned.1.call-update) | async-done | bytes 73744
  902.2 65.4 %reduce-scatter.99.cloned.1.call-done = f32[96,192]{1,0:T(8,128)} async-done(((f32[768,192]{1,0:T(8,128)}), f32[96,192]{1,0:T(8,128)}) %reduce-scatter.99.cloned.1.call-update) | async-done | bytes 73744
  967.6 65.5 %reduce-scatter.65.cloned.1.call-done = f32[96,192]{1,0:T(8,128)} async-done(((f32[768,192]{1,0:T(8,128)}), f32[96,192]{1,0:T(8,128)}) %reduce-scatter.65.cloned.1.call-update) | async-done | bytes 73744 | tf_op jit(solution)/shard_map/reduce_scatter | solution.py:405
  1033.2 65.4 %reduce-scatter.67.cloned.1.call-done = f32[96,192]{1,0:T(8,128)} async-done(((f32[768,192]{1,0:T(8,128)}), f32[96,192]{1,0:T(8,128)}) %reduce-scatter.67.cloned.1.call-update) | async-done | bytes 73744 | tf_op jit(solution)/shard_map/reduce_scatter | solution.py:406
  1098.6 65.7 %reduce-scatter.87.cloned.1.call-done = f32[96,192]{1,0:T(8,128)} async-done(((f32[768,192]{1,0:T(8,128)}), f32[96,192]{1,0:T(8,128)}) %reduce-scatter.87.cloned.1.call-update) | async-done | bytes 73744
  1164.3 65.3 %reduce-scatter.85.cloned.1.call-done = f32[96,192]{1,0:T(8,128)} async-done(((f32[768,192]{1,0:T(8,128)}), f32[96,192]{1,0:T(8,128)}) %reduce-scatter.85.cloned.1.call-update) | async-done | bytes 73744
  1229.7 65.6 %reduce-scatter.89.cloned.1.call-done = f32[96,192]{1,0:T(8,128)} async-done(((f32[768,192]{1,0:T(8,128)}), f32[96,192]{1,0:T(8,128)}) %reduce-scatter.89.cloned.1.call-update) | async-done | bytes 73744
  1295.3 72.1 %reduce-scatter.59.cloned.1.call-done = f32[96,768]{1,0:T(8,128)} async-done(((f32[768,768]{1,0:T(8,128)}), f32[96,768]{1,0:T(8,128)}) %reduce-scatter.59.cloned.1.call-update) | async-done | bytes 294928 | tf_op jit(solution)/shard_map/reduce_scatter | solution.py:417
  1367.4 72.0 %reduce-scatter.63.cloned.1.call-done = f32[384,192]{0,1:T(8,128)} async-done(((f32[3072,192]{0,1:T(8,128)}), f32[384,192]{0,1:T(8,128)}) %reduce-scatter.63.cloned.1.call-update) | async-done | bytes 294928 | tf_op jit(solution)/shard_map/reduce_scatter | solution.py:418
  1439.5 71.9 %reduce-scatter.79.cloned.1.call-done = f32[96,768]{1,0:T(8,128)} async-done(((f32[768,768]{1,0:T(8,128)}), f32[96,768]{1,0:T(8,128)}) %reduce-scatter.79.cloned.1.call-update) | async-done | bytes 294928 | tf_op jit(solution)/shard_map/reduce_scatter | solution.py:411
  1511.4 72.2 %reduce-scatter.83.cloned.1.call-done = f32[384,192]{0,1:T(8,128)} async-done(((f32[3072,192]{0,1:T(8,128)}), f32[384,192]{0,1:T(8,128)}) %reduce-scatter.83.cloned.1.call-update) | async-done | bytes 294928 | tf_op jit(solution)/shard_map/reduce_scatter | solution.py:412
  (423 shorter events, 186.1 us)
Async XLA Ops:
  7.2 103.9 %copy-start = (bf16[768,768]{1,0:T(8,128)(2,1)S(1)}, bf16[768,768]{1,0:T(8,128)(2,1)}, u32[]{:S(2)}) copy-start(bf16[768,768]{1,0:T(8,128)(2,1)} %param.45) | copy-start | bytes 3538948
  7.2 51.1 %all-to-all-start = ((bf16[4,128,768]{2,1,0:T(8,128)(2,1)}), bf16[4,128,768]{2,1,0:T(8,128)(2,1)S(1)}, u32[]{:S(2)}, u32[]{:S(2)}) async-start(bf16[4,128,768]{2,1,0:T(8,128)(2,1)} %param.26), calls=%async_computation | async-start | bytes 1572864 | tf_op jit(solution)/shard_map/all_to_all | solution.py:113
  12.1 19.6 %copy-start.14 = (s32[512,512]{1,0:T(8,128)}, s32[512,512]{1,0:T(8,128)S(1)}, u32[]{:S(2)}) copy-start(s32[512,512]{1,0:T(8,128)S(1)} %fusion.40) | copy-start | bytes 3145732
  15.0 16.6 %copy-start.74 = (bf16[768]{0:T(1024)(128)(2,1)}, bf16[768]{0:T(1024)(128)(2,1)S(1)}, u32[]{:S(2)}) copy-start(bf16[768]{0:T(1024)(128)(2,1)S(1)} %convolution_reduce_fusion.3) | copy-start | bytes 4612
  17.9 13.7 copy-start.17
  17.9 13.7 copy-start.55
  32.7 18.4 %copy-start.98 = (s32[4]{0:T(128)S(1)}, s32[4]{0:T(128)}, u32[]{:S(2)}) copy-start(s32[4]{0:T(128)} %param.28) | copy-start | bytes 52
  32.7 21.4 %copy-start.80 = (bf16[1,768]{1,0:T(2,128)(2,1)S(1)}, bf16[1,768]{1,0:T(2,128)(2,1)}, u32[]{:S(2)}) copy-start(bf16[1,768]{1,0:T(2,128)(2,1)} %param.51) | copy-start | bytes 4612
  58.4 102.6 %all-to-all-start.2 = ((bf16[4,128,768]{2,1,0:T(8,128)(2,1)}), bf16[4,128,768]{2,1,0:T(8,128)(2,1)}, u32[]{:S(2)}, u32[]{:S(2)}) async-start(bf16[4,128,768]{2,1,0:T(8,128)(2,1)} %param.50), calls=%async_computation.2 | async-start | bytes 1572864 | tf_op jit(solution)/shard_map/all_to_all | solution.py:114
  62.7 205.3 %reduce-scatter.97.cloned.1.call-start = ((), (), s32[]{:S(2)}) async-start(), calls=%async_computation.56 | async-start | bytes 1474560
  154.7 115.5 %reduce-scatter.55.cloned.1.call-start = ((), (), s32[]{:S(2)}) async-start(), calls=%async_computation.35 | async-start | bytes 1474560 | tf_op jit(solution)/shard_map/reduce_scatter | solution.py:394
  161.0 13.7 slice-start.3
  164.0 14.1 copy-start.11
  181.2 91.1 %reduce-scatter.103.cloned.1.call-start = ((), (), s32[]{:S(2)}) async-start(), calls=%async_computation.59 | async-start | bytes 1474560
  183.0 91.5 %reduce-scatter.73.cloned.1.call-start = ((), (), s32[]{:S(2)}) async-start(), calls=%async_computation.44 | async-start | bytes 1474560 | tf_op jit(solution)/shard_map/reduce_scatter | solution.py:373
  186.3 110.0 %reduce-scatter.71.cloned.1.call-start = ((), (), s32[]{:S(2)}) async-start(), calls=%async_computation.43 | async-start | bytes 1474560 | tf_op jit(solution)/shard_map/reduce_scatter | solution.py:370
  189.6 135.0 %reduce-scatter.93.cloned.1.call-start = ((), (), s32[]{:S(2)}) async-start(), calls=%async_computation.54 | async-start | bytes 1474560
  193.1 159.8 %reduce-scatter.95.cloned.1.call-start = ((), (), s32[]{:S(2)}) async-start(), calls=%async_computation.55 | async-start | bytes 1474560
  202.0 179.3 %reduce-scatter.51.cloned.1.call-start = ((), (), s32[]{:S(2)}) async-start(), calls=%async_computation.33 | async-start | bytes 1474560 | tf_op jit(solution)/shard_map/reduce_scatter | solution.py:388
  202.1 11.5 slice-start
  202.1 11.5 slice-start.1
  202.1 13.2 slice-start.2
  213.6 11.3 copy-start.31
  227.6 182.0 %reduce-scatter.49.cloned.1.call-start = ((), (), s32[]{:S(2)}) async-start(), calls=%async_computation.32 | async-start | bytes 1474560 | tf_op jit(solution)/shard_map/reduce_scatter | solution.py:385
  234.4 203.5 %reduce-scatter.53.cloned.1.call-start = ((), (), s32[]{:S(2)}) async-start(), calls=%async_computation.34 | async-start | bytes 1474560 | tf_op jit(solution)/shard_map/reduce_scatter | solution.py:391
  244.0 244.4 %reduce-scatter.57.cloned.1.call-start = ((), (), s32[]{:S(2)}) async-start(), calls=%async_computation.36 | async-start | bytes 5898240 | tf_op jit(solution)/shard_map/reduce_scatter | solution.py:397
  251.4 287.4 %reduce-scatter.61.cloned.1.call-start = ((), (), s32[]{:S(2)}) async-start(), calls=%async_computation.38 | async-start | bytes 5898240 | tf_op jit(solution)/shard_map/reduce_scatter | solution.py:400
  260.0 329.2 %reduce-scatter.77.cloned.1.call-start = ((), (), s32[]{:S(2)}) async-start(), calls=%async_computation.46 | async-start | bytes 5898240 | tf_op jit(solution)/shard_map/reduce_scatter | solution.py:379
  263.9 375.7 %reduce-scatter.81.cloned.1.call-start = ((), (), s32[]{:S(2)}) async-start(), calls=%async_computation.48 | async-start | bytes 5898240 | tf_op jit(solution)/shard_map/reduce_scatter | solution.py:382
  267.9 485.1 %reduce-scatter.69.cloned.1.call-start = ((), (), s32[]{:S(2)}) async-start(), calls=%async_computation.42 | async-start | bytes 884736 | tf_op jit(solution)/shard_map/reduce_scatter | solution.py:407
  270.1 501.3 %reduce-scatter.91.cloned.1.call-start = ((), (), s32[]{:S(2)}) async-start(), calls=%async_computation.53 | async-start | bytes 884736
  272.2 564.4 %reduce-scatter.75.cloned.1.call-start = ((), (), s32[]{:S(2)}) async-start(), calls=%async_computation.45 | async-start | bytes 884736 | tf_op jit(solution)/shard_map/reduce_scatter | solution.py:410
  274.4 627.8 %reduce-scatter.101.cloned.1.call-start = ((), (), s32[]{:S(2)}) async-start(), calls=%async_computation.58 | async-start | bytes 884736
  276.5 691.1 %reduce-scatter.99.cloned.1.call-start = ((), (), s32[]{:S(2)}) async-start(), calls=%async_computation.57 | async-start | bytes 884736
  298.3 734.8 %reduce-scatter.65.cloned.1.call-start = ((), (), s32[]{:S(2)}) async-start(), calls=%async_computation.40 | async-start | bytes 884736 | tf_op jit(solution)/shard_map/reduce_scatter | solution.py:405
  326.7 771.9 %reduce-scatter.67.cloned.1.call-start = ((), (), s32[]{:S(2)}) async-start(), calls=%async_computation.41 | async-start | bytes 884736 | tf_op jit(solution)/shard_map/reduce_scatter | solution.py:406
  355.0 809.4 %reduce-scatter.87.cloned.1.call-start = ((), (), s32[]{:S(2)}) async-start(), calls=%async_computation.51 | async-start | bytes 884736
  383.4 846.3 %reduce-scatter.85.cloned.1.call-start = ((), (), s32[]{:S(2)}) async-start(), calls=%async_computation.50 | async-start | bytes 884736
  411.7 883.6 %reduce-scatter.89.cloned.1.call-start = ((), (), s32[]{:S(2)}) async-start(), calls=%async_computation.52 | async-start | bytes 884736
  440.0 927.4 %reduce-scatter.59.cloned.1.call-start = ((), (), s32[]{:S(2)}) async-start(), calls=%async_computation.37 | async-start | bytes 2654208 | tf_op jit(solution)/shard_map/reduce_scatter | solution.py:417
  491.2 948.2 %reduce-scatter.63.cloned.1.call-start = ((), (), s32[]{:S(2)}) async-start(), calls=%async_computation.39 | async-start | bytes 2654208 | tf_op jit(solution)/shard_map/reduce_scatter | solution.py:418
  541.7 969.7 %reduce-scatter.79.cloned.1.call-start = ((), (), s32[]{:S(2)}) async-start(), calls=%async_computation.47 | async-start | bytes 2654208 | tf_op jit(solution)/shard_map/reduce_scatter | solution.py:411
  592.1 991.5 %reduce-scatter.83.cloned.1.call-start = ((), (), s32[]{:S(2)}) async-start(), calls=%async_computation.49 | async-start | bytes 2654208 | tf_op jit(solution)/shard_map/reduce_scatter | solution.py:412
  643.3 14.5 copy-start.37
  671.6 21.3 %all-to-all-start.3 = ((bf16[4,2,49152]{2,1,0:T(2,128)(2,1)}), bf16[4,2,49152]{2,1,0:T(2,128)(2,1)}, u32[]{:S(2)}, u32[]{:S(2)}) async-start(bf16[4,2,49152]{2,1,0:T(2,128)(2,1)} %reshape.964), calls=%async_computation.3 | async-start | bytes 1572864 | tf_op jit(solution)/shard_map/all_to_all | solution.py:346
  692.8 50.7 %copy-start.67 = (f32[1,768]{1,0:T(1,128)S(1)}, f32[1,768]{1,0:T(1,128)}, u32[]{:S(2)}) copy-start(f32[1,768]{1,0:T(1,128)} %get-tuple-element.176) | copy-start | bytes 9220
  692.9 58.4 %all-to-all-start.1 = ((bf16[4,2,49152]{2,1,0:T(2,128)(2,1)}), bf16[4,2,49152]{2,1,0:T(2,128)(2,1)S(1)}, u32[]{:S(2)}, u32[]{:S(2)}) async-start(bf16[4,2,49152]{2,1,0:T(2,128)(2,1)} %reshape.962), calls=%async_computation.1 | async-start | bytes 1572864 | tf_op jit(solution)/shard_map/all_to_all | solution.py:345
  751.3 832.3 %copy-start.1 = (bf16[768,768]{1,0:T(8,128)(2,1)S(1)}, bf16[768,768]{1,0:T(8,128)(2,1)}, u32[]{:S(2)}) copy-start(bf16[768,768]{1,0:T(8,128)(2,1)} %param.45) | copy-start | bytes 3538948
  (91 other events, 319.4 us)
Sparse Core Ops, SparseCore 0:
  154.8 28.0 reduce-scatter.96
  185.7 25.6 reduce-scatter.54
  214.0 25.6 reduce-scatter.102
  242.3 25.7 reduce-scatter.72
  270.6 25.6 reduce-scatter.70
  298.9 25.6 reduce-scatter.92
  327.2 25.6 reduce-scatter.94
  355.6 25.6 reduce-scatter.50
  383.9 25.6 reduce-scatter.48
  412.2 25.6 reduce-scatter.52
  440.5 47.8 reduce-scatter.56
  490.9 47.8 reduce-scatter.60
  541.3 47.8 reduce-scatter.76
  591.8 47.8 reduce-scatter.80
  643.3 62.4 reduce-scatter.68
  709.9 61.3 reduce-scatter.90
  775.1 61.4 reduce-scatter.74
  840.7 61.4 reduce-scatter.100
  906.1 61.5 reduce-scatter.98
  971.7 61.4 reduce-scatter.64
  1037.0 61.4 reduce-scatter.66
  1102.8 61.4 reduce-scatter.86
  1168.2 61.4 reduce-scatter.84
  1233.8 61.4 reduce-scatter.88
  1299.4 67.9 reduce-scatter.58
  1371.3 68.0 reduce-scatter.62
  1443.4 67.9 reduce-scatter.78
  1515.5 68.0 reduce-scatter.82
where the time goes:
time: 1600 us; the launch traced here: 1590 us
  waiting for transfers between devices  1170 us (73%)
  matrix products  164 us (10%)
  local copies, waits for them, and re-layouts  103 us (6%)
  other arithmetic  66.4 us (4%)
  blocking collectives  45.7 us (3%)
  between operations  20.6 us (1%)
  starting transfers between devices  18.8 us (1%)
    unnamed x38, waiting for transfers between devices  399 us
    reduce_scatter x1, waiting for transfers between devices, per_device(): lax.psum_scatter(all_columns[7], 'pairs', scatter_dimension=0, tiled=True)  72.2 us
    reduce_scatter x1, waiting for transfers between devices, per_device(): lax.psum_scatter(all_columns[12], 'pairs', scatter_dimension=0, tiled=True)  72.1 us
    reduce_scatter x1, waiting for transfers between devices, per_device(): lax.psum_scatter(all_columns[13], 'pairs', scatter_dimension=0, tiled=True)  72 us
    reduce_scatter x1, waiting for transfers between devices, per_device(): lax.psum_scatter(all_columns[6], 'pairs', scatter_dimension=0, tiled=True)  71.9 us
    reduce_scatter x1, waiting for transfers between devices, per_device(): lax.psum_scatter(all_columns[0], 'pairs', scatter_dimension=0, tiled=True)  65.5 us
    reduce_scatter x1, waiting for transfers between devices, per_device(): lax.psum_scatter(all_columns[1], 'pairs', scatter_dimension=0, tiled=True)  65.4 us
    reduce_scatter x1, waiting for transfers between devices, per_device(): lax.psum_scatter(all_columns[5], 'pairs', scatter_dimension=0, tiled=True)  65.2 us
  transfers between devices with their start and end apart: 32, of which 23 were waited for; matrix products, arithmetic and copies ran while one was open for 20% of the time, Pallas kernels for 0%

commit v1 on v0

v1 whole, which is shorter than its diff:
```python
import functools

import jax
import jax.numpy as jnp
from jax import lax
from jax.experimental import pallas as pl
from jax.experimental.pallas import tpu as pltpu
from jax.sharding import PartitionSpec as P

EPSILON = 1e-06
EDGES = (12, 16, 23, 32, 46, 64, 91)
HIGHEST = lax.Precision.HIGHEST
MESH = pl.DeviceIdType.MESH
BF = jnp.bfloat16
F32 = jnp.float32


def rel_bucket(query_pos, key_pos):
    offset = key_pos[None, :] - query_pos[:, None]
    distance = jnp.abs(offset)
    far_bucket = jnp.full_like(distance, 8)
    for threshold in EDGES:
        far_bucket = far_bucket + (distance >= threshold).astype(jnp.int32)
    bucket_id = jnp.where(distance < 8, distance, far_bucket)
    return bucket_id + 16 * (offset > 0).astype(jnp.int32)


def rms_norm(values, gains):
    return values * lax.rsqrt(jnp.mean(values * values, axis=-1, keepdims=True) + EPSILON) * gains


def smooth(values):
    return (
        0.5
        * values
        * (1.0 + jnp.tanh(0.7978845608 * (values + 0.044715 * values * values * values)))
    )


def mm(a, b):
    return jnp.dot(a, b, preferred_element_type=F32)


def mm_t(a, b):
    return lax.dot_general(a, b, (((1,), (1,)), ((), ())), preferred_element_type=F32)


def t_mm(a, b):
    return lax.dot_general(a, b, (((0,), (0,)), ((), ())), preferred_element_type=F32)


def norm_back(values, gains, upstream):
    return jax.vjp(rms_norm, values, gains)[1](upstream)


def smooth_back(values, upstream):
    return jax.vjp(smooth, values)[1](upstream)[0]


def exchange_kernel(np_, ns, u, small, dec, enc, red, small_out, dec_out, enc_out,
                    own, r0, r1a, r1b, s1a, s1b, r2, s2, r3, sm, smr, smz,
                    loc, s0s, s0r, s1s, s1r, s2s, s2r, s3s, s3r,
                    ms, mr, mzs, mzr, ds, dr, es, er):
    units = u.shape[0]
    nz = np_ // 2
    rows = u.shape[5]
    p = lax.axis_index("pairs")
    s = lax.axis_index("seq")
    c = lax.rem(s, 2)
    y = s // 2
    x = lax.rem(p, 2)
    z = p // 2
    me = p * ns + s
    count = np_ * ns
    core_peer = (p, s + 1 - 2 * c)
    y_peer = (p, lax.rem(s + 2, 4))
    x_peer = (p + 1 - 2 * x, s)

    def place(d):
        lin = lax.rem(me + d, count)
        return (lin // ns, lax.rem(lin, ns))

    barrier = pltpu.get_barrier_semaphore()

    @pl.loop(1, count)
    def _(d):
        pl.semaphore_signal(barrier, inc=1, device_id=place(d), device_id_type=MESH)

    pl.semaphore_wait(barrier, count - 1)

    def remote(src, dst, send, recv, peer):
        return pltpu.make_async_remote_copy(
            src_ref=src, dst_ref=dst, send_sem=send, recv_sem=recv,
            device_id=peer, device_id_type=MESH)

    def core_copy(k):
        return remote(u.at[k, 1 - c], r0.at[k], s0s.at[k], s0r.at[k], core_peer)

    def own_copy(k):
        return pltpu.make_async_copy(u.at[k, c], own.at[k], loc.at[k])

    @pl.loop(0, units)
    def _(k):
        core_copy(k).start()
        own_copy(k).start()

    def dec_copy(d):
        q = place(d)
        return remote(dec.at[q[0] * ns + q[1]], dec_out.at[me], ds.at[d], dr.at[d], q)

    keep_dec = pltpu.make_async_copy(dec.at[me], dec_out.at[me], loc.at[units])
    keep_dec.start()

    @pl.loop(1, count)
    def _(d):
        dec_copy(d).start()

    def enc_copy(d):
        t = lax.rem(s + d, ns)
        return remote(enc.at[:, t], enc_out.at[:, s], es.at[d], er.at[d], (p, t))

    keep_enc = pltpu.make_async_copy(enc.at[:, s], enc_out.at[:, s], loc.at[units + 1])
    keep_enc.start()
    for d in range(1, ns):
        enc_copy(d).start()

    sm[0] = small[...]
    for i, peer in enumerate((core_peer, y_peer, x_peer)):
        copy = remote(sm.at[i], smr.at[i], ms.at[i], mr.at[i], peer)
        copy.start()
        copy.wait()
        if i < 2:
            sm[i + 1] = sm[i] + smr[i]
        else:
            smz[z] = sm[i] + smr[i]

    def z_small(d):
        return remote(smz.at[z], smz.at[z], mzs.at[d], mzr.at[d],
                      (lax.rem(z + d, nz) * 2 + x, s))

    @pl.loop(1, nz)
    def _(d):
        z_small(d).start()

    def y_first(k):
        return remote(own.at[2 * k, 1 - y], r1a.at[k], s1s.at[2 * k], s1r.at[2 * k], y_peer)

    def x_first(k):
        return remote(own.at[2 * k + 1, :, :, 1 - x], r1b.at[k], s1s.at[2 * k + 1],
                      s1r.at[2 * k + 1], x_peer)

    def x_second(k):
        return remote(s1a.at[k, :, 1 - x], r2.at[2 * k], s2s.at[2 * k], s2r.at[2 * k], x_peer)

    def y_second(k):
        return remote(s1b.at[k, 1 - y], r2.at[2 * k + 1], s2s.at[2 * k + 1],
                      s2r.at[2 * k + 1], y_peer)

    def z_last(k, d):
        t = lax.rem(z + d, nz)
        return remote(s2.at[k, t], r3.at[k, d], s3s.at[k, d], s3r.at[k, d], (t * 2 + x, s))

    def stage0(k):
        core_copy(k).wait()
        own_copy(k).wait()

        @pl.loop(0, 2)
        def _(a):
            @pl.loop(0, nz)
            def _(b):
                for e in range(2):
                    own[k, a, b, e] = (own[k, a, b, e].astype(F32)
                                       + r0[k, a, b, e].astype(F32)).astype(BF)

    @pl.loop(0, units // 2)
    def _(k):
        stage0(2 * k)
        y_first(k).start()
        stage0(2 * k + 1)
        x_first(k).start()

    @pl.loop(0, units // 2)
    def _(k):
        y_first(k).wait()

        @pl.loop(0, nz)
        def _(b):
            for e in range(2):
                s1a[k, b, e] = (own[2 * k, y, b, e].astype(F32)
                                + r1a[k, b, e].astype(F32)).astype(BF)

        x_second(k).start()
        x_first(k).wait()

        @pl.loop(0, nz)
        def _(b):
            for e in range(2):
                s1b[k, e, b] = (own[2 * k + 1, e, b, x].astype(F32)
                                + r1b[k, e, b].astype(F32)).astype(BF)

        y_second(k).start()

    @pl.loop(0, units // 2)
    def _(k):
        x_second(k).wait()

        @pl.loop(0, nz)
        def _(b):
            s2[2 * k, b] = (s1a[k, b, x].astype(F32) + r2[2 * k, b].astype(F32)).astype(BF)

        @pl.loop(1, nz)
        def _(d):
            z_last(2 * k, d).start()

        y_second(k).wait()

        @pl.loop(0, nz)
        def _(b):
            s2[2 * k + 1, b] = (s1b[k, y, b].astype(F32)
                                + r2[2 * k + 1, b].astype(F32)).astype(BF)

        @pl.loop(1, nz)
        def _(d):
            z_last(2 * k + 1, d).start()

    @pl.loop(0, units)
    def _(k):
        red[k] = s2[k, z].astype(F32)

        @pl.loop(1, nz)
        def _(d):
            z_last(k, d).wait()
            red[k] = red[k] + r3[k, d].astype(F32)

    @pl.loop(1, nz)
    def _(d):
        z_small(d).wait()

    small_out[...] = smz[0]

    @pl.loop(1, nz)
    def _(d):
        small_out[...] = small_out[...] + smz[d]

    keep_dec.wait()
    keep_enc.wait()
    for d in range(1, ns):
        enc_copy(d).wait()

    @pl.loop(1, count)
    def _(d):
        dec_copy(d).wait()


def exchange(np_, ns, u, small, dec, enc):
    units = u.shape[0]
    half = units // 2
    nz = np_ // 2
    rows, cols = u.shape[5:]
    count = np_ * ns
    dma = pltpu.SemaphoreType.DMA
    anywhere = pl.BlockSpec(memory_space=pl.ANY)
    vmem = pl.BlockSpec(memory_space=pltpu.VMEM)
    return pl.pallas_call(
        functools.partial(exchange_kernel, np_, ns),
        out_shape=(
            jax.ShapeDtypeStruct((units, rows, cols), F32),
            jax.ShapeDtypeStruct(small.shape, F32),
            jax.ShapeDtypeStruct(dec.shape, BF),
            jax.ShapeDtypeStruct(enc.shape, BF),
        ),
        in_specs=[anywhere, vmem, anywhere, anywhere],
        out_specs=(vmem, vmem, anywhere, anywhere),
        scratch_shapes=[
            pltpu.VMEM((units, 2, nz, 2, rows, cols), BF),
            pltpu.VMEM((units, 2, nz, 2, rows, cols), BF),
            pltpu.VMEM((half, nz, 2, rows, cols), BF),
            pltpu.VMEM((half, 2, nz, rows, cols), BF),
            pltpu.VMEM((half, nz, 2, rows, cols), BF),
            pltpu.VMEM((half, 2, nz, rows, cols), BF),
            pltpu.VMEM((units, nz, rows, cols), BF),
            pltpu.VMEM((units, nz, rows, cols), BF),
            pltpu.VMEM((units, nz, rows, cols), BF),
            pltpu.VMEM((3,) + small.shape, F32),
            pltpu.VMEM((3,) + small.shape, F32),
            pltpu.VMEM((nz,) + small.shape, F32),
            dma((units + 2,)),
            dma((units,)), dma((units,)), dma((units,)), dma((units,)),
            dma((units,)), dma((units,)), dma((units, nz)), dma((units, nz)),
            dma((3,)), dma((3,)), dma((nz,)), dma((nz,)),
            dma((count,)), dma((count,)), dma((ns,)), dma((ns,)),
        ],
        compiler_params=pltpu.CompilerParams(
            collective_id=0, has_side_effects=True, vmem_limit_bytes=58 * 1024 * 1024),
        name="exchange",
    )(u, small, dec, enc)


def per_device(
    enc_input, dec_input, lengths, attend_gain, query_weight, key_weight, value_weight,
    output_weight, bias_table, expand_gain, expand_weight, reduce_weight, final_gain,
    self_gain, self_value, self_output, cross_gain, cross_query, cross_key, cross_value,
    cross_output, feed_gain, feed_expand, feed_reduce, enc_cotangent, dec_cotangent,
):
    group, local_rows, width = enc_input.shape
    heads = bias_table.shape[1]
    size = width // heads
    ns = lax.axis_size("seq")
    np_ = lax.axis_size("pairs")
    place = lax.axis_index("seq")
    seq_len = local_rows * ns
    key_pos = jnp.arange(seq_len, dtype=jnp.int32)
    length = lax.dynamic_slice_in_dim(lengths, place, 1)[0]
    enc_work = lax.all_to_all(enc_input, "seq", split_axis=0, concat_axis=1, tiled=True)[0]
    cot_work = lax.all_to_all(enc_cotangent, "seq", split_axis=0, concat_axis=1, tiled=True)[0]
    visible = key_pos < length
    row_live = visible.astype(F32)[:, None]
    onehot = (
        rel_bucket(key_pos, key_pos)[:, :, None]
        == jnp.arange(bias_table.shape[0], dtype=jnp.int32)[None, None, :]
    ).astype(F32)
    position_bias = jnp.einsum("tub,bh->htu", onehot, bias_table, precision=HIGHEST)
    enc_value = enc_work.astype(F32)

    def heads_of(array):
        return array.reshape(seq_len, heads, size)

    normed = rms_norm(enc_value, attend_gain).astype(BF)
    query = mm(normed, query_weight).astype(BF)
    key = mm(normed, key_weight).astype(BF)
    value = mm(normed, value_weight).astype(BF)
    scores = jnp.einsum("thd,uhd->htu", heads_of(query), heads_of(key),
                        preferred_element_type=F32) + position_bias
    masked = jnp.where(visible, scores, -1e30)
    probs = jax.nn.softmax(masked, axis=-1)
    probs_low = probs.astype(BF)
    context = jnp.einsum("htu,uhd->thd", probs_low, heads_of(value),
                         preferred_element_type=F32).astype(BF).reshape(seq_len, width)
    hidden = enc_value + mm(context, output_weight)
    mixed = rms_norm(hidden, expand_gain).astype(BF)
    upper = mm(mixed, expand_weight)
    active = smooth(upper).astype(BF)
    enc_block = row_live * (hidden + mm(active, reduce_weight))
    enc_normed = rms_norm(enc_block, final_gain).astype(BF)

    dec_value = dec_input.astype(F32)
    self_normed = rms_norm(dec_value, self_gain).astype(BF)
    self_values = mm(self_normed, self_value).astype(BF)
    after = dec_value + mm(self_values, self_output)
    cross_normed = rms_norm(after, cross_gain).astype(BF)
    cross_q = mm(cross_normed, cross_query).astype(BF)
    own_head = (jnp.arange(width, dtype=jnp.int32)[None, :] // size
                == jnp.arange(heads, dtype=jnp.int32)[:, None])

    def spread(row):
        return jnp.where(own_head, row, jnp.zeros_like(row))

    def collect(rows):
        return jnp.sum(jnp.where(own_head, rows, 0.0), axis=0, keepdims=True)

    q_rows = mm_t(spread(cross_q), cross_key).astype(BF)
    cross_scores = jnp.where(visible[None, :], mm_t(q_rows, enc_normed), -1e30)
    cross_probs = jax.nn.softmax(cross_scores, axis=-1)
    cross_low = cross_probs.astype(BF)
    mean_rows = mm(cross_low, enc_normed).astype(BF)
    cross_context = collect(mm(mean_rows, cross_value)).astype(BF)
    middle = after + mm(cross_context, cross_output)
    feed_normed = rms_norm(middle, feed_gain).astype(BF)
    dec_upper = mm(feed_normed, feed_expand)
    dec_active = smooth(dec_upper).astype(BF)
    dec_block = middle + mm(dec_active, feed_reduce)
    dec_grad_out = dec_cotangent.astype(F32)
    dec_upper_grad = smooth_back(dec_upper, mm_t(dec_cotangent, feed_reduce)).astype(BF)
    middle_norm, grad_feed_gain = norm_back(middle, feed_gain, mm_t(dec_upper_grad, feed_expand))
    middle_grad = dec_grad_out + middle_norm
    cross_branch = middle_grad.astype(BF)
    context_grad = mm_t(cross_branch, cross_output).astype(BF)
    g_rows = mm_t(spread(context_grad), cross_value).astype(BF)
    cross_prob_grad = mm_t(g_rows, enc_normed)
    cross_score_grad = (
        cross_probs
        * (cross_prob_grad - jnp.sum(cross_probs * cross_prob_grad, axis=-1, keepdims=True))
    ).astype(BF)
    score_rows = mm(cross_score_grad, enc_normed).astype(BF)
    cross_q_grad = collect(mm(score_rows, cross_key)).astype(BF)
    rows_grad = t_mm(
        jnp.concatenate([cross_score_grad, cross_low], axis=0),
        jnp.concatenate([q_rows, g_rows], axis=0),
    ).astype(BF)
    after_norm, grad_cross_gain = norm_back(after, cross_gain, mm_t(cross_q_grad, cross_query))
    after_grad = middle_grad + after_norm
    self_branch = after_grad.astype(BF)
    self_values_grad = mm_t(self_branch, self_output).astype(BF)
    dec_norm, grad_self_gain = norm_back(dec_value, self_gain, mm_t(self_values_grad, self_value))
    dec_input_grad = (after_grad + dec_norm).astype(BF)

    block_norm, grad_final_gain = norm_back(enc_block, final_gain, rows_grad.astype(F32))
    block_grad = row_live * (cot_work.astype(F32) + block_norm)
    reduce_branch = block_grad.astype(BF)
    upper_grad = smooth_back(upper, mm_t(reduce_branch, reduce_weight)).astype(BF)
    hidden_norm, grad_expand_gain = norm_back(hidden, expand_gain, mm_t(upper_grad, expand_weight))
    hidden_grad = block_grad + hidden_norm
    attend_branch = hidden_grad.astype(BF)
    context_back = heads_of(mm_t(attend_branch, output_weight).astype(BF))
    prob_grad = jnp.einsum("thd,uhd->htu", context_back, heads_of(value),
                           preferred_element_type=F32)
    value_grad = jnp.einsum("htu,thd->uhd", probs_low, context_back,
                            preferred_element_type=F32).astype(BF).reshape(seq_len, width)
    score_grad = (probs * (prob_grad - jnp.sum(probs * prob_grad, axis=-1, keepdims=True))
                  ).astype(BF)
    grad_bias = jnp.einsum("htu,tub->bh", score_grad.astype(F32), onehot, precision=HIGHEST)
    query_grad = jnp.einsum("htu,uhd->thd", score_grad, heads_of(key),
                            preferred_element_type=F32).astype(BF).reshape(seq_len, width)
    key_grad = jnp.einsum("htu,thd->uhd", score_grad, heads_of(query),
                          preferred_element_type=F32).astype(BF).reshape(seq_len, width)
    normed_grad = (mm_t(query_grad, query_weight) + mm_t(key_grad, key_weight)
                   + mm_t(value_grad, value_weight))
    input_norm, grad_attend_gain = norm_back(enc_value, attend_gain, normed_grad)
    input_grad = (hidden_grad + input_norm).astype(BF)

    nz = np_ // 2
    r = width // np_
    rp = -(-r // 16) * 16
    cols = width // ns

    def pad(unit):
        return jnp.pad(unit, ((0, 0),) * 4 + ((0, rp - r), (0, 0)))

    def narrow_pair(first, second):
        both = jnp.stack([first, second]).astype(BF).reshape(2, nz, 2, r, 2, 2, cols)
        return pad(both.transpose(5, 4, 1, 2, 3, 0, 6).reshape(2, 2, nz, 2, r, 2 * cols))

    grad_expand = t_mm(mixed, upper_grad).astype(BF)
    grad_reduce = t_mm(active, reduce_branch).astype(BF)
    wide = grad_expand.reshape(nz, 2, r, 2, 2, 2, 2 * cols).transpose(5, 4, 3, 0, 1, 2, 6)
    tall = grad_reduce.reshape(nz, 2, 4, r, 2, 2, cols).transpose(2, 5, 4, 0, 1, 3, 6)
    units = jnp.stack([
        pad(wide[0]), pad(wide[1]),
        pad(jnp.concatenate([tall[0], tall[1]], axis=-1)),
        pad(jnp.concatenate([tall[2], tall[3]], axis=-1)),
        narrow_pair(t_mm(normed, query_grad), t_mm(normed, key_grad)),
        narrow_pair(t_mm(normed, value_grad), t_mm(context, attend_branch)),
    ])
    small = jnp.concatenate([
        grad_attend_gain, grad_expand_gain, grad_final_gain, grad_self_gain, grad_cross_gain,
        grad_feed_gain, grad_bias.reshape(-1)])
    small_rows = -(-small.size // 1024) * 8
    small = jnp.pad(small, (0, small_rows * 128 - small.size)).reshape(small_rows, 128)

    left = jnp.concatenate([
        jnp.concatenate([self_normed, self_values, cross_normed, cross_context, feed_normed])
        .reshape(5, np_, r).transpose(1, 0, 2).reshape(np_, 5 * r),
        dec_active.reshape(np_, 4 * r)], axis=1)
    mid = jnp.stack([score_rows, mean_rows]).reshape(2, ns, heads // ns, np_, r)
    mid = mid.transpose(3, 1, 0, 2, 4).reshape(np_, ns, 6 * r)
    right = jnp.concatenate([
        jnp.concatenate([self_values_grad, self_branch, cross_q_grad, cross_branch,
                         cross_q, context_grad, dec_cotangent])
        .reshape(7, ns, cols).transpose(1, 0, 2).reshape(ns, 7 * cols),
        dec_upper_grad.reshape(ns, 4 * cols)], axis=1)
    dec_all = jnp.concatenate([
        jnp.broadcast_to(left[:, None], (np_, ns, 9 * r)), mid,
        jnp.broadcast_to(right[None], (np_, ns, 11 * cols))], axis=-1)
    dec_all = dec_all.reshape(np_ * ns, -1)
    used = dec_all.shape[1]
    dec_rows = -(-used // 2048) * 16
    dec_all = jnp.pad(dec_all, ((0, 0), (0, dec_rows * 128 - used)))
    dec_all = dec_all.reshape(np_ * ns, dec_rows, 128)
    both = jnp.stack([enc_block.astype(BF), input_grad]).reshape(2, ns, local_rows, width)

    red, small_sum, dec_got, both_out = exchange(np_, ns, units, small, dec_all, both)

    got = dec_got.reshape(np_ * ns, -1)
    lefts = got[:, :9 * r].reshape(-1, 9, r)
    mids = got[:, 9 * r:15 * r].reshape(-1, 6, r)
    rights = got[:, 15 * r:15 * r + 11 * cols].reshape(-1, 11, cols)
    plain = jnp.einsum("nkr,nkc->krc", lefts[:, :4], rights[:, :4], preferred_element_type=F32)
    crossed = jnp.einsum("nkhr,nkhd->krhd", mids.reshape(-1, 2, 3, r),
                         rights[:, 4:6].reshape(-1, 2, 3, size),
                         preferred_element_type=F32).reshape(2, r, cols)
    feed_in = jnp.einsum("nr,nc->rc", lefts[:, 4], rights[:, 7:11].reshape(-1, 4 * cols),
                         preferred_element_type=F32)
    feed_out = jnp.einsum("nr,nc->rc", lefts[:, 5:9].reshape(-1, 4 * r), rights[:, 6],
                          preferred_element_type=F32)
    red = red[:, :r]
    small_flat = small_sum.reshape(-1)
    gains = [small_flat[i * width:(i + 1) * width] for i in range(6)]
    bias = small_flat[6 * width:6 * width + bias_table.size].reshape(bias_table.shape)
    grad_reduce_out = jnp.concatenate(
        [red[2][:, :cols], red[2][:, cols:], red[3][:, :cols], red[3][:, cols:]], axis=0)
    return (
        both_out[0], dec_block.astype(BF), both_out[1], dec_input_grad,
        gains[0],
        red[4][:, :cols], red[4][:, cols:], red[5][:, :cols], red[5][:, cols:],
        bias,
        gains[1],
        jnp.concatenate([red[0], red[1]], axis=1), grad_reduce_out,
        gains[2],
        gains[3], plain[0], plain[1],
        gains[4], plain[2], crossed[0], crossed[1], plain[3],
        gains[5], feed_in, feed_out,
    )


def solution(mesh):
    rows = P("pairs", "seq", None)
    single = P(("pairs", "seq"), None)
    block = P("pairs", "seq")
    return jax.shard_map(
        per_device,
        mesh=mesh,
        in_specs=(rows, single, P("pairs")) + (P(),) * 21 + (rows, single),
        out_specs=(
            rows, single, rows, single,
            P(), block, block, block, block, P(), P(), block, block, P(),
            P(), block, block, P(), block, block, block, block, P(), block, block,
        ),
        check_vma=False,
    )
```

time: 1600 us -> 509 us (0.32)
  waiting for transfers between devices: 1170 us -> 0.01 us
  Pallas kernels: 0 us -> 118 us
  local copies, waits for them, and re-layouts: 103 us -> 150 us
  blocking collectives: 45.7 us -> 0 us
  other arithmetic: 66.4 us -> 49.5 us
    reduce_scatter x18 -> x0, waiting for transfers between devices: 773 us -> none  [the longest x1 72.2 us: per_device(): lax.psum_scatter(all_columns[7], 'pairs', scatter_dimension=0, tiled=True)]
    unnamed x38 -> x0, waiting for transfers between devices: 399 us -> none
    pallas_call x0 -> x1, Pallas kernels: none -> 118 us  [exchange(): pl.pallas_call(functools.partial(exchange_kernel, np_, ns), out_shape=(ja...]
    psum x1 -> x0, blocking collectives: 45.7 us -> none  [per_device(): lax.psum((grad_bias, grad_attend_gain, grad_expand_gain, grad_final_gain,...]
    reshape x0 -> x15, local copies, waits for them, and re-layouts: none -> 35.7 us  [the longest x2 20.1 us: per_device(): grad_reduce.reshape(nz, 2, 4, r, 2, 2, cols).transpose(2, 5, 4, 0, 1, 3, 6)]
    convert_element_type x27 -> x14, other arithmetic: 39.1 us -> 16.7 us  [the longest x1 7.02 us: per_device(): score_grad = (probs * (prob_grad - jnp.sum(probs * prob_grad, axis=-1, ke...]
    unnamed x235 -> x301, local copies, waits for them, and re-layouts: 48.7 us -> 27.9 us
    dot_general x47 -> x50, matrix products: 151 us -> 154 us  [the longest x16 35.5 us: mm_t(): lax.dot_general(a, b, (((1,), (1,)), ((), ())), preferred_element_type=F32)]
  transfers between devices with their start and end apart: 32 -> 2, of which waited for: 23 -> 0; matrix products, arithmetic and copies ran while one was open for 20% -> 25% of each run, Pallas kernels for 0% -> 0%
where the time goes in v1:
time: 509 us; the launch traced here: 501 us
  matrix products  168 us (33%)
  local copies, waits for them, and re-layouts  150 us (29%)
  Pallas kernels  118 us (23%)
  other arithmetic  49.5 us (10%)
  starting transfers between devices  8.87 us (2%)
  between operations  6.78 us (1%)
    pallas_call x1, Pallas kernels, exchange(): pl.pallas_call(functools.partial(exchange_kernel, np_, ns), out_shape=(ja...  118 us
    dot_general x16, matrix products, mm_t(): lax.dot_general(a, b, (((1,), (1,)), ((), ())), preferred_element_type=F32)  35.5 us
    dot_general x16, matrix products, mm(): return jnp.dot(a, b, preferred_element_type=F32)  33.8 us
    unnamed x301, local copies, waits for them, and re-layouts  27.9 us
    dot_general x7, matrix products, t_mm(): lax.dot_general(a, b, (((0,), (0,)), ((), ())), preferred_element_type=F32)  20.4 us
    reshape x2, local copies, waits for them, and re-layouts, per_device(): grad_reduce.reshape(nz, 2, 4, r, 2, 2, cols).transpose(2, 5, 4, 0, 1, 3, 6)  20.1 us
    dot_general x1, local copies, waits for them, and re-layouts, per_device(): jnp.einsum('tub,bh->htu', onehot, bias_table, precision=HIGHEST)  17.8 us
    another operation x3, local copies, waits for them, and re-layouts, per_device(): jnp.stack([pad(wide[0]), pad(wide[1]), pad(jnp.concatenate([tall[0], tall...  16.7 us
  transfers between devices with their start and end apart: 2, of which 0 were waited for; matrix products, arithmetic and copies ran while one was open for 25% of the time, Pallas kernels for 0%

profile of v1, /device:TPU:0, one launch (start us, length us, event | category | flops | bytes accessed | tf_op | source)
XLA Modules:
  0.0 500.8 jit_solution(16085513074586868249)
XLA Ops:
  0.7 4.4 all-to-all-start
  11.7 13.7 %fusion.2 = f32[512,512,12]{1,2,0:T(8,128)} fusion(s32[512,512]{1,0:T(8,128)S(1)} %fusion.49, f32[32,12]{0,1:T(8,128)S(1)} %copy-done.104), kind=kOutput, calls=%fused_computation.3 | convolution fusion | flops 1216348160 | bytes 13633024 | tf_op jit(solution)/shard_map/tub,bh->htu/dot_general | solution.py:322
  25.4 17.8 %copy.112 = f32[512,512,12]{0,1,2:T(8,128)} copy(f32[512,512,12]{1,2,0:T(8,128)} %fusion.2) | data formatting | bytes 25165824 | tf_op jit(solution)/shard_map/tub,bh->htu/dot_general | solution.py:322
  43.3 2.3 multiply_reduce_fusion.13
  49.7 4.3 fusion.109
  54.0 4.5 all-to-all-start.1
  59.3 3.2 convolution_convert_fusion.9
  64.0 3.2 convolution_convert_fusion.8
  68.6 11.8 %fusion.5 = f32[12,512,512]{1,2,0:T(8,128)} fusion(f32[512,512,12]{0,1,2:T(8,128)} %copy.112, pred[512]{0:T(512)(128)(4,1)S(1)} %copy-done.122, bf16[512,12,64]{0,2,1:T(8,128)(2,1)S(1)} %bitcast.308, bf16[512,12,64]{0,2,1:T(8,128)(2,1)S(1)} %bitcast.306), kind=kOutput, calls=%fused_computation.7 | convolution fusion | flops 408944640 | bytes 26739200 | tf_op jit(solution)/shard_map/thd,uhd->htu/dot_general | solution.py:332
  80.4 15.8 %fusion.141 = (f32[12,512]{1,0:T(8,128)}, f32[12,512,512]{1,2,0:T(8,128)}) fusion(f32[12,512,512]{1,2,0:T(8,128)} %fusion.5), kind=kOutput, calls=%fused_computation.295 | output fusion | flops 6291967 | bytes 25190400 | tf_op jit(solution)/shard_map/sub | solution.py:335
  99.3 12.4 %fusion.39 = bf16[12,64,512]{2,1,0:T(8,128)(2,1)} fusion(bf16[512,12,64]{0,2,1:T(8,128)(2,1)S(1)} %bitcast.321, f32[12,512]{1,0:T(8,128)} %get-tuple-element.175, f32[12,512,512]{1,2,0:T(8,128)} %fusion.5), kind=kOutput, calls=%fused_computation.92 | convolution fusion | flops 412490240 | bytes 14180352 | tf_op jit(solution)/shard_map/htu,uhd->thd/dot_general | solution.py:337
  111.8 3.1 multiply_reduce_fusion.4
  115.4 4.6 fusion.129
  120.2 3.9 multiply_reduce_fusion.3
  129.2 3.1 fusion.111
  133.5 3.8 fusion.143
  140.9 2.0 fusion.21
  143.5 4.0 fusion.133
  147.5 10.4 %fusion.9 = bf16[512,3072]{1,0:T(8,128)(2,1)S(1)} fusion(f32[512,3072]{1,0:T(8,128)} %copy-done.6, bf16[3072,768]{1,0:T(8,128)(2,1)} %param.37, f32[512,768]{1,0:T(8,128)S(1)} %get-tuple-element.139), kind=kOutput, calls=%fused_computation.18 | convolution fusion | flops 2454061056 | bytes 15728640 | tf_op jit(solution)/shard_map/dot_general | solution.py:45
  158.0 3.4 multiply_reduce_fusion.1
  164.0 1.7 convolution_convert_fusion.6
  165.7 2.3 copy.117
  168.0 12.3 %fusion.42 = bf16[12,64,512]{2,1,0:T(8,128)(2,1)} fusion(bf16[512,12,64]{0,2,1:T(8,128)(2,1)} %bitcast.326, f32[12,512]{1,0:T(8,128)} %get-tuple-element.175, f32[12,512,512]{1,2,0:T(8,128)} %fusion.5), kind=kOutput, calls=%fused_computation.93 | convolution fusion | flops 412490240 | bytes 14180352 | tf_op jit(solution)/shard_map/htu,thd->uhd/dot_general | solution.py:407
  180.4 12.0 %multiply_reduce_fusion = (f32[12,512]{1,0:T(8,128)S(1)}, f32[12,512,512]{1,2,0:T(8,128)}) fusion(f32[12,512,512]{1,2,0:T(8,128)} %get-tuple-element.176, f32[12,512]{1,0:T(8,128)} %get-tuple-element.175, bf16[512,12,64]{0,2,1:T(8,128)(2,1)} %bitcast.327, bf16[512,12,64]{0,2,1:T(8,128)(2,1)} %bitcast.322), kind=kOutput, calls=%fused_computation.9 | convolution fusion | flops 412084224 | bytes 26787840 | tf_op jit(solution)/shard_map/thd,uhd->htu/dot_general | solution.py:405
  192.4 7.0 %multiply_convert_fusion = bf16[12,512,512]{1,2,0:T(8,128)(2,1)S(1)} fusion(f32[12,512,512]{1,2,0:T(8,128)} %get-tuple-element.194, f32[12,512]{1,0:T(8,128)S(1)} %get-tuple-element.193, f32[12,512,512]{1,2,0:T(8,128)S(1)} %bitcast.304, f32[12,512]{1,0:T(8,128)S(1)} %copy-done.47), kind=kLoop, calls=%fused_computation.8 | loop fusion | flops 12582912 | bytes 31506432 | tf_op jit(solution)/shard_map/convert_element_type | solution.py:410
  199.5 2.6 convolution_convert_fusion.12
  202.4 2.9 convolution_convert_fusion.11
  215.3 14.5 %copy.124 = bf16[12,512,512]{2,0,1:T(8,128)(2,1)} copy(bf16[12,512,512]{1,2,0:T(8,128)(2,1)} %copy-done.1) | data formatting | bytes 12582912 | tf_op jit(solution)/shard_map/convert_element_type | solution.py:410
  230.3 8.5 %convolution_convert_fusion = bf16[3072,768]{1,0:T(8,128)(2,1)} fusion(f32[512,768]{1,0:T(8,128)S(1)} %copy-done.13, f32[512,3072]{1,0:T(8,128)} %copy-done.6), kind=kOutput, calls=%fused_computation.24 | convolution fusion | flops 2432827392 | bytes 12582912 | tf_op jit(solution)/shard_map/dot_general | solution.py:49
  238.9 4.5 convolution_convert_fusion.1
  245.9 3.0 fusion.34
  251.8 2.3 fusion.145
  254.7 7.8 %fusion.47 = f32[32,12]{1,0:T(8,128)} fusion(bf16[12,512,512]{2,0,1:T(8,128)(2,1)} %copy.124, s32[512,512]{1,0:T(8,128)S(1)} %copy-done.21), kind=kOutput, calls=%fused_computation.106 | convolution fusion | flops 209715200 | bytes 7341568 | tf_op jit(solution)/shard_map/htu,tub->bh/dot_general | solution.py:411
  277.6 2.4 fusion.37
  281.6 4.9 copy.123
  286.5 7.7 %stack.50 = bf16[1,2,2,4,2,96,384]{6,5,4,3,2,1,0:T(8,128)(2,1)} reshape(bf16[2,2,4,2,96,2,192]{6,5,4,3,2,1,0:T(2,128)(2,1)} %copy.123) | data formatting | bytes 4718592 | tf_op jit(solution)/shard_map/stack | solution.py:437
  296.9 4.9 copy.120
  301.8 7.4 %stack.48 = bf16[1,2,2,4,2,96,384]{6,5,4,3,2,1,0:T(8,128)(2,1)} reshape(bf16[2,2,4,2,96,2,192]{6,5,4,3,2,1,0:T(2,128)(2,1)} %copy.120) | data formatting | bytes 4718592 | tf_op jit(solution)/shard_map/stack | solution.py:437
  309.2 16.1 %reshape.605 = bf16[4,2,4,96,2,2,192]{6,5,4,3,2,1,0:T(2,128)(2,1)} reshape(bf16[3072,768]{1,0:T(8,128)(2,1)} %convolution_convert_fusion) | data formatting | bytes 9437184 | tf_op jit(solution)/shard_map/reshape | solution.py:436
  325.3 4.0 copy.178
  329.3 2.2 slice_bitcast_fusion.1
  331.6 11.8 %reshape.604 = bf16[4,2,96,2,2,2,384]{6,5,4,3,2,1,0:T(2,128)(2,1)} reshape(bf16[768,3072]{1,0:T(8,128)(2,1)} %convolution_convert_fusion.1) | data formatting | bytes 9437184 | tf_op jit(solution)/shard_map/reshape | solution.py:435
  343.4 5.6 %bitcast_dynamic-update-slice_fusion = bf16[6,2,2,4,2,96,384]{6,5,4,3,2,1,0:T(8,128)(2,1)} fusion(bf16[4,2,96,2,2,2,384]{6,5,4,3,2,1,0:T(2,128)(2,1)} %reshape.604), kind=kLoop, calls=%fused_computation.26 | loop fusion | bytes 9437184
  351.8 2.4 fusion.16
  354.1 2.3 fusion.17
  360.6 117.6 %exchange.1 = (f32[6,96,384]{2,1,0:T(8,128)}, f32[40,128]{1,0:T(8,128)}, bf16[32,32,128]{2,1,0:T(8,128)(2,1)}, bf16[2,4,128,768]{3,2,1,0:T(8,128)(2,1)}) custom-call(bf16[6,2,2,4,2,96,384]{6,5,4,3,2,1,0:T(8,128)(2,1)} %constant_dynamic-update-slice_fusion.u, f32[40,128]{1,0:T(8,128)} %pad_bitcast_fusion.1.small, bf16[32,32,128]{2,1,0:T(8,128)(2,1)} %bitcast.317, ...), custom_call_target="tpu_custom_call" | custom-call | tf_op jit(solution)/shard_map/exchange/pallas_call | solution.py:264
  487.1 2.0 slice_bitcast_fusion.7
  492.8 3.7 fusion.48
  (438 shorter events, 86.0 us)
Async XLA Ops:
  0.7 95.6 %copy-start = (bf16[768,768]{1,0:T(8,128)(2,1)S(1)}, bf16[768,768]{1,0:T(8,128)(2,1)}, u32[]{:S(2)}) copy-start(bf16[768,768]{1,0:T(8,128)(2,1)} %param.32) | copy-start | bytes 3538948
  0.7 7.9 %copy-start.48 = (bf16[1,768]{1,0:T(2,128)(2,1)S(1)}, bf16[1,768]{1,0:T(2,128)(2,1)}, u32[]{:S(2)}) copy-start(bf16[1,768]{1,0:T(2,128)(2,1)} %param.27) | copy-start | bytes 4612
  0.7 9.2 %copy-start.67 = (f32[768]{0:T(1024)S(1)}, f32[768]{0:T(1024)}, u32[]{:S(2)}) copy-start(f32[768]{0:T(1024)} %param.39) | copy-start | bytes 9220
  0.7 11.0 %copy-start.104 = (f32[32,12]{0,1:T(8,128)S(1)}, f32[32,12]{0,1:T(8,128)}, u32[]{:S(2)}) copy-start(f32[32,12]{0,1:T(8,128)} %param.34) | copy-start | bytes 4612
  0.7 53.2 %all-to-all-start = ((bf16[4,128,768]{2,1,0:T(8,128)(2,1)}), bf16[4,128,768]{2,1,0:T(8,128)(2,1)S(1)}, u32[]{:S(2)}, u32[]{:S(2)}) async-start(bf16[4,128,768]{2,1,0:T(8,128)(2,1)} %param.26), calls=%async_computation | async-start | bytes 1572864 | tf_op jit(solution)/shard_map/all_to_all | solution.py:314
  5.5 19.9 %copy-start.20 = (s32[512,512]{1,0:T(8,128)}, s32[512,512]{1,0:T(8,128)S(1)}, u32[]{:S(2)}) copy-start(s32[512,512]{1,0:T(8,128)S(1)} %fusion.49) | copy-start | bytes 3145732
  25.4 20.8 %copy-start.70 = (f32[768]{0:T(1024)S(1)}, f32[768]{0:T(1024)}, u32[]{:S(2)}) copy-start(f32[768]{0:T(1024)} %param.42) | copy-start | bytes 9220
  43.3 6.4 %copy-start.100 = (bf16[1,768]{1,0:T(2,128)(2,1)S(1)}, bf16[1,768]{1,0:T(2,128)(2,1)}, u32[]{:S(2)}) copy-start(bf16[1,768]{1,0:T(2,128)(2,1)} %param.51) | copy-start | bytes 4612
  54.0 89.6 %all-to-all-start.1 = ((bf16[4,128,768]{2,1,0:T(8,128)(2,1)}), bf16[4,128,768]{2,1,0:T(8,128)(2,1)}, u32[]{:S(2)}, u32[]{:S(2)}) async-start(bf16[4,128,768]{2,1,0:T(8,128)(2,1)} %param.50), calls=%async_computation.1 | async-start | bytes 1572864 | tf_op jit(solution)/shard_map/all_to_all | solution.py:315
  80.4 15.8 %copy-start.39 = (bf16[512,768]{1,0:T(8,128)(2,1)S(1)}, bf16[512,768]{1,0:T(8,128)(2,1)}, u32[]{:S(2)}) copy-start(bf16[512,768]{1,0:T(8,128)(2,1)} %copy-done.38) | copy-start | bytes 2359300
  99.3 12.4 %copy-start.36 = (bf16[512,768]{0,1:T(8,128)(2,1)}, bf16[512,768]{0,1:T(8,128)(2,1)S(1)}, u32[]{:S(2)}) copy-start(bf16[512,768]{0,1:T(8,128)(2,1)S(1)} %copy.109) | copy-start | bytes 2359300
  111.8 8.4 %slice-start.5 = ((s8[4718592]{0:T(1024)(128)(4,1)}), s8[4194304]{0:T(1024)(128)(4,1)S(1)}, s32[]{:S(2)}) async-start(s8[4718592]{0:T(1024)(128)(4,1)} %bitcast.340), calls=%async_computation.7 | async-start | bytes 8388608
  133.5 5.9 %copy-start.23 = (bf16[768,768]{1,0:T(8,128)(2,1)S(1)}, bf16[768,768]{1,0:T(8,128)(2,1)}, u32[]{:S(2)}) copy-start(bf16[768,768]{1,0:T(8,128)(2,1)} %param.46) | copy-start | bytes 3538948
  133.5 6.3 %copy-start.25 = (bf16[768,768]{1,0:T(8,128)(2,1)S(1)}, bf16[768,768]{1,0:T(8,128)(2,1)}, u32[]{:S(2)}) copy-start(bf16[768,768]{1,0:T(8,128)(2,1)} %param.45) | copy-start | bytes 3538948
  143.5 14.4 %slice-start.3 = ((s8[4718592]{0:T(1024)(128)(4,1)}), s8[4194304]{0:T(1024)(128)(4,1)S(1)}, s32[]{:S(2)}) async-start(s8[4718592]{0:T(1024)(128)(4,1)} %bitcast.310), calls=%async_computation.5 | async-start | bytes 8388608
  147.5 13.9 %copy-start.12 = (f32[512,768]{1,0:T(8,128)}, f32[512,768]{1,0:T(8,128)S(1)}, u32[]{:S(2)}) copy-start(f32[512,768]{1,0:T(8,128)S(1)} %get-tuple-element.139) | copy-start | bytes 4718596
  147.5 10.5 %copy-start.17 = (f32[512,768]{1,0:T(8,128)S(1)}, f32[512,768]{1,0:T(8,128)}, u32[]{:S(2)}) copy-start(f32[512,768]{1,0:T(8,128)} %copy-done.16) | copy-start | bytes 4718596
  147.5 10.5 %slice-start.4 = ((s8[4718592]{0:T(1024)(128)(4,1)}), s8[524288]{0:T(1024)(128)(4,1)S(1)}, s32[]{:S(2)}) async-start(s8[4718592]{0:T(1024)(128)(4,1)} %bitcast.310), calls=%async_computation.6 | async-start | bytes 1048576
  147.5 10.5 %copy-start.79 = (f32[512]{0:T(512)S(1)}, f32[512]{0:T(512)}, u32[]{:S(2)}) copy-start(f32[512]{0:T(512)} %copy-done.78) | copy-start | bytes 6148
  180.4 12.0 %slice-start = ((s8[12582912]{0:T(1024)(128)(4,1)}), s8[4194304]{0:T(1024)(128)(4,1)S(1)}, s32[]{:S(2)}) async-start(s8[12582912]{0:T(1024)(128)(4,1)} %bitcast.303), calls=%async_computation.2 | async-start | bytes 8388608
  180.4 12.0 %slice-start.1 = ((s8[12582912]{0:T(1024)(128)(4,1)}), s8[4194304]{0:T(1024)(128)(4,1)S(1)}, s32[]{:S(2)}) async-start(s8[12582912]{0:T(1024)(128)(4,1)} %bitcast.303), calls=%async_computation.3 | async-start | bytes 8388608
  180.4 12.0 %slice-start.2 = ((s8[12582912]{0:T(1024)(128)(4,1)}), s8[4194304]{0:T(1024)(128)(4,1)S(1)}, s32[]{:S(2)}) async-start(s8[12582912]{0:T(1024)(128)(4,1)} %bitcast.303), calls=%async_computation.4 | async-start | bytes 8388608
  180.4 12.0 %copy-start.47 = (f32[12,512]{1,0:T(8,128)S(1)}, f32[12,512]{1,0:T(8,128)}, u32[]{:S(2)}) copy-start(f32[12,512]{1,0:T(8,128)} %get-tuple-element.175) | copy-start | bytes 73732
  202.3 6.8 %copy-start.46 = (bf16[12,768]{1,0:T(8,128)(2,1)S(1)}, bf16[12,768]{1,0:T(8,128)(2,1)}, u32[]{:S(2)}) copy-start(bf16[12,768]{1,0:T(8,128)(2,1)} %copy-done.45) | copy-start | bytes 55300
  205.3 6.3 %copy-start.71 = (f32[768]{0:T(1024)S(1)}, f32[768]{0:T(1024)}, u32[]{:S(2)}) copy-start(f32[768]{0:T(1024)} %param.42) | copy-start | bytes 9220
  205.3 7.6 %copy-start.84 = (f32[1,768]{1,0:T(1,128)S(1)}, f32[1,768]{1,0:T(1,128)}, u32[]{:S(2)}) copy-start(f32[1,768]{1,0:T(1,128)} %copy-done.83) | copy-start | bytes 9220
  205.5 8.0 %copy-start.28 = (bf16[768,768]{1,0:T(8,128)(2,1)S(1)}, bf16[768,768]{1,0:T(8,128)(2,1)}, u32[]{:S(2)}) copy-start(bf16[768,768]{1,0:T(8,128)(2,1)} %param.41) | copy-start | bytes 3538948
  213.5 16.2 %copy-start.81 = (f32[1,768]{1,0:T(1,128)}, f32[1,768]{1,0:T(1,128)S(1)}, u32[]{:S(2)}) copy-start(f32[1,768]{1,0:T(1,128)S(1)} %get-tuple-element.125) | copy-start | bytes 9220
  215.2 14.5 %copy-start.74 = (f32[4,128]{1,0:T(4,128)S(1)}, f32[4,128]{1,0:T(4,128)}, u32[]{:S(2)}) copy-start(f32[4,128]{1,0:T(4,128)} %copy-done.73) | copy-start | bytes 6148
  215.3 15.1 %copy-start.13 = (f32[512,768]{1,0:T(8,128)S(1)}, f32[512,768]{1,0:T(8,128)}, u32[]{:S(2)}) copy-start(f32[512,768]{1,0:T(8,128)} %copy-done.12) | copy-start | bytes 4718596
  230.3 8.5 %copy-start.18 = (f32[512,768]{1,0:T(8,128)S(1)}, f32[512,768]{1,0:T(8,128)}, u32[]{:S(2)}) copy-start(f32[512,768]{1,0:T(8,128)} %copy-done.16) | copy-start | bytes 4718596
  230.3 8.5 %copy-start.80 = (f32[512]{0:T(512)S(1)}, f32[512]{0:T(512)}, u32[]{:S(2)}) copy-start(f32[512]{0:T(512)} %copy-done.78) | copy-start | bytes 6148
  230.3 8.5 %copy-start.130 = (bf16[512,3072]{1,0:T(8,128)(2,1)S(1)}, bf16[512,3072]{1,0:T(8,128)(2,1)}, u32[]{:S(2)}) copy-start(bf16[512,3072]{1,0:T(8,128)(2,1)} %copy-done.129) | copy-start | bytes 9437188
  248.9 5.8 %copy-start.21 = (s32[512,512]{1,0:T(8,128)S(1)}, s32[512,512]{1,0:T(8,128)}, u32[]{:S(2)}) copy-start(s32[512,512]{1,0:T(8,128)} %copy-done.20) | copy-start | bytes 3145732
  254.7 8.7 %copy-start.49 = (bf16[1,768]{1,0:T(2,128)(2,1)S(1)}, bf16[1,768]{1,0:T(2,128)(2,1)}, u32[]{:S(2)}) copy-start(bf16[1,768]{1,0:T(2,128)(2,1)} %param.27) | copy-start | bytes 4612
  254.7 10.0 %copy-start.94 = (f32[768]{0:T(1024)S(1)}, f32[768]{0:T(1024)}, u32[]{:S(2)}) copy-start(f32[768]{0:T(1024)} %get-tuple-element.111) | copy-start | bytes 9220
  262.5 14.8 %copy-start.30 = (bf16[768,512]{0,1:T(8,128)(2,1)S(1)}, bf16[768,512]{0,1:T(8,128)(2,1)}, u32[]{:S(2)}) copy-start(bf16[768,512]{0,1:T(8,128)(2,1)} %get-tuple-element.128) | copy-start | bytes 2359300
  286.5 7.7 %copy-start.32 = (bf16[12,64,512]{2,1,0:T(8,128)(2,1)S(1)}, bf16[12,64,512]{2,1,0:T(8,128)(2,1)}, u32[]{:S(2)}) copy-start(bf16[12,64,512]{2,1,0:T(8,128)(2,1)} %convolution_convert_fusion.12) | copy-start | bytes 2359300
  286.5 7.7 %copy-start.37 = (bf16[768,512]{1,0:T(8,128)(2,1)S(1)}, bf16[768,512]{1,0:T(8,128)(2,1)}, u32[]{:S(2)}) copy-start(bf16[768,512]{1,0:T(8,128)(2,1)} %copy.116) | copy-start | bytes 2359300
  343.4 5.6 %copy-start.11 = (f32[512,768]{1,0:T(8,128)S(1)}, f32[512,768]{1,0:T(8,128)}, u32[]{:S(2)}) copy-start(f32[512,768]{1,0:T(8,128)} %copy-done.10) | copy-start | bytes 4718596
  343.4 5.6 %copy-start.19 = (f32[512,768]{1,0:T(8,128)S(1)}, f32[512,768]{1,0:T(8,128)}, u32[]{:S(2)}) copy-start(f32[512,768]{1,0:T(8,128)} %get-tuple-element.195) | copy-start | bytes 4718596
  343.4 5.6 %copy-start.77 = (f32[512]{0:T(512)S(1)}, f32[512]{0:T(512)}, u32[]{:S(2)}) copy-start(f32[512]{0:T(512)} %copy-done.75) | copy-start | bytes 6148
  343.4 5.6 %copy-start.107 = (f32[512]{0:T(512)S(1)}, f32[512]{0:T(512)}, u32[]{:S(2)}) copy-start(f32[512]{0:T(512)} %multiply_multiply_fusion.4) | copy-start | bytes 6148
  360.6 122.7 %copy-start.63 = (bf16[3072]{0:T(1024)(128)(2,1)S(1)}, bf16[3072]{0:T(1024)(128)(2,1)}, u32[]{:S(2)}) copy-start(bf16[3072]{0:T(1024)(128)(2,1)} %get-tuple-element.170) | copy-start | bytes 18436
  492.8 5.6 %copy-start.43 = (f32[96,384]{1,0:T(8,128)S(1)}, f32[96,384]{1,0:T(8,128)}, u32[]{:S(2)}) copy-start(f32[96,384]{1,0:T(8,128)} %get-tuple-element.142) | copy-start | bytes 442372
  492.8 5.6 %copy-start.44 = (f32[96,384]{1,0:T(8,128)S(1)}, f32[96,384]{1,0:T(8,128)}, u32[]{:S(2)}) copy-start(f32[96,384]{1,0:T(8,128)} %get-tuple-element.143) | copy-start | bytes 442372
  492.8 7.2 %copy-start.82 = (f32[1,768]{1,0:T(1,128)S(1)}, f32[1,768]{1,0:T(1,128)}, u32[]{:S(2)}) copy-start(f32[1,768]{1,0:T(1,128)} %copy-done.81) | copy-start | bytes 9220
  492.8 7.2 %copy-start.95 = (f32[768]{0:T(1024)S(1)}, f32[768]{0:T(1024)}, u32[]{:S(2)}) copy-start(f32[768]{0:T(1024)} %get-tuple-element.120) | copy-start | bytes 9220
  (92 other events, 293.8 us)

commit v2 on v1

v2 whole, which is shorter than its diff:
```python
import functools

import jax
import jax.numpy as jnp
from jax import lax
from jax.experimental import pallas as pl
from jax.experimental.pallas import tpu as pltpu
from jax.sharding import PartitionSpec as P

EPSILON = 1e-06
EDGES = (12, 16, 23, 32, 46, 64, 91)
HIGHEST = lax.Precision.HIGHEST
MESH = pl.DeviceIdType.MESH
BF = jnp.bfloat16
F32 = jnp.float32


def rel_bucket(query_pos, key_pos):
    offset = key_pos[None, :] - query_pos[:, None]
    distance = jnp.abs(offset)
    far_bucket = jnp.full_like(distance, 8)
    for threshold in EDGES:
        far_bucket = far_bucket + (distance >= threshold).astype(jnp.int32)
    bucket_id = jnp.where(distance < 8, distance, far_bucket)
    return bucket_id + 16 * (offset > 0).astype(jnp.int32)


def mm(a, b):
    return jnp.dot(a, b, preferred_element_type=F32)
def mm_t(a, b):
    return lax.dot_general(a, b, (((1,), (1,)), ((), ())), preferred_element_type=F32)
def t_mm(a, b):
    return lax.dot_general(a, b, (((0,), (0,)), ((), ())), preferred_element_type=F32)

def rms_scale(v):
    return lax.rsqrt(jnp.mean(v * v, axis=-1, keepdims=True) + EPSILON)

def encode_kernel(length, x, ag, eg, fg, band, far, wq, wk, wv, wo, we, wr,
                  normed, q, k, v, probs, context_t, hidden, mixed, active, slope, block, rows, low,
                  wqs, wks, wvs, wos, wes, wrs, v_t, s_t, ctx, sems, psem, pbuf):
    n, width = x.shape
    heads = far.shape[0]
    ff = wes.shape[1]
    copies = [pltpu.make_async_copy(a, b, sems.at[i])
              for i, (a, b) in enumerate(((wq, wqs), (wk, wks), (wv, wvs), (wo, wos), (we, wes), (wr, wrs)))]
    for c in copies:
        c.start()

    @pl.loop(0, n // 128)
    def _(i):
        r = pl.ds(i * 128, 128)
        t = x[r].astype(F32)
        normed[r] = (t * rms_scale(t) * ag[...]).astype(BF)

    for w, out, c in ((wqs, q, copies[0]), (wks, k, copies[1]), (wvs, v, copies[2])):
        c.wait()

        @pl.loop(0, width // 256)
        def _(j):
            cols = pl.ds(j * 256, 256)
            out[:, cols] = mm(normed[...], w[:, cols]).astype(BF)

    lane = lax.broadcasted_iota(jnp.int32, (n, 128), 1)
    row = lax.broadcasted_iota(jnp.int32, (n, 128), 0)
    q_mark = jnp.where(lane == 0, 1.0, 0.0).astype(BF)
    k_mark = jnp.where((lane == 0) & (row >= length[0]), -1e30, 0.0).astype(BF)

    @pl.loop(0, heads // 2)
    def _(g):
        cols = pl.ds(g * 128, 128)
        v_t[...] = v[:, cols].T
        qq = jnp.concatenate([q[:, cols], q_mark], axis=1)
        kp = k[:, cols]
        for a in range(2):
            h = 2 * g + a
            mine = (lane < 64) if a == 0 else (lane >= 64)
            kk = jnp.concatenate([jnp.where(mine, kp, jnp.zeros_like(kp)), k_mark], axis=1)
            s_t[...] = mm_t(kk, qq)
            for j in range(n // 128):
                tile = []
                for i in range(n // 128):
                    s = s_t[i * 128:(i + 1) * 128, j * 128:(j + 1) * 128]
                    if abs(i - j) <= 1:
                        s = s + band[h, (i - j + 1) * 128:(i - j + 2) * 128, :]
                    elif i > j:
                        s = s + far[h, 1]
                    else:
                        s = s + far[h, 0]
                    tile.append(s)
                s = jnp.concatenate(tile, axis=0)
                m = jnp.max(s, axis=0, keepdims=True)
                e = jnp.exp(s - m)
                total = jnp.sum(e, axis=0, keepdims=True)
                pbuf[a, :, j * 128:(j + 1) * 128] = (e * (1.0 / total)).astype(BF)
            ctx[pl.ds(pl.multiple_of(h * 64, 64), 64), :] = mm(v_t[a * 64:(a + 1) * 64, :], pbuf[a]).astype(BF)
            cp = pltpu.make_async_copy(pbuf.at[a], probs.at[h], psem.at[a])
            cp.start()
        for a in range(2):
            pltpu.make_async_copy(pbuf.at[a], probs.at[2 * g + a], psem.at[a]).wait()

    context_t[...] = ctx[...]
    copies[3].wait()

    @pl.loop(0, n // 128)
    def _(i):
        r = pl.ds(i * 128, 128)
        hid = x[r].astype(F32) + t_mm(ctx[:, r], wos[...])
        hidden[r] = hid
        mixed[r] = (hid * rms_scale(hid) * eg[...]).astype(BF)

    copies[4].wait()

    @pl.loop(0, ff // 256)
    def _(j):
        cols = pl.ds(j * 256, 256)
        u = mm(mixed[...], wes[:, cols])
        u2 = u * u
        t = jnp.tanh(u * (0.7978845608 + (0.7978845608 * 0.044715) * u2))
        half = 0.5 + 0.5 * t
        active[:, cols] = (u * half).astype(BF)
        slope[:, cols] = (half + half * (1.0 - t) * u * (0.7978845608 + (3 * 0.7978845608 * 0.044715) * u2)).astype(BF)

    copies[5].wait()

    @pl.loop(0, width // 256)
    def _(j):
        cols = pl.ds(j * 256, 256)
        block[:, cols] = mm(active[...], wrs[:, cols])

    @pl.loop(0, n // 128)
    def _(i):
        r = pl.ds(i * 128, 128)
        alive = (lax.broadcasted_iota(jnp.int32, (128, 1), 0) + i * 128 < length[0]).astype(F32)
        b = alive * (hidden[r] + block[r])
        block[r] = b
        low[r] = b.astype(BF)
        rows[r] = (b * rms_scale(b) * fg[...]).astype(BF)


def encode(length, x, ag, eg, fg, band, far, wq, wk, wv, wo, we, wr):
    n, width = x.shape
    ff = we.shape[1]
    heads = far.shape[0]
    sm = pl.BlockSpec(memory_space=pltpu.SMEM)
    vm = pl.BlockSpec(memory_space=pltpu.VMEM)
    hb = pl.BlockSpec(memory_space=pl.ANY)
    S = jax.ShapeDtypeStruct
    full = S((n, width), BF)
    return pl.pallas_call(
        encode_kernel,
        out_shape=(full, full, full, full, S((heads, n, n), BF), S((width, n), BF), S((n, width), F32), full,
                   S((n, ff), BF), S((n, ff), BF), S((n, width), F32), full, full),
        in_specs=[sm, vm, vm, vm, vm, vm, sm] + [hb] * 6,
        out_specs=(vm,) * 4 + (hb,) + (vm,) * 8,
        scratch_shapes=[pltpu.VMEM(w.shape, BF) for w in (wq, wk, wv, wo, we, wr)] + [
            pltpu.VMEM((128, n), BF), pltpu.VMEM((n, n), F32), pltpu.VMEM((width, n), BF),
            pltpu.SemaphoreType.DMA((6,)), pltpu.SemaphoreType.DMA((2,)), pltpu.VMEM((2, n, n), BF)],
        compiler_params=pltpu.CompilerParams(vmem_limit_bytes=60 * 1024 * 1024),
        name="encode",
    )(length, x, ag.reshape(1, -1), eg.reshape(1, -1), fg.reshape(1, -1), band, far, wq, wk, wv, wo, we, wr)


def gelu_parts(u):
    u2 = u * u
    t = jnp.tanh(u * (0.7978845608 + (0.7978845608 * 0.044715) * u2))
    half = 0.5 + 0.5 * t
    return u * half, half + half * (1.0 - t) * u * (0.7978845608 + (3 * 0.7978845608 * 0.044715) * u2)

def norm_down(v, r, g, dy):
    vr = v * r
    gd = g * dy
    return r * (gd - vr * jnp.mean(vr * gd, axis=-1, keepdims=True)), vr * dy

def decode_kernel(length, rows, dec_in, dec_cot, sg, cg, fg, *rest):
    hbm = rest[:8]
    (out, in_grad, gains, left, right, wide, mids, rows_grad) = rest[8:16]
    bufs = rest[16:24]
    sems = rest[24]
    sv, so, cq, ck, cv, co, fe, fr = bufs
    copies = [pltpu.make_async_copy(a, b, sems.at[i]) for i, (a, b) in enumerate(zip(hbm, bufs))]
    for c in copies:
        c.start()
    n, width = rows.shape
    heads = mids.shape[1]
    size = width // heads
    x = dec_in[...].astype(F32)
    cot = dec_cot[...]
    own = (lax.broadcasted_iota(jnp.int32, (heads, width), 1) // size
           == lax.broadcasted_iota(jnp.int32, (heads, width), 0))

    def spread(r):
        return jnp.where(own, r.astype(F32), 0.0).astype(BF)

    def collect(r):
        return jnp.sum(jnp.where(own, r, 0.0), axis=0, keepdims=True)

    x_r = rms_scale(x)
    self_normed = (x * x_r * sg[...]).astype(BF)
    copies[0].wait()
    self_values = mm(self_normed, sv[...]).astype(BF)
    copies[1].wait()
    after = x + mm(self_values, so[...])
    after_r = rms_scale(after)
    cross_normed = (after * after_r * cg[...]).astype(BF)
    copies[2].wait()
    cross_q = mm(cross_normed, cq[...]).astype(BF)
    copies[3].wait()
    q_rows = mm_t(spread(cross_q), ck[...]).astype(BF)
    s = mm_t(q_rows, rows[...])
    s = jnp.where(lax.broadcasted_iota(jnp.int32, s.shape, 1) < length[0], s, -1e30)
    e = jnp.exp(s - jnp.max(s, axis=-1, keepdims=True))
    probs = e / jnp.sum(e, axis=-1, keepdims=True)
    low = probs.astype(BF)
    mean_rows = mm(low, rows[...]).astype(BF)
    copies[4].wait()
    cross_context = collect(mm(mean_rows, cv[...])).astype(BF)
    copies[5].wait()
    middle = after + mm(cross_context, co[...])
    middle_r = rms_scale(middle)
    feed_normed = (middle * middle_r * fg[...]).astype(BF)
    copies[6].wait()
    active, slope = gelu_parts(mm(feed_normed, fe[...]))
    active = active.astype(BF)
    copies[7].wait()
    out[...] = (middle + mm(active, fr[...])).astype(BF)
    upper_grad = (slope * mm_t(cot, fr[...])).astype(BF)
    middle_down, feed_gain = norm_down(middle, middle_r, fg[...], mm_t(upper_grad, fe[...]))
    middle_grad = cot.astype(F32) + middle_down
    cross_branch = middle_grad.astype(BF)
    context_grad = mm_t(cross_branch, co[...]).astype(BF)
    g_rows = mm_t(spread(context_grad), cv[...]).astype(BF)
    prob_grad = mm_t(g_rows, rows[...])
    score_grad = (probs * (prob_grad - jnp.sum(probs * prob_grad, axis=-1, keepdims=True))).astype(BF)
    score_rows = mm(score_grad, rows[...]).astype(BF)
    pad = jnp.zeros((16 - heads % 16, n), BF)
    padw = jnp.zeros((16 - heads % 16, width), BF)
    rows_grad[...] = t_mm(jnp.concatenate([score_grad, pad, low, pad], axis=0),
                          jnp.concatenate([q_rows, padw, g_rows, padw], axis=0)).astype(BF)
    cross_q_grad = collect(mm(score_rows, ck[...])).astype(BF)
    after_down, cross_gain = norm_down(after, after_r, cg[...], mm_t(cross_q_grad, cq[...]))
    after_grad = middle_grad + after_down
    self_branch = after_grad.astype(BF)
    self_values_grad = mm_t(self_branch, so[...]).astype(BF)
    x_down, self_gain = norm_down(x, x_r, sg[...], mm_t(self_values_grad, sv[...]))
    in_grad[...] = (after_grad + x_down).astype(BF)
    gains[0:1, :] = self_gain
    gains[1:2, :] = cross_gain
    gains[2:3, :] = feed_gain
    for i, r in enumerate((self_normed, self_values, cross_normed, cross_context, feed_normed)):
        left[i:i + 1, :] = r.astype(F32)
    for i, r in enumerate((self_values_grad, self_branch, cross_q_grad, cross_branch, cross_q, context_grad, cot)):
        right[i:i + 1, :] = r.astype(F32)
    wide[0:1, :] = active.astype(F32)
    wide[1:2, :] = upper_grad.astype(F32)
    mids[0] = score_rows.astype(F32)
    mids[1] = mean_rows.astype(F32)

def decode(length, rows, dec_in, dec_cot, sg, cg, fg, heads, *weights):
    n, width = rows.shape
    ff = weights[6].shape[1]
    sm = pl.BlockSpec(memory_space=pltpu.SMEM)
    vm = pl.BlockSpec(memory_space=pltpu.VMEM)
    hb = pl.BlockSpec(memory_space=pl.ANY)
    S = jax.ShapeDtypeStruct
    return pl.pallas_call(
        decode_kernel,
        out_shape=(S((1, width), BF), S((1, width), BF), S((3, width), F32), S((5, width), F32), S((7, width), F32),
                   S((2, ff), F32), S((2, heads, width), F32), S((n, width), BF)),
        in_specs=[sm] + [vm] * 6 + [hb] * 8,
        out_specs=(vm,) * 8,
        scratch_shapes=[pltpu.VMEM(w.shape, BF) for w in weights] + [pltpu.SemaphoreType.DMA((8,))],
        compiler_params=pltpu.CompilerParams(vmem_limit_bytes=60 * 1024 * 1024),
        name="decode",
    )(length, rows, dec_in, dec_cot, sg.reshape(1, -1), cg.reshape(1, -1), fg.reshape(1, -1), *weights)


def feed_back_kernel(length, rows_grad, block, cot, fg, hidden, eg, mixed, active, slope, wr, we,
                     wide, tall, hidden_grad, branch, gains, wrs, wes, bg, rb, rb_t, ug, mixed_t, dmixed, sems):
    n, width = block.shape
    ff = active.shape[1]
    groups, lanes = tall.shape[3], tall.shape[5]
    cols_dev = width // 4
    copies = [pltpu.make_async_copy(a, b, sems.at[i]) for i, (a, b) in enumerate(((wr, wrs), (we, wes)))]
    for c in copies:
        c.start()
    gains[...] = jnp.zeros_like(gains)

    @pl.loop(0, n // 128)
    def _(i):
        r = pl.ds(i * 128, 128)
        alive = (lax.broadcasted_iota(jnp.int32, (128, 1), 0) + i * 128 < length[0]).astype(F32)
        v = block[r]
        down, gain = norm_down(v, rms_scale(v), fg[...], rows_grad[r].astype(F32))
        b = alive * (cot[r].astype(F32) + down)
        bg[r] = b
        rb[r] = b.astype(BF)
        rb_t[:, pl.ds(pl.multiple_of(i * 128, 128), 128)] = b.T.astype(BF)
        mixed_t[:, pl.ds(pl.multiple_of(i * 128, 128), 128)] = mixed[r].T
        gains[0:1, :] += jnp.sum(gain, axis=0, keepdims=True)

    copies[0].wait()

    @pl.loop(0, ff // 256)
    def _(j):
        cols = pl.ds(pl.multiple_of(j * 256, 256), 256)
        ug[:, cols] = (slope[:, cols].astype(F32) * mm_t(rb[...], wrs[cols, :])).astype(BF)

    copies[1].wait()

    @pl.loop(0, width // 256)
    def _(j):
        cols = pl.ds(pl.multiple_of(j * 256, 256), 256)
        dmixed[:, cols] = mm_t(ug[...], wes[cols, :])

    @pl.loop(0, n // 128)
    def _(i):
        r = pl.ds(i * 128, 128)
        v = hidden[r]
        down, gain = norm_down(v, rms_scale(v), eg[...], dmixed[r])
        h = bg[r] + down
        hidden_grad[r] = h
        branch[r] = h.astype(BF)
        gains[1:2, :] += jnp.sum(gain, axis=0, keepdims=True)

    @pl.loop(0, 4)
    def _(j):
        for half in range(2):
            cols = pl.ds(pl.multiple_of(j * (ff // 4) + half * (ff // 8), 128), ff // 8)
            wide[half, lax.rem(j, 2), j // 2] = mm(mixed_t[...], ug[:, cols]).astype(BF)

    chunk = ff // 8
    per_group = lanes // chunk

    @pl.loop(0, 8)
    def _(i):
        cols = pl.ds(pl.multiple_of(i * chunk, 128), chunk)
        g = mm(rb_t[...], active[:, cols]).astype(BF)
        for j in range(4):
            for half in range(2):
                r = j * cols_dev + half * (cols_dev // 2)
                part = g[r:r + cols_dev // 2]
                if per_group == 1:
                    tall[half, j % 2, j // 2, i] = part
                else:
                    tall[half, j % 2, j // 2, 0, :, cols] = part


def feed_back(groups, length, rows_grad, block, cot, fg, hidden, eg, mixed, active, slope, wr, we):
    n, width = block.shape
    ff = active.shape[1]
    sm = pl.BlockSpec(memory_space=pltpu.SMEM)
    vm = pl.BlockSpec(memory_space=pltpu.VMEM)
    hb = pl.BlockSpec(memory_space=pl.ANY)
    S = jax.ShapeDtypeStruct
    V = pltpu.VMEM
    return pl.pallas_call(
        feed_back_kernel,
        out_shape=(S((2, 2, 2, width, ff // 8), BF),
                   S((2, 2, 2, groups, width // 8, ff // groups), BF), S((n, width), F32), S((n, width), BF), S((2, width), F32)),
        in_specs=[sm] + [vm] * 9 + [hb] * 2,
        out_specs=(vm,) * 5,
        scratch_shapes=[V(wr.shape, BF), V(we.shape, BF), V((n, width), F32), V((n, width), BF), V((width, n), BF),
                        V((n, ff), BF), V((width, n), BF), V((n, width), F32), pltpu.SemaphoreType.DMA((2,))],
        compiler_params=pltpu.CompilerParams(vmem_limit_bytes=60 * 1024 * 1024),
        name="feed_back",
    )(length, rows_grad, block, cot, fg.reshape(1, -1), hidden, eg.reshape(1, -1), mixed, active, slope, wr, we)


def attend_back_kernel(x, ag, q, k, v, probs, context_t, branch, hidden_grad, normed, wq, wk, wv, wo,
                       units, in_grad, gain_out, band, far,
                       wqs, wks, wvs, wos, d_out, dp, ds, dq_t, dq, dk, dv, k_t, normed_t, ng, pbuf, psem, sems):
    n, width = x.shape
    heads = probs.shape[0]
    copies = [pltpu.make_async_copy(a, b, sems.at[i])
              for i, (a, b) in enumerate(((wo, wos), (wq, wqs), (wk, wks), (wv, wvs)))]
    for c in copies:
        c.start()

    def fetch(h, slot):
        return pltpu.make_async_copy(probs.at[h], pbuf.at[slot], psem.at[slot])

    fetch(0, 0).start()
    fetch(1, 1).start()
    far[...] = jnp.zeros_like(far)
    copies[0].wait()

    @pl.loop(0, width // 256)
    def _(j):
        cols = pl.ds(pl.multiple_of(j * 256, 256), 256)
        d_out[:, cols] = mm_t(branch[...], wos[cols, :]).astype(BF)

    lane = lax.broadcasted_iota(jnp.int32, (n, 128), 1)

    @pl.loop(0, heads // 2)
    def _(g):
        cols = pl.ds(pl.multiple_of(g * 128, 128), 128)
        k_t[...] = k[:, cols].T
        dop = d_out[:, cols]
        qp = q[:, cols]
        vp = v[:, cols]
        zero = jnp.zeros_like(qp)
        dk_sum = None
        for a in range(2):
            h = 2 * g + a
            mine = (lane < 64) if a == 0 else (lane >= 64)
            dp[...] = mm_t(jnp.where(mine, vp, zero), dop)
            fetch(h, a).wait()
            for j in range(n // 128):
                p = pbuf[a, :, j * 128:(j + 1) * 128].astype(F32)
                pd = p * dp[:, j * 128:(j + 1) * 128]
                total = jnp.sum(pd, axis=0, keepdims=True)
                s = pd - p * total
                ds[:, j * 128:(j + 1) * 128] = s.astype(BF)
                for i in range(n // 128):
                    t = s[i * 128:(i + 1) * 128]
                    if abs(i - j) <= 1:
                        if j == 0 or (i == j + 1 and j == 0) or (j == 1 and i == 0):
                            band[h, (i - j + 1) * 128:(i - j + 2) * 128, :] = t
                        else:
                            band[h, (i - j + 1) * 128:(i - j + 2) * 128, :] += t
                    else:
                        w = 1 if i > j else 0
                        far[w, pl.ds(h, 1), :] += jnp.sum(t, axis=0, keepdims=True)
            dvp = mm(pbuf[a], jnp.where(mine, dop, zero))
            dkp = mm(ds[...], jnp.where(mine, qp, zero))
            dq_t[pl.ds(pl.multiple_of(h * 64, 64), 64), :] = mm(k_t[a * 64:(a + 1) * 64, :], ds[...]).astype(BF)
            if a == 0:
                dk_sum, dv_sum = dkp, dvp
            else:
                dk[:, cols] = (dk_sum + dkp).astype(BF)
                dv[:, cols] = (dv_sum + dvp).astype(BF)

            @pl.when(h + 2 < heads)
            def _():
                fetch(h + 2, a).start()

    @pl.loop(0, n // 128)
    def _(i):
        r = pl.ds(pl.multiple_of(i * 128, 128), 128)
        dq[r] = dq_t[:, r].T
        normed_t[:, r] = normed[r].T

    for c in copies[1:]:
        c.wait()

    @pl.loop(0, width // 256)
    def _(j):
        cols = pl.ds(pl.multiple_of(j * 256, 256), 256)
        ng[:, cols] = mm_t(dq[...], wqs[cols, :]) + mm_t(dk[...], wks[cols, :]) + mm_t(dv[...], wvs[cols, :])

    gain_out[...] = jnp.zeros_like(gain_out)

    @pl.loop(0, n // 128)
    def _(i):
        r = pl.ds(i * 128, 128)
        t = x[r].astype(F32)
        down, gain = norm_down(t, rms_scale(t), ag[...], ng[r])
        in_grad[r] = (hidden_grad[r] + down).astype(BF)
        gain_out[...] += jnp.sum(gain, axis=0, keepdims=True)

    part = width // 4
    zero = jnp.zeros((n, part), BF)
    for j in range(4):
        c = slice(j * part, (j + 1) * part)
        g = mm(normed_t[...], jnp.concatenate([dq[:, c], dk[:, c]], axis=1))
        units[0, j % 2, j // 2] = g.astype(BF)
        g = (mm(normed_t[...], jnp.concatenate([dv[:, c], zero], axis=1))
             + mm(context_t[...], jnp.concatenate([zero, branch[:, c]], axis=1)))
        units[1, j % 2, j // 2] = g.astype(BF)


def attend_back(x, ag, q, k, v, probs, context_t, branch, hidden_grad, normed, wq, wk, wv, wo):
    n, width = x.shape
    heads = probs.shape[0]
    vm = pl.BlockSpec(memory_space=pltpu.VMEM)
    hb = pl.BlockSpec(memory_space=pl.ANY)
    S = jax.ShapeDtypeStruct
    V = pltpu.VMEM
    nar = V((n, width), BF)
    return pl.pallas_call(
        attend_back_kernel,
        out_shape=(S((2, 2, 2, width, width // 2), BF), S((n, width), BF), S((1, width), F32),
                   S((heads, 384, 128), F32), S((2, heads, 128), F32)),
        in_specs=[vm] * 5 + [hb] + [vm] * 4 + [hb] * 4,
        out_specs=(vm,) * 5,
        scratch_shapes=[V(w.shape, BF) for w in (wq, wk, wv, wo)] + [
            nar, V((n, n), F32), V((n, n), BF), V((width, n), BF), nar, nar, nar, V((128, n), BF),
            V((width, n), BF), V((n, width), F32), V((2, n, n), BF), pltpu.SemaphoreType.DMA((2,)), pltpu.SemaphoreType.DMA((4,))],
        compiler_params=pltpu.CompilerParams(vmem_limit_bytes=60 * 1024 * 1024),
        name="attend_back",
    )(x, ag.reshape(1, -1), q, k, v, probs, context_t, branch, hidden_grad, normed, wq, wk, wv, wo)


def exchange_kernel(np_, ns, wide, tall, attn, small, dec, enc, red, small_out, dec_out, enc_out,
                    own, r0, r1a, r1b, s1a, s1b, r2, s2, r3, sm, smr, smz,
                    loc, s0s, s0r, s1s, s1r, s2s, s2r, s3s, s3r,
                    ms, mr, mzs, mzr, ds, dr, es, er):
    units = 6
    nz = np_ // 2
    p = lax.axis_index("pairs")
    s = lax.axis_index("seq")
    c = lax.rem(s, 2)
    y = s // 2
    x = lax.rem(p, 2)
    z = p // 2
    me = p * ns + s
    count = np_ * ns
    core_peer = (p, s + 1 - 2 * c)
    y_peer = (p, lax.rem(s + 2, 4))
    x_peer = (p + 1 - 2 * x, s)

    def place(d):
        lin = lax.rem(me + d, count)
        return (lin // ns, lax.rem(lin, ns))

    barrier = pltpu.get_barrier_semaphore()

    @pl.loop(1, count)
    def _(d):
        pl.semaphore_signal(barrier, inc=1, device_id=place(d), device_id_type=MESH)

    pl.semaphore_wait(barrier, count - 1)

    def remote(src, dst, send, recv, peer):
        return pltpu.make_async_remote_copy(
            src_ref=src, dst_ref=dst, send_sem=send, recv_sem=recv,
            device_id=peer, device_id_type=MESH)

    def unit(k, core):
        return (wide, tall, attn)[k // 2].at[k % 2, core]

    def core_copy(k):
        return remote(unit(k, 1 - c), r0.at[k], s0s.at[k], s0r.at[k], core_peer)

    def own_copy(k):
        return pltpu.make_async_copy(unit(k, c), own.at[k], loc.at[k])

    for k in range(units):
        core_copy(k).start()
        own_copy(k).start()

    def dec_copy(d):
        q = place(d)
        return remote(dec.at[q[0] * ns + q[1]], dec_out.at[me], ds.at[d], dr.at[d], q)

    keep_dec = pltpu.make_async_copy(dec.at[me], dec_out.at[me], loc.at[units])
    keep_dec.start()

    @pl.loop(1, count)
    def _(d):
        dec_copy(d).start()

    def enc_copy(d):
        t = lax.rem(s + d, ns)
        return remote(enc.at[:, t], enc_out.at[:, s], es.at[d], er.at[d], (p, t))

    keep_enc = pltpu.make_async_copy(enc.at[:, s], enc_out.at[:, s], loc.at[units + 1])
    keep_enc.start()
    for d in range(1, ns):
        enc_copy(d).start()

    sm[0] = small[...]
    for i, peer in enumerate((core_peer, y_peer, x_peer)):
        copy = remote(sm.at[i], smr.at[i], ms.at[i], mr.at[i], peer)
        copy.start()
        copy.wait()
        if i < 2:
            sm[i + 1] = sm[i] + smr[i]
        else:
            smz[z] = sm[i] + smr[i]

    def z_small(d):
        return remote(smz.at[z], smz.at[z], mzs.at[d], mzr.at[d],
                      (lax.rem(z + d, nz) * 2 + x, s))

    @pl.loop(1, nz)
    def _(d):
        z_small(d).start()

    def y_first(k):
        return remote(own.at[2 * k, 1 - y], r1a.at[k], s1s.at[2 * k], s1r.at[2 * k], y_peer)

    def x_first(k):
        return remote(own.at[2 * k + 1, :, :, 1 - x], r1b.at[k], s1s.at[2 * k + 1],
                      s1r.at[2 * k + 1], x_peer)

    def x_second(k):
        return remote(s1a.at[k, :, 1 - x], r2.at[2 * k], s2s.at[2 * k], s2r.at[2 * k], x_peer)

    def y_second(k):
        return remote(s1b.at[k, 1 - y], r2.at[2 * k + 1], s2s.at[2 * k + 1],
                      s2r.at[2 * k + 1], y_peer)

    def z_last(k, d):
        t = lax.rem(z + d, nz)
        return remote(s2.at[k, t], r3.at[k, d], s3s.at[k, d], s3r.at[k, d], (t * 2 + x, s))

    def stage0(k):
        core_copy(k).wait()
        own_copy(k).wait()

        @pl.loop(0, 2)
        def _(a):
            @pl.loop(0, nz)
            def _(b):
                for e in range(2):
                    own[k, a, b, e] = (own[k, a, b, e].astype(F32)
                                       + r0[k, a, b, e].astype(F32)).astype(BF)

    for k in range(units // 2):
        stage0(2 * k)
        y_first(k).start()
        stage0(2 * k + 1)
        x_first(k).start()

    @pl.loop(0, units // 2)
    def _(k):
        y_first(k).wait()

        @pl.loop(0, nz)
        def _(b):
            for e in range(2):
                s1a[k, b, e] = (own[2 * k, y, b, e].astype(F32)
                                + r1a[k, b, e].astype(F32)).astype(BF)

        x_second(k).start()
        x_first(k).wait()

        @pl.loop(0, nz)
        def _(b):
            for e in range(2):
                s1b[k, e, b] = (own[2 * k + 1, e, b, x].astype(F32)
                                + r1b[k, e, b].astype(F32)).astype(BF)

        y_second(k).start()

    @pl.loop(0, units // 2)
    def _(k):
        x_second(k).wait()

        @pl.loop(0, nz)
        def _(b):
            s2[2 * k, b] = (s1a[k, b, x].astype(F32) + r2[2 * k, b].astype(F32)).astype(BF)

        @pl.loop(1, nz)
        def _(d):
            z_last(2 * k, d).start()

        y_second(k).wait()

        @pl.loop(0, nz)
        def _(b):
            s2[2 * k + 1, b] = (s1b[k, y, b].astype(F32)
                                + r2[2 * k + 1, b].astype(F32)).astype(BF)

        @pl.loop(1, nz)
        def _(d):
            z_last(2 * k + 1, d).start()

    @pl.loop(0, units)
    def _(k):
        red[k] = s2[k, z].astype(F32)

        @pl.loop(1, nz)
        def _(d):
            z_last(k, d).wait()
            red[k] = red[k] + r3[k, d].astype(F32)

    @pl.loop(1, nz)
    def _(d):
        z_small(d).wait()

    small_out[...] = smz[0]

    @pl.loop(1, nz)
    def _(d):
        small_out[...] = small_out[...] + smz[d]

    keep_dec.wait()
    keep_enc.wait()
    for d in range(1, ns):
        enc_copy(d).wait()

    @pl.loop(1, count)
    def _(d):
        dec_copy(d).wait()


def exchange(np_, ns, wide, tall, attn, small, dec, enc):
    units = 6
    half = units // 2
    nz = np_ // 2
    rows, cols = wide.shape[5:]
    count = np_ * ns
    dma = pltpu.SemaphoreType.DMA
    anywhere = pl.BlockSpec(memory_space=pl.ANY)
    vmem = pl.BlockSpec(memory_space=pltpu.VMEM)
    return pl.pallas_call(
        functools.partial(exchange_kernel, np_, ns),
        out_shape=(
            jax.ShapeDtypeStruct((units, rows, cols), F32),
            jax.ShapeDtypeStruct(small.shape, F32),
            jax.ShapeDtypeStruct(dec.shape, BF),
            jax.ShapeDtypeStruct(enc.shape, BF),
        ),
        in_specs=[anywhere, anywhere, anywhere, vmem, anywhere, anywhere],
        out_specs=(vmem, vmem, anywhere, anywhere),
        scratch_shapes=[
            pltpu.VMEM((units, 2, nz, 2, rows, cols), BF),
            pltpu.VMEM((units, 2, nz, 2, rows, cols), BF),
            pltpu.VMEM((half, nz, 2, rows, cols), BF),
            pltpu.VMEM((half, 2, nz, rows, cols), BF),
            pltpu.VMEM((half, nz, 2, rows, cols), BF),
            pltpu.VMEM((half, 2, nz, rows, cols), BF),
            pltpu.VMEM((units, nz, rows, cols), BF),
            pltpu.VMEM((units, nz, rows, cols), BF),
            pltpu.VMEM((units, nz, rows, cols), BF),
            pltpu.VMEM((3,) + small.shape, F32),
            pltpu.VMEM((3,) + small.shape, F32),
            pltpu.VMEM((nz,) + small.shape, F32),
            dma((units + 2,)),
            dma((units,)), dma((units,)), dma((units,)), dma((units,)),
            dma((units,)), dma((units,)), dma((units, nz)), dma((units, nz)),
            dma((3,)), dma((3,)), dma((nz,)), dma((nz,)),
            dma((count,)), dma((count,)), dma((ns,)), dma((ns,)),
        ],
        compiler_params=pltpu.CompilerParams(
            collective_id=0, has_side_effects=True, vmem_limit_bytes=58 * 1024 * 1024),
        name="exchange",
    )(wide, tall, attn, small, dec, enc)


def per_device(
    enc_input, dec_input, lengths, attend_gain, query_weight, key_weight, value_weight,
    output_weight, bias_table, expand_gain, expand_weight, reduce_weight, final_gain,
    self_gain, self_value, self_output, cross_gain, cross_query, cross_key, cross_value,
    cross_output, feed_gain, feed_expand, feed_reduce, enc_cotangent, dec_cotangent,
):
    group, local_rows, width = enc_input.shape
    buckets, heads = bias_table.shape
    size = width // heads
    ff = expand_weight.shape[1]
    ns = lax.axis_size("seq")
    np_ = lax.axis_size("pairs")
    place = lax.axis_index("seq")
    seq_len = local_rows * ns
    length = lax.dynamic_slice_in_dim(lengths, place, 1)
    x = lax.all_to_all(enc_input, "seq", split_axis=0, concat_axis=1, tiled=True)[0]
    cot = lax.all_to_all(enc_cotangent, "seq", split_axis=0, concat_axis=1, tiled=True)[0]

    band_bucket = rel_bucket(jnp.arange(128), jnp.arange(384) - 128).T
    onehot = (jnp.arange(buckets, dtype=jnp.int32)[:, None, None] == band_bucket).astype(F32)
    band = jnp.einsum("but,bh->hut", onehot, bias_table, precision=HIGHEST)
    far = jnp.stack([bias_table[15], bias_table[31]], axis=1)

    (normed, query, key, value, probs, context_t, hidden, mixed, active, slope, block, enc_rows,
     encoded) = encode(length, x, attend_gain, expand_gain, final_gain, band, far, query_weight,
                       key_weight, value_weight, output_weight, expand_weight, reduce_weight)
    dec_block, dec_input_grad, dec_gains, left, right, wide_rows, mids, rows_grad = decode(
        length, enc_rows, dec_input, dec_cotangent, self_gain, cross_gain, feed_gain, heads,
        self_value, self_output, cross_query, cross_key, cross_value, cross_output, feed_expand,
        feed_reduce)
    nz = np_ // 2
    r = width // np_
    aligned = r % 16 == 0 and (ff // np_) % 128 == 0
    wide, tall, hidden_grad, branch, feed_gains = feed_back(
        np_ if aligned else 1, length, rows_grad, block, cot, final_gain, hidden, expand_gain,
        mixed, active, slope, reduce_weight, expand_weight)
    attn, input_grad, attend_gain_sum, band_grad, far_grad = attend_back(
        x, attend_gain, query, key, value, probs, context_t, branch, hidden_grad, normed,
        query_weight, key_weight, value_weight, output_weight)
    far_sum = jnp.sum(far_grad, axis=-1)
    grad_bias = jnp.einsum("but,hut->bh", onehot, band_grad, precision=HIGHEST)
    grad_bias = grad_bias.at[15].add(far_sum[0]).at[31].add(far_sum[1])

    rp = -(-r // 16) * 16
    lanes = ff // 8
    side = width // 8 // r

    def pad(unit):
        return jnp.pad(unit, ((0, 0),) * 5 + ((0, rp - r), (0, 0)))

    if aligned:
        tall = tall.reshape(2, 2, 2, nz, 2, r, lanes)
    else:
        tall = tall.reshape(2, 2, 2, r, side, nz, 2, ff // np_).transpose(0, 1, 2, 5, 6, 3, 4, 7)
        tall = pad(tall.reshape(2, 2, 2, nz, 2, r, lanes))
    wide = pad(wide.reshape(2, 2, 2, nz, 2, r, lanes))
    attn = pad(attn.reshape(2, 2, 2, nz, 2, r, lanes))
    cols = width // ns
    small = jnp.concatenate([
        dec_gains, feed_gains, attend_gain_sum,
        jnp.pad(grad_bias.reshape(1, -1), ((0, 1), (0, width - grad_bias.size)))])

    left_cut = jnp.concatenate([
        left.reshape(5, np_, r).transpose(1, 0, 2).reshape(np_, 5 * r),
        wide_rows[0].reshape(np_, 4 * r),
    ], axis=1)
    mid_cut = mids.reshape(2, ns, heads // ns, np_, r).transpose(3, 1, 0, 2, 4)
    mid_cut = mid_cut.reshape(np_, ns, 6 * r)
    right_cut = jnp.concatenate([
        right.reshape(7, ns, cols).transpose(1, 0, 2).reshape(ns, 7 * cols),
        wide_rows[1].reshape(ns, 4 * cols)], axis=1)
    dec_all = jnp.concatenate([
        jnp.broadcast_to(left_cut[:, None], (np_, ns, 9 * r)), mid_cut,
        jnp.broadcast_to(right_cut[None], (np_, ns, 11 * cols))], axis=-1)
    dec_all = dec_all.astype(BF).reshape(np_ * ns, -1)
    used = dec_all.shape[1]
    dec_rows = -(-used // 2048) * 16
    dec_all = jnp.pad(dec_all, ((0, 0), (0, dec_rows * 128 - used)))
    dec_all = dec_all.reshape(np_ * ns, dec_rows, 128)
    both = jnp.stack([encoded, input_grad]).reshape(2, ns, local_rows, width)

    red, small_sum, dec_got, both_out = exchange(np_, ns, wide, tall, attn, small, dec_all, both)

    got = dec_got.reshape(np_ * ns, -1)
    lefts = got[:, :9 * r].reshape(-1, 9, r)
    mid_got = got[:, 9 * r:15 * r].reshape(-1, 2, 3, r)
    rights = got[:, 15 * r:15 * r + 11 * cols].reshape(-1, 11, cols)
    plain = jnp.einsum("nkr,nkc->krc", lefts[:, :4], rights[:, :4], preferred_element_type=F32)
    crossed = jnp.einsum("nkhr,nkhd->krhd", mid_got, rights[:, 4:6].reshape(-1, 2, 3, size),
                         preferred_element_type=F32).reshape(2, r, cols)
    feed_in = jnp.einsum("nr,nc->rc", lefts[:, 4], rights[:, 7:11].reshape(-1, 4 * cols),
                         preferred_element_type=F32)
    feed_out = jnp.einsum("nr,nc->rc", lefts[:, 5:9].reshape(-1, 4 * r), rights[:, 6],
                          preferred_element_type=F32)
    red = red[:, :r]
    grad_reduce = red[2:4].reshape(2, r, side, ff // np_).reshape(cols, ff // np_).T
    bias = small_sum[6, :bias_table.size].reshape(bias_table.shape)
    return (
        both_out[0], dec_block, both_out[1], dec_input_grad,
        small_sum[5],
        red[4][:, :cols], red[4][:, cols:], red[5][:, :cols], red[5][:, cols:],
        bias,
        small_sum[4],
        jnp.concatenate([red[0], red[1]], axis=1), grad_reduce,
        small_sum[3],
        small_sum[0], plain[0], plain[1],
        small_sum[1], plain[2], crossed[0], crossed[1], plain[3],
        small_sum[2], feed_in, feed_out,
    )


def solution(mesh):
    rows = P("pairs", "seq", None)
    single = P(("pairs", "seq"), None)
    block = P("pairs", "seq")
    return jax.shard_map(
        per_device,
        mesh=mesh,
        in_specs=(rows, single, P("pairs")) + (P(),) * 21 + (rows, single),
        out_specs=(
            rows, single, rows, single,
            P(), block, block, block, block, P(), P(), block, block, P(),
            P(), block, block, P(), block, block, block, block, P(), block, block,
        ),
        check_vma=False,
    )
```

time: 509 us -> 287 us (0.56); the launches traced: 501 us -> 286 us
  matrix products: 168 us -> 7.65 us
  local copies, waits for them, and re-layouts: 150 us -> 22.9 us
  Pallas kernels: 118 us -> 229 us
  other arithmetic: 49.5 us -> 5.39 us
  waiting for transfers between devices: 0.01 us -> 11.5 us
  between operations: 6.78 us -> 1.14 us
    dot_general x48 -> x3, matrix products: 166 us -> 5.51 us  [the longest x1 3.31 us: per_device(): grad_bias = jnp.einsum('but,hut->bh', onehot, band_grad, precision=HIGHEST)]
    pallas_call x0 -> x4, Pallas kernels: none -> 111 us  [the longest x1 37.8 us: encode(): pl.pallas_call(encode_kernel, out_shape=(full, full, full, full, S((heads...]
    reshape x10 -> x15, local copies, waits for them, and re-layouts: 35 us -> 4.19 us  [the longest x1 0.58 us: encode(): ag.reshape(1, -1)]
    unnamed x301 -> x44, local copies, waits for them, and re-layouts: 27.9 us -> 4.25 us
    convert_element_type x13 -> x0, local copies, waits for them, and re-layouts: 23.5 us -> none  [the longest x1 14.5 us: per_device(): score_grad = (probs * (prob_grad - jnp.sum(probs * prob_grad, axis=-1, ke...]
    another operation x8 -> x5, local copies, waits for them, and re-layouts: 18.2 us -> 0.84 us  [the longest x1 0.69 us: per_device(): far = jnp.stack([bias_table[15], bias_table[31]], axis=1)]
    dot_general x3 -> x1, local copies, waits for them, and re-layouts: 19.3 us -> 2.15 us  [per_device(): band = jnp.einsum('but,bh->hut', onehot, bias_table, precision=HIGHEST)]
    convert_element_type x14 -> x0, other arithmetic: 16.7 us -> none  [the longest x1 7.02 us: per_device(): score_grad = (probs * (prob_grad - jnp.sum(probs * prob_grad, axis=-1, ke...]
  transfers between devices with their start and end apart: 2 -> 2, of which waited for: 0 -> 1; matrix products, arithmetic and copies ran while one was open for 25% -> 3% of each run, Pallas kernels for 0% -> 19%
where the time goes in v2:
time: 287 us; the launch traced here: 286 us
  Pallas kernels  229 us (80%)
  local copies, waits for them, and re-layouts  22.9 us (8%)
  waiting for transfers between devices  11.5 us (4%)
  starting transfers between devices  8.58 us (3%)
  matrix products  7.65 us (3%)
  other arithmetic  5.39 us (2%)
    pallas_call x1, Pallas kernels, exchange(): pl.pallas_call(functools.partial(exchange_kernel, np_, ns), out_shape=(ja...  118 us
    pallas_call x1, Pallas kernels, encode(): pl.pallas_call(encode_kernel, out_shape=(full, full, full, full, S((heads...  37.8 us
    pallas_call x1, Pallas kernels, attend_back(): pl.pallas_call(attend_back_kernel, out_shape=(S((2, 2, 2, width, width //...  29.4 us
    pallas_call x1, Pallas kernels, feed_back(): pl.pallas_call(feed_back_kernel, out_shape=(S((2, 2, 2, width, ff // 8),...  28.9 us
    pallas_call x1, Pallas kernels, decode(): pl.pallas_call(decode_kernel, out_shape=(S((1, width), BF), S((1, width),...  15.3 us
    all_to_all x1, waiting for transfers between devices, per_device(): lax.all_to_all(enc_input, 'seq', split_axis=0, concat_axis=1, tiled=True)[0]  11.5 us
  transfers between devices with their start and end apart: 2, of which 1 were waited for; matrix products, arithmetic and copies ran while one was open for 3% of the time, Pallas kernels for 19%

profile of v2, /device:TPU:0, one launch (start us, length us, event | category | flops | bytes accessed | tf_op | source)
XLA Modules:
  0.0 286.3 jit_solution(185331311526062516)
XLA Ops:
  0.7 4.4 %all-to-all-start = ((bf16[4,128,768]{2,1,0:T(8,128)(2,1)}), bf16[4,128,768]{2,1,0:T(8,128)(2,1)S(1)}, u32[]{:S(2)}, u32[]{:S(2)}) async-start(bf16[4,128,768]{2,1,0:T(8,128)(2,1)} %param.30), calls=%async_computation | async-start | bytes 1572864 | tf_op jit(solution)/shard_map/all_to_all | solution.py:748
  5.1 0.2 slice_reduce_fusion.3
  5.3 11.5 %all-to-all-done = bf16[4,128,768]{2,1,0:T(8,128)(2,1)S(1)} async-done(((bf16[4,128,768]{2,1,0:T(8,128)(2,1)}), bf16[4,128,768]{2,1,0:T(8,128)(2,1)S(1)}, u32[]{:S(2)}, u32[]{:S(2)}) %all-to-all-start) | async-done | bytes 786464 | tf_op jit(solution)/shard_map/all_to_all | solution.py:748
  16.8 4.2 %all-to-all-start.1 = ((bf16[4,128,768]{2,1,0:T(8,128)(2,1)}), bf16[4,128,768]{2,1,0:T(8,128)(2,1)}, u32[]{:S(2)}, u32[]{:S(2)}) async-start(bf16[4,128,768]{2,1,0:T(8,128)(2,1)} %param.54), calls=%async_computation.1 | async-start | bytes 1572864 | tf_op jit(solution)/shard_map/all_to_all | solution.py:749
  21.0 0.6 reshape.248.ag
  21.6 0.6 reshape.249.eg
  22.2 0.6 reshape.250.fg
  22.8 0.6 reshape.251.sg
  23.3 0.6 reshape.252.cg
  23.9 0.6 reshape.253.fg
  24.5 0.7 copy.98.far
  25.2 0.2 fusion.5
  25.4 2.0 fusion.1
  27.4 2.1 copy.97
  29.6 0.6 dynamic_slice.3.length
  30.1 37.8 %encode.1 = (bf16[512,768]{1,0:T(8,128)(2,1)}, bf16[512,768]{1,0:T(8,128)(2,1)}, bf16[512,768]{1,0:T(8,128)(2,1)}, bf16[512,768]{1,0:T(8,128)(2,1)}, bf16[12,512...) custom-call(s32[1]{0:T(128)} %dynamic_slice.3.length, ...), custom_call_target="tpu_custom_call" | custom-call | tf_op jit(solution)/shard_map/encode/pallas_call | solution.py:149
  68.0 15.3 %decode.1 = (bf16[1,768]{1,0:T(2,128)(2,1)}, bf16[1,768]{1,0:T(2,128)(2,1)}, f32[3,768]{1,0:T(4,128)}, f32[5,768]{1,0:T(8,128)}, f32[7,768]{1,0:T(8,128)}, /*ind...) custom-call(s32[1]{0:T(128)} %dynamic_slice.3.length, bf16[512,768]{1,0:T(8,128)(2,1)} %get-tuple-element.84.rows, ...), custom_call_target="tpu_custom_call" | custom-call | tf_op jit(solution)/shard_map/decode/pallas_call | solution.py:265
  83.3 28.9 %feed_back.1 = (bf16[2,2,2,768,384]{4,3,2,1,0:T(8,128)(2,1)}, bf16[2,2,2,8,96,384]{5,4,3,2,1,0:T(8,128)(2,1)}, f32[512,768]{1,0:T(8,128)}, bf16[512,768]{1,0:T(8,128)(2,1)}, f32[2,768]{1,0:T(2,128)}) custom-call(s32[1]{0:T(128)} %dynamic_slice.3.length, bf16[512,768]{1,0:T(8,128)(2,1)} %get-tuple-element.85.rows_grad, f32[512,768]{1,0:T(8,128)} %get-tuple-element.86.block, ...), custom_call_target="tpu_custom_call" | custom-call | tf_op jit(solution)/shard_map/feed_back/pallas_call | solution.py:356
  112.3 29.4 %attend_back.1 = (bf16[2,2,2,768,384]{4,3,2,1,0:T(8,128)(2,1)}, bf16[512,768]{1,0:T(8,128)(2,1)}, f32[1,768]{1,0:T(1,128)}, f32[12,384,128]{2,1,0:T(8,128)}, f32[2,12,128]{2,1,0:T(8,128)}) custom-call(bf16[512,768]{1,0:T(8,128)(2,1)} %bitcast.69, f32[1,768]{1,0:T(1,128)} %reshape.248.ag, bf16[512,768]{1,0:T(8,128)(2,1)} %get-tuple-element.93.q, ...), custom_call_target="tpu_custom_call" | custom-call | tf_op jit(solution)/shard_map/attend_back/pallas_call | solution.py:480
  141.7 0.8 reduce_sum.9
  143.9 0.2 concatenate.34
  144.1 0.7 copy.123
  144.8 2.7 copy.99
  147.5 3.3 %fusion.4 = f32[32,12]{0,1:T(8,128)S(1)} fusion(f32[12,384,128]{1,0,2:T(8,128)S(1)} %copy.99, s32[384,128]{0,1:T(8,128)S(1)} %fusion.5), kind=kOutput, calls=%fused_computation.7 | convolution fusion | flops 228065280 | bytes 2557440 | tf_op jit(solution)/shard_map/but,hut->bh/dot_general | solution.py:773
  151.2 0.1 reshape.257
  151.4 2.7 pad_maximum_fusion.enc
  154.1 0.6 select_maximum_fusion.small
  154.7 117.7 %exchange.1 = (f32[6,96,384]{2,1,0:T(8,128)}, f32[8,768]{1,0:T(8,128)}, bf16[32,32,128]{2,1,0:T(8,128)(2,1)}, bf16[2,4,128,768]{3,2,1,0:T(8,128)(2,1)}) custom-call(bf16[2,2,2,4,2,96,384]{6,5,4,3,2,1,0:T(8,128)(2,1)} %bitcast.70, bf16[2,2,2,4,2,96,384]{6,5,4,3,2,1,0:T(8,128)(2,1)} %bitcast.71, bf16[2,2,2,4,2,96,384]{6,5,4,3,2,1,0:T(8,128)(2,1)} %bitcast.72, ...), custom_call_target="tpu_custom_call" | custom-call | tf_op jit(solution)/shard_map/exchange/pallas_call | solution.py:698
  272.5 0.8 slice_reduce_fusion.10
  273.3 1.7 slice_reduce_fusion.4
  275.0 1.1 copy.144
  276.2 0.1 slice.208
  276.3 0.1 reshape.265
  276.5 0.3 reshape.266
  276.9 0.7 slice.179
  277.7 1.2 slice_bitcast_fusion
  279.1 0.7 copy.112
  279.7 0.1 reshape.268
  279.9 0.1 reshape.273
  280.2 0.2 convolution_bitcast_fusion
  280.4 0.7 copy.114
  281.1 0.7 copy.113
  281.9 0.2 fusion.15
  282.1 0.8 slice_bitcast_fusion.6
  282.9 0.9 fusion.23
  283.8 1.0 fusion.20
  284.8 0.7 pad_maximum_fusion.1
  285.5 0.8 fusion.29
  (80 shorter events, 2.4 us)
Async XLA Ops:
  0.7 4.5 %copy-start.4 = (f32[32,12]{0,1:T(8,128)S(1)}, f32[32,12]{0,1:T(8,128)}, u32[]{:S(2)}) copy-start(f32[32,12]{0,1:T(8,128)} %param.38) | copy-start | bytes 4612
  0.7 20.3 %copy-start.10 = (f32[768]{0:T(1024)S(1)}, f32[768]{0:T(1024)}, u32[]{:S(2)}) copy-start(f32[768]{0:T(1024)} %param.33) | copy-start | bytes 9220
  0.7 20.9 %copy-start.11 = (f32[768]{0:T(1024)S(1)}, f32[768]{0:T(1024)}, u32[]{:S(2)}) copy-start(f32[768]{0:T(1024)} %param.39) | copy-start | bytes 9220
  0.7 21.5 %copy-start.12 = (f32[768]{0:T(1024)S(1)}, f32[768]{0:T(1024)}, u32[]{:S(2)}) copy-start(f32[768]{0:T(1024)} %param.42) | copy-start | bytes 9220
  0.7 22.1 %copy-start.13 = (f32[768]{0:T(1024)S(1)}, f32[768]{0:T(1024)}, u32[]{:S(2)}) copy-start(f32[768]{0:T(1024)} %param.43) | copy-start | bytes 9220
  0.7 22.6 %copy-start.14 = (f32[768]{0:T(1024)S(1)}, f32[768]{0:T(1024)}, u32[]{:S(2)}) copy-start(f32[768]{0:T(1024)} %param.46) | copy-start | bytes 9220
  0.7 23.2 %copy-start.15 = (f32[768]{0:T(1024)S(1)}, f32[768]{0:T(1024)}, u32[]{:S(2)}) copy-start(f32[768]{0:T(1024)} %param.51) | copy-start | bytes 9220
  0.7 16.0 %all-to-all-start = ((bf16[4,128,768]{2,1,0:T(8,128)(2,1)}), bf16[4,128,768]{2,1,0:T(8,128)(2,1)S(1)}, u32[]{:S(2)}, u32[]{:S(2)}) async-start(bf16[4,128,768]{2,1,0:T(8,128)(2,1)} %param.30), calls=%async_computation | async-start | bytes 1572864 | tf_op jit(solution)/shard_map/all_to_all | solution.py:748
  16.8 8.4 %copy-start = (bf16[4,128,768]{2,1,0:T(8,128)(2,1)}, bf16[4,128,768]{2,1,0:T(8,128)(2,1)S(1)}, u32[]{:S(2)}) copy-start(bf16[4,128,768]{2,1,0:T(8,128)(2,1)S(1)} %all-to-all-done) | copy-start | bytes 2359300
  16.8 66.5 %all-to-all-start.1 = ((bf16[4,128,768]{2,1,0:T(8,128)(2,1)}), bf16[4,128,768]{2,1,0:T(8,128)(2,1)}, u32[]{:S(2)}, u32[]{:S(2)}) async-start(bf16[4,128,768]{2,1,0:T(8,128)(2,1)} %param.54), calls=%async_computation.1 | async-start | bytes 1572864 | tf_op jit(solution)/shard_map/all_to_all | solution.py:749
  27.4 2.2 copy-start.17
  112.2 30.5 %copy-start.7 = (f32[5,768]{1,0:T(8,128)S(1)}, f32[5,768]{1,0:T(8,128)}, u32[]{:S(2)}) copy-start(f32[5,768]{1,0:T(8,128)} %get-tuple-element.107) | copy-start | bytes 46084
  112.2 30.7 %copy-start.6 = (f32[2,3072]{1,0:T(2,128)S(1)}, f32[2,3072]{1,0:T(2,128)}, u32[]{:S(2)}) copy-start(f32[2,3072]{1,0:T(2,128)} %get-tuple-element.108) | copy-start | bytes 73732
  112.2 30.8 %copy-start.5 = (f32[7,768]{1,0:T(8,128)S(1)}, f32[7,768]{1,0:T(8,128)}, u32[]{:S(2)}) copy-start(f32[7,768]{1,0:T(8,128)} %get-tuple-element.110) | copy-start | bytes 64516
  112.3 31.1 %copy-start.3 = (f32[2,12,768]{2,1,0:T(8,128)S(1)}, f32[2,12,768]{2,1,0:T(8,128)}, u32[]{:S(2)}) copy-start(f32[2,12,768]{2,1,0:T(8,128)} %get-tuple-element.109) | copy-start | bytes 221188
  151.3 2.7 copy-start.8
  151.4 2.7 copy-start.9
  151.4 2.7 copy-start.16
  272.4 4.5 %copy-start.2 = (f32[6,96,384]{2,1,0:T(8,128)S(1)}, f32[6,96,384]{2,1,0:T(8,128)}, u32[]{:S(2)}) copy-start(f32[6,96,384]{2,1,0:T(8,128)} %get-tuple-element.117) | copy-start | bytes 2654212
  276.2 1.5 copy-start.1

commit v3 on v2

--- a/solution.py
+++ b/solution.py
@@ -366,61 +366,231 @@
     )(length, rows_grad, block, cot, fg.reshape(1, -1), hidden, eg.reshape(1, -1), mixed, active, slope, wr, we)
 
 
-def attend_back_kernel(x, ag, q, k, v, probs, context_t, branch, hidden_grad, normed, wq, wk, wv, wo,
-                       units, in_grad, gain_out, band, far,
-                       wqs, wks, wvs, wos, d_out, dp, ds, dq_t, dq, dk, dv, k_t, normed_t, ng, pbuf, psem, sems):
+def backward_kernel(np_, ns, x, ag, q, k, v, context_t, branch, hidden_grad, normed, gains_dec, gains_feed,
+                    probs, wo, wq, wk, wv, wide, tall, dec, encoded,
+                    red, small_out, dec_out, enc_out, grad_out,
+                    wos, wqs, wks, wvs, d_out, dp, ds, dq_t, dq, dk, dv, k_t, normed_t, ng, in_grad,
+                    pbuf, band, diag, own, au, r0, r1y, r1x, r1a, r2, r3, sm, smr, smz,
+                    psem, wsem, loc, c_s, c_r, a_s, a_r, b_s, b_r, ac_s, ac_r, ax_s, ax_r, z_s, z_r,
+                    m_s, m_r, mz_s, mz_r, d_s, d_r, e_s, e_r, g_s, g_r):
     n, width = x.shape
     heads = probs.shape[0]
-    copies = [pltpu.make_async_copy(a, b, sems.at[i])
-              for i, (a, b) in enumerate(((wo, wos), (wq, wqs), (wk, wks), (wv, wvs)))]
-    for c in copies:
-        c.start()
+    nz = np_ // 2
+    rows, lanes = r0.shape[4:]
+    count = np_ * ns
+    p = lax.axis_index("pairs")
+    s = lax.axis_index("seq")
+    c = lax.rem(s, 2)
+    y = s // 2
+    xx = lax.rem(p, 2)
+    z = p // 2
+    me = p * ns + s
+    core_peer = (p, s + 1 - 2 * c)
+    y_peer = (p, lax.rem(s + 2, 4))
+    x_peer = (p + 1 - 2 * xx, s)
+
+    def place(d):
+        lin = lax.rem(me + d, count)
+        return (lin // ns, lax.rem(lin, ns))
+
+    barrier = pltpu.get_barrier_semaphore()
+
+    @pl.loop(1, count)
+    def _(d):
+        pl.semaphore_signal(barrier, inc=1, device_id=place(d), device_id_type=MESH)
+
+    def remote(src, dst, send, recv, peer):
+        return pltpu.make_async_remote_copy(
+            src_ref=src, dst_ref=dst, send_sem=send, recv_sem=recv,
+            device_id=peer, device_id_type=MESH)
+
+    weights = [pltpu.make_async_copy(a, b, wsem.at[i])
+               for i, (a, b) in enumerate(((wo, wos), (wq, wqs), (wk, wks), (wv, wvs)))]
 
     def fetch(h, slot):
         return pltpu.make_async_copy(probs.at[h], pbuf.at[slot], psem.at[slot])
 
-    fetch(0, 0).start()
-    fetch(1, 1).start()
-    far[...] = jnp.zeros_like(far)
-    copies[0].wait()
-
-    @pl.loop(0, width // 256)
+    def unit(i, core):
+        return (wide, tall)[i // 2].at[i % 2, core]
+
+    def core_copy(i):
+        return remote(unit(i, 1 - c), r0.at[i], c_s.at[i], c_r.at[i], core_peer)
+
+    def own_copy(i):
+        return pltpu.make_async_copy(unit(i, c), own.at[i], loc.at[i])
+
+    def first(i):
+        if i % 2 == 0:
+            return remote(own.at[i, 1 - y], r1y.at[i // 2], a_s.at[i], a_r.at[i], y_peer)
+        return remote(own.at[i, :, :, 1 - xx], r1x.at[i // 2], a_s.at[i], a_r.at[i], x_peer)
+
+    def second(i):
+        if i % 2 == 0:
+            return remote(own.at[i, y, :, 1 - xx], r2.at[i], b_s.at[i], b_r.at[i], x_peer)
+        return remote(own.at[i, 1 - y, :, xx], r2.at[i], b_s.at[i], b_r.at[i], y_peer)
+
+    def final(i):
+        return own.at[i, y] if i < 4 else au.at[i - 4, c, y]
+
+    def last(i, d):
+        t = lax.rem(z + d, nz)
+        return remote(final(i).at[t, xx], r3.at[i, d], z_s.at[i, d], z_r.at[i, d], (t * 2 + xx, s))
+
+    def attn_core(w, half):
+        return remote(au.at[w, 1 - c, half], r0.at[4 + w, half], ac_s.at[w, half], ac_r.at[w, half], core_peer)
+
+    def attn_x(w, half):
+        return remote(au.at[w, c, half, :, 1 - xx], r1a.at[w, half], ax_s.at[w, half], ax_r.at[w, half], x_peer)
+
+    def attn_y(w):
+        return remote(au.at[w, c, 1 - y, :, xx], r2.at[4 + w], b_s.at[4 + w], b_r.at[4 + w], y_peer)
+
+    def dec_copy(d):
+        to = place(d)
+        return remote(dec.at[to[0] * ns + to[1]], dec_out.at[me], d_s.at[d], d_r.at[d], to)
+
+    def enc_copy(d):
+        t = lax.rem(s + d, ns)
+        return remote(encoded.at[t], enc_out.at[s], e_s.at[d], e_r.at[d], (p, t))
+
+    def grad_copy(d):
+        t = lax.rem(s + d, ns)
+        return remote(in_grad.at[t], grad_out.at[s], g_s.at[d], g_r.at[d], (p, t))
+
+    keep_dec = pltpu.make_async_copy(dec.at[me], dec_out.at[me], loc.at[4])
+    keep_enc = pltpu.make_async_copy(encoded.at[s], enc_out.at[s], loc.at[5])
+    keep_grad = pltpu.make_async_copy(in_grad.at[s], grad_out.at[s], loc.at[6])
+
+    def step_a(i):
+        core_copy(i).wait()
+        own_copy(i).wait()
+
+        @pl.loop(0, nz)
+        def _(b):
+            for a in range(2):
+                for e in range(2):
+                    own[i, a, b, e] = own[i, a, b, e] + r0[i, a, b, e]
+
+        first(i).start()
+
+    def step_b(i):
+        first(i).wait()
+
+        @pl.loop(0, nz)
+        def _(b):
+            for e in range(2):
+                if i % 2 == 0:
+                    own[i, y, b, e] = own[i, y, b, e] + r1y[i // 2, b, e]
+                else:
+                    own[i, e, b, xx] = own[i, e, b, xx] + r1x[i // 2, e, b]
+
+        second(i).start()
+
+    def step_c(i):
+        if i < 4:
+            second(i).wait()
+        else:
+            attn_y(i - 4).wait()
+
+        @pl.loop(0, nz)
+        def _(b):
+            f = final(i)
+            f[b, xx] = f[b, xx] + r2[i, b]
+
+        @pl.loop(1, nz)
+        def _(d):
+            last(i, d).start()
+
+    def step_d(i):
+        red[i] = final(i)[z, xx].astype(F32)
+
+        @pl.loop(1, nz)
+        def _(d):
+            last(i, d).wait()
+            red[i] = red[i] + r3[i, d].astype(F32)
+
+    def attn_a(w, half):
+        attn_core(w, half).wait()
+
+        @pl.loop(0, nz)
+        def _(b):
+            for e in range(2):
+                au[w, c, half, b, e] = au[w, c, half, b, e] + r0[4 + w, half, b, e]
+
+        attn_x(w, half).start()
+
+    def attn_b(w, half):
+        attn_x(w, half).wait()
+
+        @pl.loop(0, nz)
+        def _(b):
+            au[w, c, half, b, xx] = au[w, c, half, b, xx] + r1a[w, half, b]
+
+    for copy in weights:
+        copy.start()
+    first_half, last_half = 1 - y, y
+    fetch(first_half * (heads // 2), 0).start()
+    fetch(first_half * (heads // 2) + 1, 1).start()
+    for i in range(4):
+        own_copy(i).start()
+    keep_dec.start()
+    keep_enc.start()
+    diag[...] = jnp.zeros_like(diag)
+    weights[0].wait()
+
+    @pl.loop(0, width // 384)
     def _(j):
-        cols = pl.ds(pl.multiple_of(j * 256, 256), 256)
+        cols = pl.ds(pl.multiple_of(j * 384, 128), 384)
         d_out[:, cols] = mm_t(branch[...], wos[cols, :]).astype(BF)
 
+    pl.semaphore_wait(barrier, count - 1)
+    for i in range(4):
+        core_copy(i).start()
+    for d in range(1, ns):
+        enc_copy(d).start()
+
+    @pl.loop(1, count)
+    def _(d):
+        dec_copy(d).start()
+
+    @pl.loop(0, n // 128)
+    def _(i):
+        r = pl.ds(pl.multiple_of(i * 128, 128), 128)
+        normed_t[:, r] = normed[r].T
+
     lane = lax.broadcasted_iota(jnp.int32, (n, 128), 1)
-
-    @pl.loop(0, heads // 2)
-    def _(g):
-        cols = pl.ds(pl.multiple_of(g * 128, 128), 128)
+    lane_s = lax.broadcasted_iota(jnp.int32, (128, 128), 1)
+    row_s = lax.broadcasted_iota(jnp.int32, (128, 128), 0)
+
+    def pair(half, g):
+        cols = pl.ds(pl.multiple_of(half * (width // 2) + g * 128, 128), 128)
         k_t[...] = k[:, cols].T
         dop = d_out[:, cols]
         qp = q[:, cols]
         vp = v[:, cols]
         zero = jnp.zeros_like(qp)
-        dk_sum = None
         for a in range(2):
-            h = 2 * g + a
+            h = half * (heads // 2) + 2 * g + a
             mine = (lane < 64) if a == 0 else (lane >= 64)
             dp[...] = mm_t(jnp.where(mine, vp, zero), dop)
             fetch(h, a).wait()
             for j in range(n // 128):
-                p = pbuf[a, :, j * 128:(j + 1) * 128].astype(F32)
-                pd = p * dp[:, j * 128:(j + 1) * 128]
+                pj = pbuf[a, :, j * 128:(j + 1) * 128].astype(F32)
+                pd = pj * dp[:, j * 128:(j + 1) * 128]
                 total = jnp.sum(pd, axis=0, keepdims=True)
-                s = pd - p * total
-                ds[:, j * 128:(j + 1) * 128] = s.astype(BF)
+                sg = pd - pj * total
+                ds[:, j * 128:(j + 1) * 128] = sg.astype(BF)
                 for i in range(n // 128):
-                    t = s[i * 128:(i + 1) * 128]
+                    t = sg[i * 128:(i + 1) * 128]
                     if abs(i - j) <= 1:
-                        if j == 0 or (i == j + 1 and j == 0) or (j == 1 and i == 0):
-                            band[h, (i - j + 1) * 128:(i - j + 2) * 128, :] = t
+                        b = (i - j + 1) * 128
+                        if j == 0 or (j == 1 and i == 0):
+                            band[b:b + 128, :] = t
                         else:
-                            band[h, (i - j + 1) * 128:(i - j + 2) * 128, :] += t
+                            band[b:b + 128, :] += t
                     else:
-                        w = 1 if i > j else 0
-                        far[w, pl.ds(h, 1), :] += jnp.sum(t, axis=0, keepdims=True)
+                        f = 5 if i > j else 4
+                        diag[h, f:f + 1, :] += jnp.sum(t, axis=0, keepdims=True)
             dvp = mm(pbuf[a], jnp.where(mine, dop, zero))
             dkp = mm(ds[...], jnp.where(mine, qp, zero))
             dq_t[pl.ds(pl.multiple_of(h * 64, 64), 64), :] = mm(k_t[a * 64:(a + 1) * 64, :], ds[...]).astype(BF)
@@ -429,305 +599,219 @@
             else:
                 dk[:, cols] = (dk_sum + dkp).astype(BF)
                 dv[:, cols] = (dv_sum + dvp).astype(BF)
-
-            @pl.when(h + 2 < heads)
-            def _():
-                fetch(h + 2, a).start()
-
-    @pl.loop(0, n // 128)
+            for b in range(3):
+                t = band[b * 128:(b + 1) * 128, :]
+                for bit in range(7):
+                    t = jnp.where((row_s >> bit) % 2 == 1, pltpu.roll(t, 128 - (1 << bit), 1), t)
+                straight = jnp.sum(jnp.where(lane_s + row_s < 128, t, 0.0), axis=0, keepdims=True)
+                whole = jnp.sum(t, axis=0, keepdims=True)
+                diag[h, b:b + 1, :] += straight
+                diag[h, b + 1:b + 2, :] += whole - straight
+
+    part = width // 4
+
+    def units_of(half):
+        cols = pl.ds(pl.multiple_of(half * (width // 2), 128), width // 2)
+        lower = pl.ds(pl.multiple_of(half * (width // 2), 128), width // 2)
+        dq_h = dq_t[lower, :].T
+        dq[:, cols] = dq_h
+        dk_h = dk[:, cols]
+        dv_h = dv[:, cols]
+        br_h = branch[:, cols]
+        zero = jnp.zeros((n, part), BF)
+        for cc in range(2):
+            e = slice(cc * part, (cc + 1) * part)
+            g = mm(normed_t[...], jnp.concatenate([dq_h[:, e], dk_h[:, e]], axis=1))
+            au[0, cc, half] = g.astype(BF).reshape(nz, 2, rows, lanes)
+            g = (mm(normed_t[...], jnp.concatenate([dv_h[:, e], zero], axis=1))
+                 + mm(context_t[...], jnp.concatenate([zero, br_h[:, e]], axis=1)))
+            au[1, cc, half] = g.astype(BF).reshape(nz, 2, rows, lanes)
+        for w in range(2):
+            attn_core(w, half).start()
+
+    quarter = heads // 4
+
+    @pl.loop(0, quarter)
+    def _(g):
+        pair(first_half, g)
+        nxt = jnp.where(g == quarter - 1, last_half * (heads // 2), first_half * (heads // 2) + 2 * (g + 1))
+        fetch(nxt, 0).start()
+        fetch(nxt + 1, 1).start()
+
+        @pl.when(g == 0)
+        def _():
+            step_a(0)
+            step_a(1)
+
+        @pl.when(g == 1)
+        def _():
+            step_a(2)
+            step_a(3)
+
+    units_of(first_half)
+
+    @pl.loop(0, quarter)
+    def _(g):
+        pair(last_half, g)
+
+        @pl.when(g < quarter - 1)
+        def _():
+            nxt = last_half * (heads // 2) + 2 * (g + 1)
+            fetch(nxt, 0).start()
+            fetch(nxt + 1, 1).start()
+
+        @pl.when(g == 0)
+        def _():
+            attn_a(0, first_half)
+            attn_a(1, first_half)
+
+        @pl.when(g == 1)
+        def _():
+            step_b(0)
+            step_b(1)
+
+    units_of(last_half)
+    for copy in weights[1:]:
+        copy.wait()
+
+    @pl.loop(0, 2)
     def _(i):
-        r = pl.ds(pl.multiple_of(i * 128, 128), 128)
-        dq[r] = dq_t[:, r].T
-        normed_t[:, r] = normed[r].T
-
-    for c in copies[1:]:
-        c.wait()
-
-    @pl.loop(0, width // 256)
-    def _(j):
-        cols = pl.ds(pl.multiple_of(j * 256, 256), 256)
-        ng[:, cols] = mm_t(dq[...], wqs[cols, :]) + mm_t(dk[...], wks[cols, :]) + mm_t(dv[...], wvs[cols, :])
-
-    gain_out[...] = jnp.zeros_like(gain_out)
-
-    @pl.loop(0, n // 128)
-    def _(i):
-        r = pl.ds(i * 128, 128)
+        r = pl.ds(pl.multiple_of(i * (n // 2), 128), n // 2)
+        ng[r] = mm_t(dq[r], wqs[...]) + mm_t(dk[r], wks[...]) + mm_t(dv[r], wvs[...])
+
+    attn_a(0, last_half)
+    attn_a(1, last_half)
+    sm[...] = jnp.zeros_like(sm)
+    slot_rows = n // ns
+    gain_sum = jnp.zeros((1, width), F32)
+    for i in range(ns):
+        r = slice(i * slot_rows, (i + 1) * slot_rows)
         t = x[r].astype(F32)
         down, gain = norm_down(t, rms_scale(t), ag[...], ng[r])
-        in_grad[r] = (hidden_grad[r] + down).astype(BF)
-        gain_out[...] += jnp.sum(gain, axis=0, keepdims=True)
-
-    part = width // 4
-    zero = jnp.zeros((n, part), BF)
-    for j in range(4):
-        c = slice(j * part, (j + 1) * part)
-        g = mm(normed_t[...], jnp.concatenate([dq[:, c], dk[:, c]], axis=1))
-        units[0, j % 2, j // 2] = g.astype(BF)
-        g = (mm(normed_t[...], jnp.concatenate([dv[:, c], zero], axis=1))
-             + mm(context_t[...], jnp.concatenate([zero, branch[:, c]], axis=1)))
-        units[1, j % 2, j // 2] = g.astype(BF)
-
-
-def attend_back(x, ag, q, k, v, probs, context_t, branch, hidden_grad, normed, wq, wk, wv, wo):
+        in_grad[i] = (hidden_grad[r] + down).astype(BF)
+        gain_sum = gain_sum + jnp.sum(gain, axis=0, keepdims=True)
+    keep_grad.start()
+    for d in range(1, ns):
+        grad_copy(d).start()
+
+    col = lax.broadcasted_iota(jnp.int32, (128, width), 1)
+    offset = (col // 128 - 1) * 128 - lax.rem(col, 128)
+    offset = jnp.where(col >= width - 128, 256, jnp.where(col >= width - 256, -256, offset))
+    dist = jnp.abs(offset)
+    bucket = jnp.full_like(dist, 8)
+    for edge in EDGES:
+        bucket = bucket + (dist >= edge).astype(jnp.int32)
+    bucket = jnp.where(dist < 8, dist, bucket) + jnp.where(offset > 0, 16, 0)
+    pick = jnp.where(bucket == lax.broadcasted_iota(jnp.int32, (128, width), 0), 1.0, 0.0)
+    bias = jnp.zeros((16, 128), F32)
+    for i in range(width // 128):
+        bias = bias + lax.dot_general(diag[:, i, :], pick[:, i * 128:(i + 1) * 128], (((1,), (1,)), ((), ())),
+                                      precision=HIGHEST, preferred_element_type=F32)
+    sm[0, 40:56, :] = bias
+    gains = [gains_dec[i:i + 1, :] for i in range(3)] + [gains_feed[i:i + 1, :] for i in range(2)] + [gain_sum]
+    for i, gain in enumerate(gains):
+        for j in range(width // 128):
+            sm[0, i * 6 + j:i * 6 + j + 1, :] = gain[:, j * 128:(j + 1) * 128]
+
+    def small_copy(i):
+        return remote(sm.at[i], smr.at[i], m_s.at[i], m_r.at[i], (core_peer, y_peer, x_peer)[i])
+
+    def z_small(d):
+        return remote(smz.at[z], smz.at[z], mz_s.at[d], mz_r.at[d], (lax.rem(z + d, nz) * 2 + xx, s))
+
+    small_copy(0).start()
+    step_b(2)
+    step_b(3)
+    small_copy(0).wait()
+    sm[1] = sm[0] + smr[0]
+    small_copy(1).start()
+    attn_b(0, first_half)
+    attn_y(0).start()
+    attn_b(1, first_half)
+    attn_y(1).start()
+    step_c(0)
+    step_c(1)
+    small_copy(1).wait()
+    sm[2] = sm[1] + smr[1]
+    small_copy(2).start()
+    step_c(2)
+    step_c(3)
+    attn_b(0, last_half)
+    small_copy(2).wait()
+    smz[z] = sm[2] + smr[2]
+
+    @pl.loop(1, nz)
+    def _(d):
+        z_small(d).start()
+
+    step_c(4)
+    attn_b(1, last_half)
+    step_c(5)
+    for i in range(6):
+        step_d(i)
+
+    @pl.loop(1, nz)
+    def _(d):
+        z_small(d).wait()
+
+    small_out[...] = smz[0]
+
+    @pl.loop(1, nz)
+    def _(d):
+        small_out[...] = small_out[...] + smz[d]
+
+    keep_dec.wait()
+    keep_enc.wait()
+    keep_grad.wait()
+    for d in range(1, ns):
+        enc_copy(d).wait()
+        grad_copy(d).wait()
+
+    @pl.loop(1, count)
+    def _(d):
+        dec_copy(d).wait()
+
+
+def backward(np_, ns, x, ag, q, k, v, context_t, branch, hidden_grad, normed, gains_dec, gains_feed,
+             probs, wo, wq, wk, wv, wide, tall, dec, encoded):
     n, width = x.shape
     heads = probs.shape[0]
+    nz = np_ // 2
+    rows, lanes = wide.shape[5:]
+    count = np_ * ns
+    padded = normed.shape[1]
     vm = pl.BlockSpec(memory_space=pltpu.VMEM)
     hb = pl.BlockSpec(memory_space=pl.ANY)
     S = jax.ShapeDtypeStruct
     V = pltpu.VMEM
+    dma = pltpu.SemaphoreType.DMA
     nar = V((n, width), BF)
+    square = V((width, width), BF)
+    slots = (ns, n // ns, width)
+    small = (64, 128)
     return pl.pallas_call(
-        attend_back_kernel,
-        out_shape=(S((2, 2, 2, width, width // 2), BF), S((n, width), BF), S((1, width), F32),
-                   S((heads, 384, 128), F32), S((2, heads, 128), F32)),
-        in_specs=[vm] * 5 + [hb] + [vm] * 4 + [hb] * 4,
-        out_specs=(vm,) * 5,
-        scratch_shapes=[V(w.shape, BF) for w in (wq, wk, wv, wo)] + [
-            nar, V((n, n), F32), V((n, n), BF), V((width, n), BF), nar, nar, nar, V((128, n), BF),
-            V((width, n), BF), V((n, width), F32), V((2, n, n), BF), pltpu.SemaphoreType.DMA((2,)), pltpu.SemaphoreType.DMA((4,))],
-        compiler_params=pltpu.CompilerParams(vmem_limit_bytes=60 * 1024 * 1024),
-        name="attend_back",
-    )(x, ag.reshape(1, -1), q, k, v, probs, context_t, branch, hidden_grad, normed, wq, wk, wv, wo)
-
-
-def exchange_kernel(np_, ns, wide, tall, attn, small, dec, enc, red, small_out, dec_out, enc_out,
-                    own, r0, r1a, r1b, s1a, s1b, r2, s2, r3, sm, smr, smz,
-                    loc, s0s, s0r, s1s, s1r, s2s, s2r, s3s, s3r,
-                    ms, mr, mzs, mzr, ds, dr, es, er):
-    units = 6
-    nz = np_ // 2
-    p = lax.axis_index("pairs")
-    s = lax.axis_index("seq")
-    c = lax.rem(s, 2)
-    y = s // 2
-    x = lax.rem(p, 2)
-    z = p // 2
-    me = p * ns + s
-    count = np_ * ns
-    core_peer = (p, s + 1 - 2 * c)
-    y_peer = (p, lax.rem(s + 2, 4))
-    x_peer = (p + 1 - 2 * x, s)
-
-    def place(d):
-        lin = lax.rem(me + d, count)
-        return (lin // ns, lax.rem(lin, ns))
-
-    barrier = pltpu.get_barrier_semaphore()
-
-    @pl.loop(1, count)
-    def _(d):
-        pl.semaphore_signal(barrier, inc=1, device_id=place(d), device_id_type=MESH)
-
-    pl.semaphore_wait(barrier, count - 1)
-
-    def remote(src, dst, send, recv, peer):
-        return pltpu.make_async_remote_copy(
-            src_ref=src, dst_ref=dst, send_sem=send, recv_sem=recv,
-            device_id=peer, device_id_type=MESH)
-
-    def unit(k, core):
-        return (wide, tall, attn)[k // 2].at[k % 2, core]
-
-    def core_copy(k):
-        return remote(unit(k, 1 - c), r0.at[k], s0s.at[k], s0r.at[k], core_peer)
-
-    def own_copy(k):
-        return pltpu.make_async_copy(unit(k, c), own.at[k], loc.at[k])
-
-    for k in range(units):
-        core_copy(k).start()
-        own_copy(k).start()
-
-    def dec_copy(d):
-        q = place(d)
-        return remote(dec.at[q[0] * ns + q[1]], dec_out.at[me], ds.at[d], dr.at[d], q)
-
-    keep_dec = pltpu.make_async_copy(dec.at[me], dec_out.at[me], loc.at[units])
-    keep_dec.start()
-
-    @pl.loop(1, count)
-    def _(d):
-        dec_copy(d).start()
-
-    def enc_copy(d):
-        t = lax.rem(s + d, ns)
-        return remote(enc.at[:, t], enc_out.at[:, s], es.at[d], er.at[d], (p, t))
-
-    keep_enc = pltpu.make_async_copy(enc.at[:, s], enc_out.at[:, s], loc.at[units + 1])
-    keep_enc.start()
-    for d in range(1, ns):
-        enc_copy(d).start()
-
-    sm[0] = small[...]
-    for i, peer in enumerate((core_peer, y_peer, x_peer)):
-        copy = remote(sm.at[i], smr.at[i], ms.at[i], mr.at[i], peer)
-        copy.start()
-        copy.wait()
-        if i < 2:
-            sm[i + 1] = sm[i] + smr[i]
-        else:
-            smz[z] = sm[i] + smr[i]
-
-    def z_small(d):
-        return remote(smz.at[z], smz.at[z], mzs.at[d], mzr.at[d],
-                      (lax.rem(z + d, nz) * 2 + x, s))
-
-    @pl.loop(1, nz)
-    def _(d):
-        z_small(d).start()
-
-    def y_first(k):
-        return remote(own.at[2 * k, 1 - y], r1a.at[k], s1s.at[2 * k], s1r.at[2 * k], y_peer)
-
-    def x_first(k):
-        return remote(own.at[2 * k + 1, :, :, 1 - x], r1b.at[k], s1s.at[2 * k + 1],
-                      s1r.at[2 * k + 1], x_peer)
-
-    def x_second(k):
-        return remote(s1a.at[k, :, 1 - x], r2.at[2 * k], s2s.at[2 * k], s2r.at[2 * k], x_peer)
-
-    def y_second(k):
-        return remote(s1b.at[k, 1 - y], r2.at[2 * k + 1], s2s.at[2 * k + 1],
-                      s2r.at[2 * k + 1], y_peer)
-
-    def z_last(k, d):
-        t = lax.rem(z + d, nz)
-        return remote(s2.at[k, t], r3.at[k, d], s3s.at[k, d], s3r.at[k, d], (t * 2 + x, s))
-
-    def stage0(k):
-        core_copy(k).wait()
-        own_copy(k).wait()
-
-        @pl.loop(0, 2)
-        def _(a):
-            @pl.loop(0, nz)
-            def _(b):
-                for e in range(2):
-                    own[k, a, b, e] = (own[k, a, b, e].astype(F32)
-                                       + r0[k, a, b, e].astype(F32)).astype(BF)
-
-    for k in range(units // 2):
-        stage0(2 * k)
-        y_first(k).start()
-        stage0(2 * k + 1)
-        x_first(k).start()
-
-    @pl.loop(0, units // 2)
-    def _(k):
-        y_first(k).wait()
-
-        @pl.loop(0, nz)
-        def _(b):
-            for e in range(2):
-                s1a[k, b, e] = (own[2 * k, y, b, e].astype(F32)
-                                + r1a[k, b, e].astype(F32)).astype(BF)
-
-        x_second(k).start()
-        x_first(k).wait()
-
-        @pl.loop(0, nz)
-        def _(b):
-            for e in range(2):
-                s1b[k, e, b] = (own[2 * k + 1, e, b, x].astype(F32)
-                                + r1b[k, e, b].astype(F32)).astype(BF)
-
-        y_second(k).start()
-
-    @pl.loop(0, units // 2)
-    def _(k):
-        x_second(k).wait()
-
-        @pl.loop(0, nz)
-        def _(b):
-            s2[2 * k, b] = (s1a[k, b, x].astype(F32) + r2[2 * k, b].astype(F32)).astype(BF)
-
-        @pl.loop(1, nz)
-        def _(d):
-            z_last(2 * k, d).start()
-
-        y_second(k).wait()
-
-        @pl.loop(0, nz)
-        def _(b):
-            s2[2 * k + 1, b] = (s1b[k, y, b].astype(F32)
-                                + r2[2 * k + 1, b].astype(F32)).astype(BF)
-
-        @pl.loop(1, nz)
-        def _(d):
-            z_last(2 * k + 1, d).start()
-
-    @pl.loop(0, units)
-    def _(k):
-        red[k] = s2[k, z].astype(F32)
-
-        @pl.loop(1, nz)
-        def _(d):
-            z_last(k, d).wait()
-            red[k] = red[k] + r3[k, d].astype(F32)
-
-    @pl.loop(1, nz)
-    def _(d):
-        z_small(d).wait()
-
-    small_out[...] = smz[0]
-
-    @pl.loop(1, nz)
-    def _(d):
-        small_out[...] = small_out[...] + smz[d]
-
-    keep_dec.wait()
-    keep_enc.wait()
-    for d in range(1, ns):
-        enc_copy(d).wait()
-
-    @pl.loop(1, count)
-    def _(d):
-        dec_copy(d).wait()
-
-
-def exchange(np_, ns, wide, tall, attn, small, dec, enc):
-    units = 6
-    half = units // 2
-    nz = np_ // 2
-    rows, cols = wide.shape[5:]
-    count = np_ * ns
-    dma = pltpu.SemaphoreType.DMA
-    anywhere = pl.BlockSpec(memory_space=pl.ANY)
-    vmem = pl.BlockSpec(memory_space=pltpu.VMEM)
-    return pl.pallas_call(
-        functools.partial(exchange_kernel, np_, ns),
-        out_shape=(
-            jax.ShapeDtypeStruct((units, rows, cols), F32),
-            jax.ShapeDtypeStruct(small.shape, F32),
-            jax.ShapeDtypeStruct(dec.shape, BF),
-            jax.ShapeDtypeStruct(enc.shape, BF),
-        ),
-        in_specs=[anywhere, anywhere, anywhere, vmem, anywhere, anywhere],
-        out_specs=(vmem, vmem, anywhere, anywhere),
+        functools.partial(backward_kernel, np_, ns),
+        out_shape=(S((6, rows, lanes), F32), S(small, F32), S(dec.shape, BF), S(slots, BF), S(slots, BF)),
+        in_specs=[vm] * 11 + [hb] * 9,
+        out_specs=(vm, vm, hb, hb, hb),
         scratch_shapes=[
-            pltpu.VMEM((units, 2, nz, 2, rows, cols), BF),
-            pltpu.VMEM((units, 2, nz, 2, rows, cols), BF),
-            pltpu.VMEM((half, nz, 2, rows, cols), BF),
-            pltpu.VMEM((half, 2, nz, rows, cols), BF),
-            pltpu.VMEM((half, nz, 2, rows, cols), BF),
-            pltpu.VMEM((half, 2, nz, rows, cols), BF),
-            pltpu.VMEM((units, nz, rows, cols), BF),
-            pltpu.VMEM((units, nz, rows, cols), BF),
-            pltpu.VMEM((units, nz, rows, cols), BF),
-            pltpu.VMEM((3,) + small.shape, F32),
-            pltpu.VMEM((3,) + small.shape, F32),
-            pltpu.VMEM((nz,) + small.shape, F32),
-            dma((units + 2,)),
-            dma((units,)), dma((units,)), dma((units,)), dma((units,)),
-            dma((units,)), dma((units,)), dma((units, nz)), dma((units, nz)),
-            dma((3,)), dma((3,)), dma((nz,)), dma((nz,)),
-            dma((count,)), dma((count,)), dma((ns,)), dma((ns,)),
+            square, square, square, square, nar, V((n, n), F32), V((n, n), BF), V((width, n), BF), nar, nar, nar,
+            V((128, n), BF), V((padded, n), BF), V((n, width), F32), V(slots, BF),
+            V((2, n, n), BF), V((384, 128), F32), V((16, 8, 128), F32),
+            V((4, 2, nz, 2, rows, lanes), BF), V((2, 2, 2, nz, 2, rows, lanes), BF), V((6, 2, nz, 2, rows, lanes), BF),
+            V((2, nz, 2, rows, lanes), BF), V((2, 2, nz, rows, lanes), BF), V((2, 2, nz, rows, lanes), BF),
+            V((6, nz, rows, lanes), BF), V((6, nz, rows, lanes), BF),
+            V((3,) + small, F32), V((3,) + small, F32), V((nz,) + small, F32),
+            dma((2,)), dma((4,)), dma((7,)), dma((4,)), dma((4,)), dma((4,)), dma((4,)), dma((6,)), dma((6,)),
+            dma((2, 2)), dma((2, 2)), dma((2, 2)), dma((2, 2)), dma((6, nz)), dma((6, nz)),
+            dma((3,)), dma((3,)), dma((nz,)), dma((nz,)), dma((count,)), dma((count,)),
+            dma((ns,)), dma((ns,)), dma((ns,)), dma((ns,)),
         ],
         compiler_params=pltpu.CompilerParams(
-            collective_id=0, has_side_effects=True, vmem_limit_bytes=58 * 1024 * 1024),
-        name="exchange",
-    )(wide, tall, attn, small, dec, enc)
+            collective_id=0, has_side_effects=True, vmem_limit_bytes=62 * 1024 * 1024),
+        name="backward",
+    )(x, ag.reshape(1, -1), q, k, v, context_t, branch, hidden_grad, normed, gains_dec, gains_feed,
+      probs, wo, wq, wk, wv, wide, tall, dec, encoded.reshape(slots))
 
 
 def per_device(
@@ -766,13 +850,6 @@
     wide, tall, hidden_grad, branch, feed_gains = feed_back(
         np_ if aligned else 1, length, rows_grad, block, cot, final_gain, hidden, expand_gain,
         mixed, active, slope, reduce_weight, expand_weight)
-    attn, input_grad, attend_gain_sum, band_grad, far_grad = attend_back(
-        x, attend_gain, query, key, value, probs, context_t, branch, hidden_grad, normed,
-        query_weight, key_weight, value_weight, output_weight)
-    far_sum = jnp.sum(far_grad, axis=-1)
-    grad_bias = jnp.einsum("but,hut->bh", onehot, band_grad, precision=HIGHEST)
-    grad_bias = grad_bias.at[15].add(far_sum[0]).at[31].add(far_sum[1])
-
     rp = -(-r // 16) * 16
     lanes = ff // 8
     side = width // 8 // r
@@ -786,11 +863,7 @@
         tall = tall.reshape(2, 2, 2, r, side, nz, 2, ff // np_).transpose(0, 1, 2, 5, 6, 3, 4, 7)
         tall = pad(tall.reshape(2, 2, 2, nz, 2, r, lanes))
     wide = pad(wide.reshape(2, 2, 2, nz, 2, r, lanes))
-    attn = pad(attn.reshape(2, 2, 2, nz, 2, r, lanes))
     cols = width // ns
-    small = jnp.concatenate([
-        dec_gains, feed_gains, attend_gain_sum,
-        jnp.pad(grad_bias.reshape(1, -1), ((0, 1), (0, width - grad_bias.size)))])
 
     left_cut = jnp.concatenate([
         left.reshape(5, np_, r).transpose(1, 0, 2).reshape(np_, 5 * r),
@@ -809,9 +882,16 @@
     dec_rows = -(-used // 2048) * 16
     dec_all = jnp.pad(dec_all, ((0, 0), (0, dec_rows * 128 - used)))
     dec_all = dec_all.reshape(np_ * ns, dec_rows, 128)
-    both = jnp.stack([encoded, input_grad]).reshape(2, ns, local_rows, width)
-
-    red, small_sum, dec_got, both_out = exchange(np_, ns, wide, tall, attn, small, dec_all, both)
+
+    if rp != r:
+        gap = ((0, 0), (0, 0), (0, rp - r))
+        normed = jnp.pad(normed.reshape(seq_len, np_, r), gap).reshape(seq_len, np_ * rp)
+        gap = ((0, 0), (0, rp - r), (0, 0))
+        context_t = jnp.pad(context_t.reshape(np_, r, seq_len), gap).reshape(np_ * rp, seq_len)
+    red, small_sum, dec_got, enc_out, grad_out = backward(
+        np_, ns, x, attend_gain, query, key, value, context_t, branch, hidden_grad, normed,
+        dec_gains, feed_gains, probs, output_weight, query_weight, key_weight, value_weight,
+        wide, tall, dec_all, encoded)
 
     got = dec_got.reshape(np_ * ns, -1)
     lefts = got[:, :9 * r].reshape(-1, 9, r)
@@ -826,18 +906,19 @@
                           preferred_element_type=F32)
     red = red[:, :r]
     grad_reduce = red[2:4].reshape(2, r, side, ff // np_).reshape(cols, ff // np_).T
-    bias = small_sum[6, :bias_table.size].reshape(bias_table.shape)
+    gains = small_sum[:36].reshape(6, width)
+    bias = small_sum[40:40 + heads, :buckets].T
     return (
-        both_out[0], dec_block, both_out[1], dec_input_grad,
-        small_sum[5],
+        enc_out, dec_block, grad_out, dec_input_grad,
+        gains[5],
         red[4][:, :cols], red[4][:, cols:], red[5][:, :cols], red[5][:, cols:],
         bias,
-        small_sum[4],
+        gains[4],
         jnp.concatenate([red[0], red[1]], axis=1), grad_reduce,
-        small_sum[3],
-        small_sum[0], plain[0], plain[1],
-        small_sum[1], plain[2], crossed[0], crossed[1], plain[3],
-        small_sum[2], feed_in, feed_out,
+        gains[3],
+        gains[0], plain[0], plain[1],
+        gains[1], plain[2], crossed[0], crossed[1], plain[3],
+        gains[2], feed_in, feed_out,
     )
 
 

time: 287 us -> 235 us (0.82)
  Pallas kernels: 229 us -> 194 us
  waiting for transfers between devices: 11.5 us -> 2.12 us
  other arithmetic: 5.39 us -> 2.06 us
  matrix products: 7.65 us -> 4.42 us
    pallas_call x2 -> x1, Pallas kernels: 147 us -> 111 us  [backward(): pl.pallas_call(functools.partial(backward_kernel, np_, ns), out_shape=(S(...]
    all_to_all x1, waiting for transfers between devices: 11.5 us -> 2.12 us  [per_device(): lax.all_to_all(enc_input, 'seq', split_axis=0, concat_axis=1, tiled=True)[0]]
    dot_general x1 -> x0, matrix products: 3.31 us -> none  [per_device(): grad_bias = jnp.einsum('but,hut->bh', onehot, band_grad, precision=HIGHEST)]
    unnamed x44 -> x33, local copies, waits for them, and re-layouts: 4.25 us -> 6 us
  transfers between devices with their start and end apart: 2 -> 2, of which waited for: 1 -> 1; matrix products, arithmetic and copies ran while one was open for 3% -> 6% of each run, Pallas kernels for 19% -> 23%
where the time goes in v3:
time: 235 us; the launch traced here: 234 us
  Pallas kernels  194 us (83%)
  local copies, waits for them, and re-layouts  22.8 us (10%)
  starting transfers between devices  8.06 us (3%)
  matrix products  4.42 us (2%)
    pallas_call x1, Pallas kernels, backward(): pl.pallas_call(functools.partial(backward_kernel, np_, ns), out_shape=(S(...  111 us
    pallas_call x1, Pallas kernels, encode(): pl.pallas_call(encode_kernel, out_shape=(full, full, full, full, S((heads...  37.8 us
    pallas_call x1, Pallas kernels, feed_back(): pl.pallas_call(feed_back_kernel, out_shape=(S((2, 2, 2, width, ff // 8),...  29.1 us
    pallas_call x1, Pallas kernels, decode(): pl.pallas_call(decode_kernel, out_shape=(S((1, width), BF), S((1, width),...  15.3 us
    unnamed x33, local copies, waits for them, and re-layouts  6 us
  transfers between devices with their start and end apart: 2, of which 1 were waited for; matrix products, arithmetic and copies ran while one was open for 6% of the time, Pallas kernels for 23%

profile of v3, /device:TPU:0, one launch (start us, length us, event | category | flops | bytes accessed | tf_op | source)
XLA Modules:
  0.0 234.0 jit_solution(4150915756999653085)
XLA Ops:
  0.7 4.4 %all-to-all-start = ((bf16[4,128,768]{2,1,0:T(8,128)(2,1)}), bf16[4,128,768]{2,1,0:T(8,128)(2,1)S(1)}, u32[]{:S(2)}, u32[]{:S(2)}) async-start(bf16[4,128,768]{2,1,0:T(8,128)(2,1)} %param.26), calls=%async_computation | async-start | bytes 1572864 | tf_op jit(solution)/shard_map/all_to_all | solution.py:832
  5.1 0.2 slice_reduce_fusion.3
  5.3 0.6 reshape.206.ag
  5.9 0.6 reshape.207.eg
  6.5 0.6 reshape.208.fg
  7.1 0.6 reshape.209.sg
  7.7 0.6 reshape.210.cg
  8.3 0.6 reshape.211.fg
  8.8 0.7 copy.87.far
  9.5 0.3 fusion.2
  9.8 2.1 fusion
  11.9 2.2 copy.127
  14.1 0.6 dynamic_slice.3.length
  14.7 2.1 all-to-all-done
  16.8 3.7 %all-to-all-start.1 = ((bf16[4,128,768]{2,1,0:T(8,128)(2,1)}), bf16[4,128,768]{2,1,0:T(8,128)(2,1)S(1)}, u32[]{:S(2)}, u32[]{:S(2)}) async-start(bf16[4,128,768]{2,1,0:T(8,128)(2,1)} %param.50), calls=%async_computation.1 | async-start | bytes 1572864 | tf_op jit(solution)/shard_map/all_to_all | solution.py:833
  20.5 37.8 %encode.1 = (bf16[512,768]{1,0:T(8,128)(2,1)}, bf16[512,768]{1,0:T(8,128)(2,1)}, bf16[512,768]{1,0:T(8,128)(2,1)}, bf16[512,768]{1,0:T(8,128)(2,1)}, bf16[12,512...) custom-call(s32[1]{0:T(128)} %dynamic_slice.3.length, ...), custom_call_target="tpu_custom_call" | custom-call | tf_op jit(solution)/shard_map/encode/pallas_call | solution.py:149
  58.3 15.3 %decode.1 = (bf16[1,768]{1,0:T(2,128)(2,1)}, bf16[1,768]{1,0:T(2,128)(2,1)}, f32[3,768]{1,0:T(4,128)}, f32[5,768]{1,0:T(8,128)}, f32[7,768]{1,0:T(8,128)}, /*ind...) custom-call(s32[1]{0:T(128)} %dynamic_slice.3.length, bf16[512,768]{1,0:T(8,128)(2,1)} %get-tuple-element.60.rows, ...), custom_call_target="tpu_custom_call" | custom-call | tf_op jit(solution)/shard_map/decode/pallas_call | solution.py:265
  73.6 0.9 slice_reduce_fusion
  74.5 0.8 reshape.214
  75.4 0.8 reshape.217
  76.5 0.9 convert.17
  77.6 0.1 concatenate.22
  77.9 0.2 concatenate.25
  78.1 0.7 copy.105
  78.8 0.9 copy-done.1
  79.7 29.1 %feed_back.1 = (bf16[2,2,2,768,384]{4,3,2,1,0:T(8,128)(2,1)}, bf16[2,2,2,8,96,384]{5,4,3,2,1,0:T(8,128)(2,1)}, f32[512,768]{1,0:T(8,128)}, bf16[512,768]{1,0:T(8,128)(2,1)}, f32[2,768]{1,0:T(2,128)}) custom-call(s32[1]{0:T(128)} %dynamic_slice.3.length, bf16[512,768]{1,0:T(8,128)(2,1)} %get-tuple-element.61.rows_grad, f32[512,768]{1,0:T(8,128)} %get-tuple-element.62.block, ...), custom_call_target="tpu_custom_call" | custom-call | tf_op jit(solution)/shard_map/feed_back/pallas_call | solution.py:356
  108.8 111.4 %backward.1 = (f32[6,96,384]{2,1,0:T(8,128)}, f32[64,128]{1,0:T(8,128)}, bf16[32,32,128]{2,1,0:T(8,128)(2,1)}, bf16[4,128,768]{2,1,0:T(8,128)(2,1)}, bf16[4,128,768]{2,1,0:T(8,128)(2,1)}) custom-call(bf16[512,768]{1,0:T(8,128)(2,1)} %bitcast.76, f32[1,768]{1,0:T(1,128)} %reshape.206.ag, bf16[512,768]{1,0:T(8,128)(2,1)} %get-tuple-element.56.q, ...), custom_call_target="tpu_custom_call" | custom-call | tf_op jit(solution)/shard_map/backward/pallas_call | solution.py:792
  220.2 1.4 slice_bitcast_fusion.8
  221.6 1.4 slice_bitcast_fusion.9
  223.0 1.1 copy.128
  224.1 0.1 slice.167
  224.2 0.1 reshape.222
  224.5 0.3 reshape.223
  224.9 0.7 slice.140
  225.7 0.1 reshape.225
  225.9 0.1 reshape.229
  226.0 0.1 reshape.226
  226.1 0.2 convolution_bitcast_fusion
  226.3 0.7 copy.98
  227.1 0.7 copy.97
  227.8 0.2 fusion.12
  228.1 0.8 slice_bitcast_fusion.4
  228.8 0.9 fusion.20
  229.8 1.0 fusion.17
  230.7 0.7 pad_maximum_fusion
  231.4 0.8 fusion.26
  232.2 0.9 copy.133
  233.1 0.9 copy.134
  (54 shorter events, 1.2 us)
Async XLA Ops:
  0.7 4.5 %copy-start.5 = (f32[32,12]{0,1:T(8,128)S(1)}, f32[32,12]{0,1:T(8,128)}, u32[]{:S(2)}) copy-start(f32[32,12]{0,1:T(8,128)} %param.34) | copy-start | bytes 4612
  0.7 4.6 %copy-start.6 = (f32[768]{0:T(1024)S(1)}, f32[768]{0:T(1024)}, u32[]{:S(2)}) copy-start(f32[768]{0:T(1024)} %param.29) | copy-start | bytes 9220
  0.7 5.2 %copy-start.7 = (f32[768]{0:T(1024)S(1)}, f32[768]{0:T(1024)}, u32[]{:S(2)}) copy-start(f32[768]{0:T(1024)} %param.35) | copy-start | bytes 9220
  0.7 5.8 %copy-start.8 = (f32[768]{0:T(1024)S(1)}, f32[768]{0:T(1024)}, u32[]{:S(2)}) copy-start(f32[768]{0:T(1024)} %param.38) | copy-start | bytes 9220
  0.7 6.4 %copy-start.9 = (f32[768]{0:T(1024)S(1)}, f32[768]{0:T(1024)}, u32[]{:S(2)}) copy-start(f32[768]{0:T(1024)} %param.39) | copy-start | bytes 9220
  0.7 7.0 %copy-start.10 = (f32[768]{0:T(1024)S(1)}, f32[768]{0:T(1024)}, u32[]{:S(2)}) copy-start(f32[768]{0:T(1024)} %param.42) | copy-start | bytes 9220
  0.7 7.5 %copy-start.11 = (f32[768]{0:T(1024)S(1)}, f32[768]{0:T(1024)}, u32[]{:S(2)}) copy-start(f32[768]{0:T(1024)} %param.47) | copy-start | bytes 9220
  0.7 16.0 %all-to-all-start = ((bf16[4,128,768]{2,1,0:T(8,128)(2,1)}), bf16[4,128,768]{2,1,0:T(8,128)(2,1)S(1)}, u32[]{:S(2)}, u32[]{:S(2)}) async-start(bf16[4,128,768]{2,1,0:T(8,128)(2,1)} %param.26), calls=%async_computation | async-start | bytes 1572864 | tf_op jit(solution)/shard_map/all_to_all | solution.py:832
  11.9 2.2 copy-start.12
  16.8 3.7 %copy-start = (bf16[4,128,768]{2,1,0:T(8,128)(2,1)}, bf16[4,128,768]{2,1,0:T(8,128)(2,1)S(1)}, u32[]{:S(2)}) copy-start(bf16[4,128,768]{2,1,0:T(8,128)(2,1)S(1)} %all-to-all-done) | copy-start | bytes 2359300
  16.8 62.0 %all-to-all-start.1 = ((bf16[4,128,768]{2,1,0:T(8,128)(2,1)}), bf16[4,128,768]{2,1,0:T(8,128)(2,1)S(1)}, u32[]{:S(2)}, u32[]{:S(2)}) async-start(bf16[4,128,768]{2,1,0:T(8,128)(2,1)} %param.50), calls=%async_computation.1 | async-start | bytes 1572864 | tf_op jit(solution)/shard_map/all_to_all | solution.py:833
  78.8 0.9 copy-start.1
  220.2 4.7 %copy-start.2 = (f32[6,96,384]{2,1,0:T(8,128)S(1)}, f32[6,96,384]{2,1,0:T(8,128)}, u32[]{:S(2)}) copy-start(f32[6,96,384]{2,1,0:T(8,128)} %get-tuple-element.85) | copy-start | bytes 2654212
  227.8 4.4 %copy-start.4 = (bf16[4,128,768]{2,1,0:T(8,128)(2,1)S(1)}, bf16[4,128,768]{2,1,0:T(8,128)(2,1)}, u32[]{:S(2)}) copy-start(bf16[4,128,768]{2,1,0:T(8,128)(2,1)} %get-tuple-element.242) | copy-start | bytes 2359300
  230.7 2.4 %copy-start.3 = (bf16[4,128,768]{2,1,0:T(8,128)(2,1)S(1)}, bf16[4,128,768]{2,1,0:T(8,128)(2,1)}, u32[]{:S(2)}) copy-start(bf16[4,128,768]{2,1,0:T(8,128)(2,1)} %get-tuple-element.244) | copy-start | bytes 2359300
